TPU v7x, 128 devices: a whole 4x4x4 slice. The times are simulated.
128 devices in a mesh: dp: 4 (over y), seq: 2 (over core), expert: 16 (over z, x).
Axes of the slice: x: 4, y: 4, z: 4, core: 2. Of those that a mesh axis runs over, the one named last changes fastest.
Arguments:
- hidden_in: bfloat16 [16384, 1152], P(('dp', 'seq', 'expert')), may hold values from -6 to 6
- grad_out: bfloat16 [16384, 1152], P(('dp', 'seq', 'expert')), may hold values from -1.5 to 1.5
- combine: float32 [16384, 2], P(('dp', 'seq', 'expert')), may hold values from 0.1 to 1
- routes: int32 [16384, 2], P(('dp', 'seq', 'expert')), may hold values from 0 to 15, all different within a row; in each aligned block of 128 rows (0 to 127, 128 to 255, ...) at most 20 rows name the same one
- w_in: bfloat16 [16, 1152, 4608], P('expert', None, ('dp', 'seq')), may hold values from -0.1875 to 0.1875
- w_out: bfloat16 [16, 4608, 1152], P('expert', ('dp', 'seq')), may hold values from -0.09375 to 0.09375
Outputs:
- grad_x: bfloat16 [16384, 1152], P(('dp', 'seq', 'expert'))
- grad_combine: float32 [16384, 2], P(('dp', 'seq', 'expert'))
- grad_w_in: bfloat16 [16, 1152, 4608], P('expert', None, ('dp', 'seq'))
- grad_w_out: bfloat16 [16, 4608, 1152], P('expert', ('dp', 'seq'))
Inputs may be any that keep to these rules, and one draw needn't show every extreme that they name: `routes`: each token names 2 different experts. Within the 128 tokens of one device (aligned blocks of rows) no expert is named by more than 20 tokens, and in every draw some expert is named by exactly 20 tokens of some block.
All inputs are finite; a program needn't handle non-finite values.
Results may differ from a plain program's by a relative error of at most 0.023.
Values may be sent and summed in bfloat16 or wider, within the bound.
No kernel may reach another device: no remote copies, remote signals or barrier semaphores. Data moves between devices by JAX's collectives and lax.ppermute only.
A program may use at most 128 MiB of HBM per device.

v0:
```python
import math

import jax
import jax.numpy as jnp
from jax import lax
from jax.sharding import PartitionSpec as P


def gelu_slope(preact):
    coeff = math.sqrt(2.0 / math.pi)
    inner = coeff * (preact + 0.044715 * preact * preact * preact)
    tanh_val = jnp.tanh(inner)
    return 0.5 * (1.0 + tanh_val) + 0.5 * preact * (1.0 - tanh_val * tanh_val) * coeff * (
        1.0 + 3.0 * 0.044715 * preact * preact
    )


def local(hidden_in, grad_out, combine, routes, w_in, w_out):
    tokens_here = hidden_in.shape[0]
    width = hidden_in.shape[1]
    top_count = routes.shape[1]
    local_count = w_in.shape[0]
    expert_count = lax.axis_size("expert")
    experts_all = local_count * expert_count
    capacity = 5 * tokens_here * top_count // (4 * experts_all)
    flat_routes = routes.reshape(-1)
    onehot = (flat_routes[:, None] == jnp.arange(experts_all, dtype=jnp.int32)[None, :]).astype(
        jnp.int32
    )
    earlier = jnp.cumsum(onehot, axis=0) - onehot
    slot_index = jnp.sum(earlier * onehot, axis=1)
    position = flat_routes * capacity + slot_index
    chosen = position[None, :] == jnp.arange(experts_all * capacity, dtype=jnp.int32)[:, None]
    picker = (
        chosen.reshape(experts_all * capacity, tokens_here, top_count)
        .any(axis=2)
        .astype(jnp.bfloat16)
    )
    send_x = jnp.dot(picker, hidden_in, preferred_element_type=jnp.float32).astype(jnp.bfloat16)
    send_dy = jnp.dot(picker, grad_out, preferred_element_type=jnp.float32).astype(jnp.bfloat16)
    send_gate = jnp.sum(jnp.where(chosen, combine.reshape(-1)[None, :], jnp.float32(0.0)), axis=1)
    send_x = send_x.reshape(experts_all, capacity, width)
    send_dy = send_dy.reshape(experts_all, capacity, width)
    send_gate = send_gate.reshape(experts_all, capacity)
    got_x, got_dy, got_gate = (
        lax.all_to_all(send_x, "expert", split_axis=0, concat_axis=0, tiled=True),
        lax.all_to_all(send_dy, "expert", split_axis=0, concat_axis=0, tiled=True),
        lax.all_to_all(
            send_gate.astype(jnp.bfloat16), "expert", split_axis=0, concat_axis=0, tiled=True
        ).astype(send_gate.dtype),
    )

    def to_local(block):
        shaped = block.reshape((expert_count, local_count) + block.shape[1:])
        shaped = jnp.swapaxes(shaped, 0, 1)
        return shaped.reshape((local_count, expert_count * capacity) + block.shape[2:])

    rows_x, rows_dy, rows_gate = (
        lax.all_gather(to_local(got_x), ("dp", "seq"), axis=1, tiled=True),
        lax.all_gather(to_local(got_dy), ("dp", "seq"), axis=1, tiled=True),
        lax.all_gather(
            to_local(got_gate).astype(jnp.bfloat16), ("dp", "seq"), axis=1, tiled=True
        ).astype(jnp.float32),
    )
    preact = jnp.einsum("erd,edf->erf", rows_x, w_in, preferred_element_type=jnp.float32)
    hidden = jax.nn.gelu(preact, approximate=True).astype(jnp.bfloat16)
    back_proj = jnp.einsum("erd,efd->erf", rows_dy, w_out, preferred_element_type=jnp.float32)
    gate_part = jnp.sum(hidden.astype(jnp.float32) * back_proj, axis=2)
    weighted = (rows_gate[:, :, None] * hidden.astype(jnp.float32)).astype(jnp.bfloat16)
    grad_w_out = jnp.einsum(
        "erf,erd->efd", weighted, rows_dy, preferred_element_type=jnp.float32
    ).astype(jnp.bfloat16)
    dpre = (rows_gate[:, :, None] * back_proj * gelu_slope(preact)).astype(jnp.bfloat16)
    grad_w_in = jnp.einsum("erd,erf->edf", rows_x, dpre, preferred_element_type=jnp.float32).astype(
        jnp.bfloat16
    )
    part_x = jnp.einsum("erf,edf->erd", dpre, w_in, preferred_element_type=jnp.float32)
    own_x, own_gate = (
        lax.psum_scatter(
            part_x.astype(jnp.bfloat16), ("dp", "seq"), scatter_dimension=1, tiled=True
        ).astype(jnp.float32),
        lax.psum_scatter(
            gate_part.astype(jnp.bfloat16), ("dp", "seq"), scatter_dimension=1, tiled=True
        ).astype(jnp.float32),
    )

    def to_source(block):
        shaped = block.reshape((local_count, expert_count, capacity) + block.shape[2:])
        shaped = jnp.swapaxes(shaped, 0, 1)
        return shaped.reshape((expert_count * local_count, capacity) + block.shape[2:])

    ret_x, ret_gate = (
        lax.all_to_all(
            to_source(own_x).astype(jnp.bfloat16), "expert", split_axis=0, concat_axis=0, tiled=True
        ).astype(jnp.float32),
        lax.all_to_all(
            to_source(own_gate).astype(jnp.bfloat16),
            "expert",
            split_axis=0,
            concat_axis=0,
            tiled=True,
        ).astype(jnp.float32),
    )
    grad_x = jnp.dot(
        picker.astype(jnp.float32).T,
        ret_x.reshape(experts_all * capacity, width),
        precision=lax.Precision.HIGHEST,
        preferred_element_type=jnp.float32,
    ).astype(jnp.bfloat16)
    grad_combine = jnp.sum(
        jnp.where(chosen, ret_gate.reshape(-1)[:, None], jnp.float32(0.0)), axis=0
    ).reshape(tokens_here, top_count)
    return (grad_x, grad_combine, grad_w_in, grad_w_out)


def solution(mesh):
    placed = (
        P(("dp", "seq", "expert"), None),
        P(("dp", "seq", "expert"), None),
        P(("dp", "seq", "expert"), None),
        P(("dp", "seq", "expert"), None),
        P("expert", None, ("dp", "seq")),
        P("expert", ("dp", "seq"), None),
    )
    return jax.shard_map(
        local,
        mesh=mesh,
        in_specs=placed,
        out_specs=(
            P(("dp", "seq", "expert"), None),
            P(("dp", "seq", "expert"), None),
            P("expert", None, ("dp", "seq")),
            P("expert", ("dp", "seq"), None),
        ),
        check_vma=False,
    )
```

profile of v0, /device:TPU:0, one launch (start us, length us, event | category | flops | bytes accessed | tf_op | source)
XLA Modules:
  0.0 281.3 jit_solution(5066833093765969339)
XLA Ops:
  7.2 0.9 copy.37
  9.6 0.7 multiply_add_fusion.2
  10.3 1.3 convolution_convert_fusion.1
  11.8 23.2 %all_to_all.30 = bf16[16,20,1152]{2,1,0:T(8,128)(2,1)S(1)} all-to-all(bf16[16,20,1152]{2,1,0:T(8,128)(2,1)S(1)} %reshape.178), channel_id=1, replica_groups=mesh['dp'=4,'seq'=2,'expert'=16] {'expert'}, dimensions={0} | all-to-all | bytes 1474560 | tf_op jit(solution)/shard_map/all_to_all | solution.py:46
  35.0 1.0 reshape_transpose_reshape.10
  36.6 17.8 %all_to_all.31 = bf16[16,20,1152]{2,1,0:T(8,128)(2,1)S(1)} all-to-all(bf16[16,20,1152]{2,1,0:T(8,128)(2,1)S(1)} %reshape.175), channel_id=1, replica_groups=mesh['dp'=4,'seq'=2,'expert'=16] {'expert'}, dimensions={0} | all-to-all | bytes 1474560 | tf_op jit(solution)/shard_map/all_to_all | solution.py:47
  54.4 1.0 reshape_transpose_reshape.4
  55.5 17.5 %all-gather.5.cloned.1.call-done = bf16[1,2560,1152]{2,1,0:T(8,128)(2,1)} async-done(((bf16[1,320,1152]{2,1,0:T(8,128)(2,1)}), bf16[1,2560,1152]{2,1,0:T(8,128)(2,1)}) %all-gather.5.cloned.1.call-update) | async-done | bytes 5898256 | tf_op jit(solution)/shard_map/all_gather | solution.py:59
  73.0 8.5 %fusion.20 = f32[2560,576]{0,1:T(8,128)} fusion(bf16[1,2560,1152]{2,1,0:T(8,128)(2,1)} %all-gather.5.cloned.1.call-done, bf16[1,1152,576]{1,2,0:T(8,128)(2,1)S(1)} %copy-done), kind=kOutput, calls=%fused_computation.26 | convolution fusion | flops 3397386240 | bytes 13123584 | tf_op jit(solution)/shard_map/erd,edf->erf/dot_general | solution.py:65
  81.4 33.1 %all-gather.3.cloned.1.call-done = bf16[1,2560,1152]{2,1,0:T(8,128)(2,1)} async-done(((bf16[1,320,1152]{2,1,0:T(8,128)(2,1)}), bf16[1,2560,1152]{2,1,0:T(8,128)(2,1)}) %all-gather.3.cloned.1.call-update) | async-done | bytes 5898256 | tf_op jit(solution)/shard_map/all_gather | solution.py:60
  114.6 9.7 %fusion.1 = (bf16[2560]{0:T(1024)(128)(2,1)S(1)}, f32[2560,576]{0,1:T(8,128)}) fusion(f32[2560,576]{0,1:T(8,128)} %fusion.20, bf16[1,576,1152]{2,1,0:T(8,128)(2,1)S(1)} %copy-done.4, bf16[1,2560,1152]{2,1,0:T(8,128)(2,1)} %all-gather.3.cloned.1.call-done), kind=kOutput, calls=%fused_computation.7 | convolution fusion | flops 3415078400 | bytes 19026944 | tf_op jit(solution)/shard_map/erd,efd->erf/dot_general | solution.py:67
  124.2 1.2 reshape_bitcast_fusion
  125.5 31.4 %reduce-scatter.7.cloned.1.call-done = bf16[320,1]{1,0:T(8,128)(2,1)} async-done(((bf16[2560,1]{1,0:T(8,128)(2,1)}), bf16[320,1]{1,0:T(8,128)(2,1)}) %reduce-scatter.7.cloned.1.call-update) | async-done | bytes 656
  156.9 1.0 bitcast_reduce_fusion
  157.9 0.7 convert_element_type.140
  158.6 6.9 %all-to-all-start.4 = ((bf16[16,1,20]{2,1,0:T(2,128)(2,1)}), bf16[16,1,20]{2,1,0:T(2,128)(2,1)S(1)}, u32[]{:S(2)}, u32[]{:S(2)}) async-start(bf16[16,1,20]{2,1,0:T(2,128)(2,1)} %convert_element_type.140), calls=%async_computation.5 | async-start | bytes 16384 | tf_op jit(solution)/shard_map/all_to_all | solution.py:96
  165.8 7.2 %all-to-all-done.4 = bf16[16,1,20]{2,1,0:T(2,128)(2,1)S(1)} async-done(((bf16[16,1,20]{2,1,0:T(2,128)(2,1)}), bf16[16,1,20]{2,1,0:T(2,128)(2,1)S(1)}, u32[]{:S(2)}, u32[]{:S(2)}) %all-to-all-start.4) | async-done | bytes 672 | tf_op jit(solution)/shard_map/all_to_all | solution.py:96
  173.4 0.7 convert_element_type.139
  174.1 3.5 %all-to-all-start = ((bf16[16,1,20]{2,1,0:T(2,128)(2,1)}), bf16[16,1,20]{2,1,0:T(2,128)(2,1)S(1)}, u32[]{:S(2)}, u32[]{:S(2)}) async-start(bf16[16,1,20]{2,1,0:T(2,128)(2,1)} %convert_element_type.139), calls=%async_computation | async-start | bytes 16384 | tf_op jit(solution)/shard_map/all_to_all | solution.py:48
  178.8 6.1 %all-to-all-done = bf16[16,1,20]{2,1,0:T(2,128)(2,1)S(1)} async-done(((bf16[16,1,20]{2,1,0:T(2,128)(2,1)}), bf16[16,1,20]{2,1,0:T(2,128)(2,1)S(1)}, u32[]{:S(2)}, u32[]{:S(2)}) %all-to-all-start) | async-done | bytes 672 | tf_op jit(solution)/shard_map/all_to_all | solution.py:48
  185.4 12.8 %all-reduce = bf16[2560]{0:T(1024)(128)(2,1)S(1)} all-reduce(bf16[2560]{0:T(1024)(128)(2,1)S(1)} %dynamic-update-slice), channel_id=1, replica_groups=mesh['dp'=4,'seq'=2,'expert'=16] {'dp','seq'}, use_global_device_ids=true, to_apply=%add | all-reduce | flops 2560 | bytes 10240
  198.2 6.7 %fusion.9 = bf16[2560,576]{0,1:T(8,128)(2,1)S(1)} fusion(f32[2560,576]{0,1:T(8,128)} %fusion.20, f32[2560,576]{0,1:T(8,128)} %get-tuple-element.23, f32[2560]{0:T(1024)S(1)} %mul.143), kind=kLoop, calls=%fused_computation.15 | loop fusion | flops 29491200 | bytes 14755840 | tf_op jit(solution)/shard_map/convert_element_type | solution.py:73
  204.9 1.6 copy-done.1
  206.5 7.0 %fusion = bf16[1,2560,1152]{2,1,0:T(8,128)(2,1)} fusion(bf16[2560,576]{0,1:T(8,128)(2,1)S(1)} %fusion.9, bf16[1,1152,576]{1,2,0:T(8,128)(2,1)S(1)} %copy-done), kind=kOutput, calls=%fused_computation.1 | convolution fusion | flops 3400335360 | bytes 10174464 | tf_op jit(solution)/shard_map/erf,edf->erd/dot_general | solution.py:77
  213.7 0.6 copy.44
  214.4 11.2 %fusion.37 = bf16[1,576,1152]{2,1,0:T(8,128)(2,1)} fusion(bf16[1,2560,1152]{2,1,0:T(8,128)(2,1)} %all-gather.3.cloned.1.call-done, f32[2560]{0:T(1024)S(1)} %mul.143, f32[2560,576]{0,1:T(8,128)} %fusion.20), kind=kOutput, calls=%fused_computation.36 | convolution fusion | flops 3415744512 | bytes 13133824 | tf_op jit(solution)/shard_map/erf,erd->efd/dot_general | solution.py:70
  225.6 24.7 %reduce-scatter.5.cloned.1.call-done = bf16[1,320,1152]{2,1,0:T(8,128)(2,1)} async-done(((bf16[1,2560,1152]{2,1,0:T(8,128)(2,1)}), bf16[1,320,1152]{2,1,0:T(8,128)(2,1)}) %reduce-scatter.5.cloned.1.call-update) | async-done | bytes 737296 | tf_op jit(solution)/shard_map/reduce_scatter | solution.py:79
  250.3 2.1 convert_element_type.124
  252.4 6.9 %all-to-all-start.3 = ((bf16[16,20,1152]{2,1,0:T(8,128)(2,1)}), bf16[16,20,1152]{2,1,0:T(8,128)(2,1)S(1)}, u32[]{:S(2)}, u32[]{:S(2)}) async-start(bf16[16,20,1152]{2,1,0:T(8,128)(2,1)} %convert_element_type.124), calls=%async_computation.4 | async-start | bytes 1769472 | tf_op jit(solution)/shard_map/all_to_all | solution.py:93
  259.4 8.6 %fusion.34 = bf16[1,1152,576]{1,2,0:T(8,128)(2,1)} fusion(bf16[2560,576]{0,1:T(8,128)(2,1)} %copy-done.1, bf16[1,2560,1152]{2,1,0:T(8,128)(2,1)} %all-gather.5.cloned.1.call-done), kind=kOutput, calls=%fused_computation.35 | convolution fusion | flops 3398049792 | bytes 10174464 | tf_op jit(solution)/shard_map/erd,erf->edf/dot_general | solution.py:74
  268.0 5.5 %all-to-all-done.3 = bf16[16,20,1152]{2,1,0:T(8,128)(2,1)S(1)} async-done(((bf16[16,20,1152]{2,1,0:T(8,128)(2,1)}), bf16[16,20,1152]{2,1,0:T(8,128)(2,1)S(1)}, u32[]{:S(2)}, u32[]{:S(2)}) %all-to-all-start.3) | async-done | bytes 737312 | tf_op jit(solution)/shard_map/all_to_all | solution.py:93
  273.7 1.1 convolution_convert_fusion.3
  (47 shorter events, 4.2 us)
Async XLA Ops:
  7.2 65.8 %copy-start = (bf16[1,1152,576]{1,2,0:T(8,128)(2,1)S(1)}, bf16[1,1152,576]{1,2,0:T(8,128)(2,1)}, u32[]{:S(2)}) copy-start(bf16[1,1152,576]{1,2,0:T(8,128)(2,1)} %param.10) | copy-start | bytes 3981316
  7.2 28.9 %copy-start.2 = (bf16[128,1152]{1,0:T(8,128)(2,1)S(1)}, bf16[128,1152]{1,0:T(8,128)(2,1)}, u32[]{:S(2)}) copy-start(bf16[128,1152]{1,0:T(8,128)(2,1)} %param.7) | copy-start | bytes 884740
  7.2 65.8 %all-gather.5.cloned.1.call-start = ((), (), s32[]{:S(2)}) async-start(), calls=%async_computation.8 | async-start | bytes 6635520 | tf_op jit(solution)/shard_map/all_gather | solution.py:59
  36.0 78.6 %all-gather.3.cloned.1.call-start = ((), (), s32[]{:S(2)}) async-start(), calls=%async_computation.7 | async-start | bytes 6635520 | tf_op jit(solution)/shard_map/all_gather | solution.py:60
  55.4 59.2 %copy-start.4 = (bf16[1,576,1152]{2,1,0:T(8,128)(2,1)S(1)}, bf16[1,576,1152]{2,1,0:T(8,128)(2,1)}, u32[]{:S(2)}) copy-start(bf16[1,576,1152]{2,1,0:T(8,128)(2,1)} %param.11) | copy-start | bytes 3981316
  55.4 101.5 %reduce-scatter.7.cloned.1.call-start = ((), (), s32[]{:S(2)}) async-start(), calls=%async_computation.10 | async-start | bytes 737280
  81.4 84.1 %copy-start.3 = (f32[128,2]{0,1:T(2,128)S(1)}, f32[128,2]{0,1:T(2,128)}, u32[]{:S(2)}) copy-start(f32[128,2]{0,1:T(2,128)} %param.8) | copy-start | bytes 3076
  81.4 96.2 %copy-start.5 = (u32[128]{0:T(128)S(1)}, u32[128]{0:T(128)}, u32[]{:S(2)}) copy-start(u32[128]{0:T(128)} %constant.26) | copy-start | bytes 1540
  158.6 14.4 %all-to-all-start.4 = ((bf16[16,1,20]{2,1,0:T(2,128)(2,1)}), bf16[16,1,20]{2,1,0:T(2,128)(2,1)S(1)}, u32[]{:S(2)}, u32[]{:S(2)}) async-start(bf16[16,1,20]{2,1,0:T(2,128)(2,1)} %convert_element_type.140), calls=%async_computation.5 | async-start | bytes 16384 | tf_op jit(solution)/shard_map/all_to_all | solution.py:96
  174.1 10.9 %all-to-all-start = ((bf16[16,1,20]{2,1,0:T(2,128)(2,1)}), bf16[16,1,20]{2,1,0:T(2,128)(2,1)S(1)}, u32[]{:S(2)}, u32[]{:S(2)}) async-start(bf16[16,1,20]{2,1,0:T(2,128)(2,1)} %convert_element_type.139), calls=%async_computation | async-start | bytes 16384 | tf_op jit(solution)/shard_map/all_to_all | solution.py:48
  177.5 72.8 %reduce-scatter.5.cloned.1.call-start = ((), (), s32[]{:S(2)}) async-start(), calls=%async_computation.9 | async-start | bytes 6635520 | tf_op jit(solution)/shard_map/reduce_scatter | solution.py:79
  204.9 1.7 copy-start.1
  252.4 21.1 %all-to-all-start.3 = ((bf16[16,20,1152]{2,1,0:T(8,128)(2,1)}), bf16[16,20,1152]{2,1,0:T(8,128)(2,1)S(1)}, u32[]{:S(2)}, u32[]{:S(2)}) async-start(bf16[16,20,1152]{2,1,0:T(8,128)(2,1)} %convert_element_type.124), calls=%async_computation.4 | async-start | bytes 1769472 | tf_op jit(solution)/shard_map/all_to_all | solution.py:93
Sparse Core Ops, SparseCore 0:
  36.1 36.8 all-gather.4
  75.2 39.2 all-gather.2
  125.6 31.2 reduce-scatter.6
  213.7 36.5 reduce-scatter.4
where the time goes:
time: 282 us; the launch traced here: 281 us
  waiting for transfers between devices  126 us (45%)
  blocking collectives  53.8 us (19%)
  matrix products  47.7 us (17%)
  starting transfers between devices  17.4 us (6%)
  between operations  14.6 us (5%)
  local copies, waits for them, and re-layouts  13.5 us (5%)
  other arithmetic  8.43 us (3%)
    all_gather x1, waiting for transfers between devices, local(): lax.all_gather(to_local(got_dy), ('dp', 'seq'), axis=1, tiled=True)  33.1 us
    unnamed x5, waiting for transfers between devices  31.5 us
    reduce_scatter x1, waiting for transfers between devices, local(): lax.psum_scatter(part_x.astype(jnp.bfloat16), ('dp', 'seq'), scatter_dime...  24.7 us
    all_to_all x1, blocking collectives, local(): lax.all_to_all(send_x, 'expert', split_axis=0, concat_axis=0, tiled=True)  23.2 us
    all_to_all x1, blocking collectives, local(): lax.all_to_all(send_dy, 'expert', split_axis=0, concat_axis=0, tiled=True)  17.8 us
    all_gather x1, waiting for transfers between devices, local(): lax.all_gather(to_local(got_x), ('dp', 'seq'), axis=1, tiled=True)  17.5 us
    unnamed x1, blocking collectives  12.8 us
    dot_general x1, matrix products, local(): jnp.einsum('erf,erd->efd', weighted, rows_dy, preferred_element_type=jnp....  11.2 us
  transfers between devices with their start and end apart: 7, of which 7 were waited for; matrix products, arithmetic and copies ran while one was open for 11% of the time, Pallas kernels for 0%

commit v1 on v0

v1 whole, which is shorter than its diff:
```python
import functools
import math

import jax
import jax.numpy as jnp
from jax import lax
from jax.experimental import pallas as pl
from jax.experimental.pallas import tpu as pltpu
from jax.sharding import PartitionSpec as P

BF = jnp.bfloat16
F32 = jnp.float32
CHUNKS = (12, 8)
META = 16
LANES = 128
VMEM = 60 * 1024 * 1024


def mm(a, b, dims):
    return lax.dot_general(a, b, (dims, ((), ())), preferred_element_type=F32)


NN = ((1,), (0,))
NT = ((1,), (1,))
TN = ((0,), (0,))


def positions(names, experts):
    tokens = names.shape[1]
    expert = lax.broadcasted_iota(jnp.int32, (experts, tokens), 0).astype(F32)
    member = (names[0:1] == expert) | (names[1:2] == expert)
    first = lax.broadcasted_iota(jnp.int32, (tokens, tokens), 0)
    second = lax.broadcasted_iota(jnp.int32, (tokens, tokens), 1)
    earlier = jnp.where(first < second, 1.0, 0.0).astype(BF)
    count = mm(jnp.where(member, 1.0, 0.0).astype(BF), earlier, NN)
    return jnp.where(member, count, -1.0)


def row_owner(experts, span):
    rows = experts * span
    row = lax.broadcasted_iota(jnp.int32, (rows, experts), 0)
    expert = lax.broadcasted_iota(jnp.int32, (rows, experts), 1)
    own = (row >= expert * span) & (row < (expert + 1) * span)
    number = jnp.sum(jnp.where(own, expert, 0).astype(F32), axis=1, keepdims=True)
    slot = row[:, 0:1].astype(F32) - number * span
    return jnp.where(own, 1.0, 0.0).astype(BF), number, slot


def prep_kernel(experts, chunks, x_ref, dy_ref, names_ref, gates_ref, *outs):
    msg_ref, xs_ref = outs
    tokens, width = x_ref.shape
    names = names_ref[...].astype(F32)
    gates = gates_ref[...]
    high = gates.astype(BF).astype(F32)
    low = gates - high
    msg_ref[0:tokens, :] = dy_ref[...]
    line = lax.broadcasted_iota(jnp.int32, (META, tokens), 0)
    meta = jnp.zeros((META, tokens), F32)
    for at, part in enumerate((names, high, low)):
        for k in range(2):
            meta = jnp.where(line == 2 * at + k, part[k : k + 1], meta)
    msg_ref[tokens:, :] = jnp.zeros((META, width), BF)
    msg_ref[tokens:, 0:tokens] = meta.astype(BF)
    pos = positions(names, experts)
    span = sum(chunks)
    own, _, slot = row_owner(experts, span)
    picker = mm(own, pos.astype(BF), NN) == slot
    xs_ref[...] = mm(jnp.where(picker, 1.0, 0.0).astype(BF), x_ref[...], NN).astype(BF)


def expand_kernel(experts, chunks, *refs):
    blocks = len(refs) - len(chunks)
    msgs, outs = refs[:blocks], refs[blocks:]
    tokens = msgs[0].shape[0] - META
    dy = jnp.concatenate([m[0:tokens, :] for m in msgs], axis=0)
    expert = lax.broadcasted_iota(jnp.int32, (experts, tokens), 0).astype(F32)
    pos, gate = [], []
    for m in msgs:
        meta = m[tokens:, 0:tokens].astype(F32)
        pos.append(positions(meta[0:2], experts))
        both = meta[2:4] + meta[4:6]
        gate.append(
            jnp.where(meta[0:1] == expert, both[0:1], 0.0)
            + jnp.where(meta[1:2] == expert, both[1:2], 0.0)
        )
    gate = jnp.concatenate(gate, axis=1)
    high = gate.astype(BF)
    low = (gate - high.astype(F32)).astype(BF)
    base = 0
    for s, out in zip(chunks, outs):
        own, _, slot = row_owner(experts, blocks * s)
        here = jnp.concatenate(
            [
                jnp.where((p >= base) & (p < base + s), p - base + k * s, -1.0)
                for k, p in enumerate(pos)
            ],
            axis=1,
        )
        picker = mm(own, here.astype(BF), NN) == slot
        row_gate = jnp.sum(
            jnp.where(picker, mm(own, high, NN) + mm(own, low, NN), 0.0), axis=1, keepdims=True
        )
        rows = mm(jnp.where(picker, 1.0, 0.0).astype(BF), dy, NN)
        out[...] = (rows * row_gate).astype(BF)
        base += s


def rows_kernel(x_ref, dy_ref, wi_ref, wo_ref, hid_ref, dpre_ref, dx_ref):
    width = x_ref.shape[1]
    coeff = math.sqrt(2.0 / math.pi)
    pre = mm(wi_ref[...], x_ref[...], NT)
    back = mm(wo_ref[...], dy_ref[...], NT)
    square = pre * pre
    tanh = jnp.tanh(coeff * pre * (1.0 + 0.044715 * square))
    half = 0.5 * (1.0 + tanh)
    hidden = (pre * half).astype(BF)
    slope = half + 0.5 * coeff * pre * (1.0 - tanh * tanh) * (1.0 + 3.0 * 0.044715 * square)
    dpre = (back * slope).astype(BF)
    hid_ref[...] = hidden
    dpre_ref[...] = dpre
    prod = hidden.astype(F32) * back
    part = jnp.sum(prod.reshape(prod.shape[0] // 16, 16, prod.shape[1]), axis=0).astype(BF)
    line = lax.broadcasted_iota(jnp.int32, (16, LANES), 0)
    lane = lax.broadcasted_iota(jnp.int32, (16, LANES), 1)
    dx_ref[:, 0:width] = mm(dpre, wi_ref[...], TN).astype(BF)
    dx_ref[:, width:] = mm(part, jnp.where(line == lane, 1.0, 0.0).astype(BF), TN).astype(BF)


def weights_kernel(count, add, *refs):
    per = 4
    ins, rest = refs[: per * count], refs[per * count :]
    total_o = total_i = None
    for c in range(count):
        hid, dpre, x, dy = ins[per * c : per * c + per]
        part_o = mm(hid[...], dy[...], NN)
        part_i = mm(dpre[...], x[...], NN)
        total_o = part_o if c == 0 else total_o + part_o
        total_i = part_i if c == 0 else total_i + part_i
    if add:
        got_o, got_i, out_o, out_i = rest
        total_o = total_o + got_o[...].astype(F32)
        total_i = total_i + got_i[...].astype(F32)
    else:
        out_o, out_i = rest
    out_o[...] = total_o.astype(BF)
    out_i[...] = total_i.astype(BF)


def combine_kernel(experts, chunks, *refs):
    names_ref, gates_ref = refs[:2]
    rets = refs[2 : 2 + len(chunks)]
    dx_ref, gate_ref = refs[2 + len(chunks) :]
    width = dx_ref.shape[1]
    names = names_ref[...].astype(F32)
    pos = positions(names, experts)
    base, total = 0, None
    sums = [None, None]
    for s, ret in zip(chunks, rets):
        own, number, slot = row_owner(experts, s)
        here = jnp.where((pos >= base) & (pos < base + s), pos - base, -1.0)
        picker = mm(own, here.astype(BF), NN) == slot
        part = mm(jnp.where(picker, 1.0, 0.0).astype(BF), ret[:, 0:width], TN)
        total = part if total is None else total + part
        value = jnp.sum(ret[:, width:].astype(F32), axis=1, keepdims=True)
        for k in range(2):
            mine = jnp.sum(
                jnp.where(picker & (names[k : k + 1] == number), value, 0.0), axis=0, keepdims=True
            )
            sums[k] = mine if sums[k] is None else sums[k] + mine
        base += s
    dx_ref[...] = total.astype(BF)
    line = lax.broadcasted_iota(jnp.int32, gate_ref.shape, 0)
    gate_ref[...] = jnp.where(line == 0, sums[0], sums[1]) / gates_ref[...]


def call(kernel, outs, flops, moved, **more):
    return pl.pallas_call(
        kernel,
        out_shape=outs,
        compiler_params=pltpu.CompilerParams(vmem_limit_bytes=VMEM),
        cost_estimate=pl.CostEstimate(flops=int(flops), bytes_accessed=int(moved), transcendentals=0),
        **more,
    )


def shift(value, axis, by):
    size = lax.axis_size(axis)
    return lax.ppermute(value, axis, [(i, (i + by) % size) for i in range(size)])


def exchange(value):
    return lax.all_to_all(value, "expert", split_axis=0, concat_axis=0, tiled=True)


def local(hidden_in, grad_out, combine, routes, w_in, w_out):
    tokens, width = hidden_in.shape
    units = w_out.shape[1]
    experts = lax.axis_size("expert")
    planes = lax.axis_size("dp")
    cap = sum(CHUNKS)
    names, gates = routes.T, combine.T
    wi = w_in[0].T
    wo = w_out[0]
    wi = jnp.concatenate([wi, shift(wi, "seq", 1)], axis=0)
    wo = jnp.concatenate([wo, shift(wo, "seq", 1)], axis=0)
    hidden_units = 2 * units

    def arr(*shape, kind=BF):
        return jax.ShapeDtypeStruct(shape, kind)

    msg, xs = call(
        functools.partial(prep_kernel, experts, CHUNKS),
        [arr(tokens + META, width), arr(experts * cap, width)],
        2 * experts * cap * tokens * width,
        3e6,
    )(hidden_in, grad_out, names, gates)
    msgs = [msg] + [shift(msg, "dp", k) for k in range(1, planes)]
    xa = exchange(xs)
    xall = [xa] + [shift(xa, "dp", k) for k in range(1, planes)]
    sent = call(
        functools.partial(expand_kernel, experts, CHUNKS),
        [arr(experts * planes * s, width) for s in CHUNKS],
        2 * experts * planes * cap * planes * tokens * width,
        5e6,
    )(*msgs)
    base = 0
    done, rets = [], []
    for s, rows in zip(CHUNKS, sent):
        got = exchange(rows)
        got = got.reshape(experts, planes, s, width).swapaxes(0, 1)
        dy = got.reshape(planes * experts * s, width)
        x = jnp.concatenate(
            [
                v.reshape(experts, cap, width)[:, base : base + s].reshape(experts * s, width)
                for v in xall
            ],
            axis=0,
        )
        base += s
        count = x.shape[0]
        tile = 256
        hid, dpre, dx = call(
            rows_kernel,
            [arr(hidden_units, count), arr(hidden_units, count), arr(count, width + LANES)],
            6 * count * hidden_units * width,
            15e6,
            grid=(count // tile,),
            in_specs=[
                pl.BlockSpec((tile, width), lambda i: (i, 0)),
                pl.BlockSpec((tile, width), lambda i: (i, 0)),
                pl.BlockSpec((hidden_units, width), lambda i: (0, 0)),
                pl.BlockSpec((hidden_units, width), lambda i: (0, 0)),
            ],
            out_specs=[
                pl.BlockSpec((hidden_units, tile), lambda i: (0, i)),
                pl.BlockSpec((hidden_units, tile), lambda i: (0, i)),
                pl.BlockSpec((tile, width + LANES), lambda i: (i, 0)),
            ],
        )(x, dy, wi, wo)
        done.append((hid, dpre, x, dy))
        block = experts * s
        own = dx[0:block].astype(F32)
        for k in range(1, planes):
            own = own + shift(dx[k * block : (k + 1) * block], "dp", -k).astype(F32)
        rets.append(exchange(own.astype(BF)))

    def weight_call(half, extra):
        tiles = 2
        size = units // tiles
        specs, args = [], []
        for hid, dpre, x, dy in done:
            count = x.shape[0]
            specs += [pl.BlockSpec((size, count), lambda i: (half * tiles + i, 0))] * 2
            specs += [pl.BlockSpec((count, width), lambda i: (0, 0))] * 2
            args += [hid, dpre, x, dy]
        block = pl.BlockSpec((size, width), lambda i: (i, 0))
        return call(
            functools.partial(weights_kernel, len(done), bool(extra)),
            [arr(units, width), arr(units, width)],
            4 * units * width * planes * experts * cap,
            12e6,
            grid=(tiles,),
            in_specs=specs + [block] * len(extra),
            out_specs=[block, block],
        )(*args, *extra)

    theirs = weight_call(1, ())
    received = [shift(v, "seq", 1) for v in theirs]
    grad_wo, grad_wi = weight_call(0, tuple(received))
    grad_x, grad_gate = call(
        functools.partial(combine_kernel, experts, CHUNKS),
        [arr(tokens, width), arr(2, tokens, kind=F32)],
        2 * experts * cap * tokens * width,
        2e6,
    )(names, gates, *rets)
    return grad_x, grad_gate.T, grad_wi.T[None], grad_wo[None]


def solution(mesh):
    rows = P(("dp", "seq", "expert"), None)
    first = P("expert", None, ("dp", "seq"))
    second = P("expert", ("dp", "seq"), None)
    return jax.shard_map(
        local,
        mesh=mesh,
        in_specs=(rows, rows, rows, rows, first, second),
        out_specs=(rows, rows, first, second),
        check_vma=False,
    )
```

time: 282 us -> 217 us (0.77)
  blocking collectives: 53.8 us -> 0 us
  Pallas kernels: 0 us -> 51.4 us
  matrix products: 47.7 us -> 0 us
  waiting for transfers between devices: 126 us -> 80.8 us
  starting transfers between devices: 17.4 us -> 42 us
  local copies, waits for them, and re-layouts: 13.5 us -> 29.7 us
  between operations: 14.6 us -> 0.92 us
  other arithmetic: 8.43 us -> 11.8 us
    ppermute x0 -> x16, waiting for transfers between devices: none -> 53.5 us  [shift(): lax.ppermute(value, axis, [(i, (i + by) % size) for i in range(size)])]
    pallas_call x0 -> x7, Pallas kernels: none -> 51.4 us  [the longest x2 23.8 us: local(): call(rows_kernel, [arr(hidden_units, count), arr(hidden_units, count), ar...]
    all_gather x2 -> x0, waiting for transfers between devices: 50.6 us -> none  [the longest x1 33.1 us: local(): lax.all_gather(to_local(got_dy), ('dp', 'seq'), axis=1, tiled=True)]
    dot_general x8 -> x0, matrix products: 47.7 us -> none  [the longest x1 11.2 us: local(): jnp.einsum('erf,erd->efd', weighted, rows_dy, preferred_element_type=jnp....]
    all_to_all x2 -> x0, blocking collectives: 41 us -> none  [the longest x1 23.2 us: local(): lax.all_to_all(send_x, 'expert', split_axis=0, concat_axis=0, tiled=True)]
    unnamed x5 -> x0, waiting for transfers between devices: 31.5 us -> none
    reduce_scatter x1 -> x0, waiting for transfers between devices: 24.7 us -> none  [local(): lax.psum_scatter(part_x.astype(jnp.bfloat16), ('dp', 'seq'), scatter_dime...]
    unnamed x1 -> x0, blocking collectives: 12.8 us -> none
  transfers between devices with their start and end apart: 7 -> 21, of which waited for: 7 -> 11; matrix products, arithmetic and copies ran while one was open for 11% -> 13% of each run, Pallas kernels for 0% -> 12%
where the time goes in v1:
time: 217 us; the launch traced here: 216 us
  waiting for transfers between devices  80.8 us (37%)
  Pallas kernels  51.4 us (24%)
  starting transfers between devices  42 us (19%)
  local copies, waits for them, and re-layouts  29.7 us (14%)
  other arithmetic  11.8 us (5%)
    ppermute x16, waiting for transfers between devices, shift(): lax.ppermute(value, axis, [(i, (i + by) % size) for i in range(size)])  53.5 us
    all_to_all x5, starting transfers between devices, exchange(): lax.all_to_all(value, 'expert', split_axis=0, concat_axis=0, tiled=True)  30 us
    all_to_all x5, waiting for transfers between devices, exchange(): lax.all_to_all(value, 'expert', split_axis=0, concat_axis=0, tiled=True)  27.3 us
    pallas_call x2, Pallas kernels, local(): call(rows_kernel, [arr(hidden_units, count), arr(hidden_units, count), ar...  23.8 us
    pallas_call x2, Pallas kernels, weight_call(): call(functools.partial(weights_kernel, len(done), bool(extra)), [arr(unit...  17.2 us
    ppermute x16, starting transfers between devices, shift(): lax.ppermute(value, axis, [(i, (i + by) % size) for i in range(size)])  12 us
    reshape x11, local copies, waits for them, and re-layouts, local(): v.reshape(experts, cap, width)[:, base:base + s].reshape(experts * s, width)  11 us
    unnamed x35, local copies, waits for them, and re-layouts  6.7 us
  transfers between devices with their start and end apart: 21, of which 11 were waited for; matrix products, arithmetic and copies ran while one was open for 13% of the time, Pallas kernels for 12%

profile of v1, /device:TPU:0, one launch (start us, length us, event | category | flops | bytes accessed | tf_op | source)
XLA Modules:
  0.0 216.5 jit_solution(17008294176144347938)
XLA Ops:
  0.6 2.6 %shard_map.93 = (bf16[144,1152]{1,0:T(8,128)(2,1)}, bf16[320,1152]{1,0:T(8,128)(2,1)}) custom-call(bf16[128,1152]{1,0:T(8,128)(2,1)} %x_ref.1, bf16[128,1152]{1,0:T(8,128)(2,1)} %dy_ref.1, s32[2,128]{1,0:T(2,128)} %bitcast.38, f32[2,128]{1,0:T(2,128)} %bitcast.40), custom_call_target="tpu_custom_call" | custom-call | flops 94371840 | bytes 3000000 | tf_op jit(solution)/shard_map/pallas_call | solution.py:211
  3.2 2.1 all_to_all.34
  5.3 8.0 %all-to-all-start = ((bf16[16,20,1152]{2,1,0:T(8,128)(2,1)}), bf16[16,20,1152]{2,1,0:T(8,128)(2,1)S(1)}, u32[]{:S(2)}, u32[]{:S(2)}) async-start(bf16[16,20,1152]{2,1,0:T(8,128)(2,1)} %all_to_all.34), calls=%async_computation | async-start | bytes 1769472 | tf_op jit(solution)/shard_map/all_to_all | solution.py:192
  13.4 3.1 %collective-permute-start.5 = (bf16[144,1152]{1,0:T(8,128)(2,1)S(1)}, bf16[144,1152]{1,0:T(8,128)(2,1)S(1)}, u32[]{:S(2)}, u32[]{:S(2)}) collective-permute-start(bf16[144,1152]{1,0:T(8,128)(2,1)S(1)} %copy-done.12), channel_id=1, source_target_pairs={{0,96},{32,0},{64,32},{96,64},{1,97},{33,1},{65,33},{97,65},{2,98}... | collective-permute-start | bytes 995336 | tf_op jit(solution)/shard_map/ppermute | solution.py:188
  18.1 13.2 %collective-permute-done.5.refs_3_ = bf16[144,1152]{1,0:T(8,128)(2,1)S(1)} collective-permute-done((bf16[144,1152]{1,0:T(8,128)(2,1)S(1)}, bf16[144,1152]{1,0:T(8,128)(2,1)S(1)}, u32[]{:S(2)}, u32[]{:S(2)}) %collective-permute-start.5) | collective-permute-done | bytes 331808 | tf_op jit(solution)/shard_map/ppermute | solution.py:188
  31.3 3.7 %collective-permute-done.3.refs_1_ = bf16[144,1152]{1,0:T(8,128)(2,1)S(1)} collective-permute-done((bf16[144,1152]{1,0:T(8,128)(2,1)S(1)}, bf16[144,1152]{1,0:T(8,128)(2,1)S(1)}, u32[]{:S(2)}, u32[]{:S(2)}) %collective-permute-start.3) | collective-permute-done | bytes 331808 | tf_op jit(solution)/shard_map/ppermute | solution.py:188
  35.7 5.3 %shard_map.94 = (bf16[768,1152]{1,0:T(8,128)(2,1)}, bf16[512,1152]{1,0:T(8,128)(2,1)}) custom-call(bf16[144,1152]{1,0:T(8,128)(2,1)} %get-tuple-element.21.refs_0_, bf16[144,1152]{1,0:T(8,128)(2,1)} %copy-done.15, bf16[144,1152]{1,0:T(8,128)(2,1)} %copy-done.14, bf16[144,1152]{1,0:T(8,128)(2,1)} %copy-done.13), custom_call_target="tpu_custom_call" | custom-call | flops 1509949440 | bytes 5000000 | tf_op jit(solution)/shard_map/pallas_call | solution.py:220
  41.0 7.1 %all-to-all-start.3 = ((bf16[16,32,1152]{2,1,0:T(8,128)(2,1)}), bf16[16,32,1152]{2,1,0:T(8,128)(2,1)S(1)}, u32[]{:S(2)}, u32[]{:S(2)}) async-start(bf16[16,32,1152]{2,1,0:T(8,128)(2,1)} %bitcast.37), calls=%async_computation.3 | async-start | bytes 2359296 | tf_op jit(solution)/shard_map/all_to_all | solution.py:192
  53.0 3.4 %pad_maximum_fusion.wi_ref = bf16[1152,1152]{1,0:T(8,128)(2,1)} fusion(bf16[576,1152]{1,0:T(8,128)(2,1)} %collective-permute-done.6, bf16[576,1152]{1,0:T(8,128)(2,1)} %bitcast.6), kind=kLoop, calls=%fused_computation | loop fusion | flops 5308416 | bytes 5308416 | tf_op jit(solution)/shard_map/concatenate | solution.py:204
  56.5 3.5 %pad_maximum_fusion.1.wo_ref = bf16[1152,1152]{1,0:T(8,128)(2,1)} fusion(bf16[576,1152]{1,0:T(8,128)(2,1)} %collective-permute-done.7, bf16[576,1152]{1,0:T(8,128)(2,1)} %bitcast.8), kind=kLoop, calls=%fused_computation.1 | loop fusion | flops 5308416 | bytes 5308416 | tf_op jit(solution)/shard_map/concatenate | solution.py:205
  59.9 9.0 %collective-permute-done.2 = bf16[320,1152]{1,0:T(8,128)(2,1)} collective-permute-done((bf16[320,1152]{1,0:T(8,128)(2,1)}, bf16[320,1152]{1,0:T(8,128)(2,1)}, u32[]{:S(2)}, u32[]{:S(2)}) %collective-permute-start.2) | collective-permute-done | bytes 737312 | tf_op jit(solution)/shard_map/ppermute | solution.py:188
  73.7 11.4 %collective-permute-done = bf16[320,1152]{1,0:T(8,128)(2,1)} collective-permute-done((bf16[320,1152]{1,0:T(8,128)(2,1)}, bf16[320,1152]{1,0:T(8,128)(2,1)}, u32[]{:S(2)}, u32[]{:S(2)}) %collective-permute-start) | collective-permute-done | bytes 737312 | tf_op jit(solution)/shard_map/ppermute | solution.py:188
  88.6 1.9 slice_bitcast_fusion
  90.5 7.1 %all-to-all-start.1 = ((bf16[16,48,1152]{2,1,0:T(8,128)(2,1)}), bf16[16,48,1152]{2,1,0:T(8,128)(2,1)S(1)}, u32[]{:S(2)}, u32[]{:S(2)}) async-start(bf16[16,48,1152]{2,1,0:T(8,128)(2,1)} %bitcast.36), calls=%async_computation.1 | async-start | bytes 3538944 | tf_op jit(solution)/shard_map/all_to_all | solution.py:192
  103.1 10.3 %shard_map.96 = (bf16[1152,512]{1,0:T(8,128)(2,1)}, bf16[1152,512]{1,0:T(8,128)(2,1)}, bf16[512,1280]{1,0:T(8,128)(2,1)}) custom-call(bf16[512,1152]{1,0:T(8,128)(2,1)} %pad_maximum_fusion.2.x_ref.refs_6_, bf16[512,1152]{1,0:T(8,128)(2,1)} %bitcast.32, bf16[1152,1152]{1,0:T(8,128)(2,1)} %pad_maximum_fusion.wi_ref, bf16[1152,1152]{1,0:T(8,128)(2,1)} %pad_maximum_fusion.1.wo_ref), custom_call_target="tpu_custom_call" | custom-call | flops 4076863488 | bytes 15000000 | tf_op jit(solution)/shard_map/pallas_call | solution.py:242
  113.3 11.7 %all-to-all-done.1 = bf16[16,48,1152]{2,1,0:T(8,128)(2,1)S(1)} async-done(((bf16[16,48,1152]{2,1,0:T(8,128)(2,1)}), bf16[16,48,1152]{2,1,0:T(8,128)(2,1)S(1)}, u32[]{:S(2)}, u32[]{:S(2)}) %all-to-all-start.1) | async-done | bytes 1769504 | tf_op jit(solution)/shard_map/all_to_all | solution.py:192
  125.8 1.5 reshape.79.dy_ref.refs_3_
  127.3 13.5 %shard_map.95 = (bf16[1152,768]{1,0:T(8,128)(2,1)}, bf16[1152,768]{1,0:T(8,128)(2,1)}, bf16[768,1280]{1,0:T(8,128)(2,1)}) custom-call(bf16[768,1152]{1,0:T(8,128)(2,1)} %constant_dynamic-update-slice_fusion.x_ref.refs_2_, bf16[768,1152]{1,0:T(8,128)(2,1)} %reshape.79.dy_ref.refs_3_, bf16[1152,1152]{1,0:T(8,128)(2,1)} %pad_maximum_fusion.wi_ref, ...), custom_call_target="tpu_custom_call" | custom-call | flops 6115295232 | bytes 15000000 | tf_op jit(solution)/shard_map/pallas_call | solution.py:242
  142.8 1.6 collective-permute-start.10
  145.9 2.2 %collective-permute-start.11 = (bf16[128,1280]{1,0:T(8,128)(2,1)}, bf16[128,1280]{1,0:T(8,128)(2,1)}, u32[]{:S(2)}, u32[]{:S(2)}) collective-permute-start(bf16[128,1280]{1,0:T(8,128)(2,1)} %get-tuple-element.39), channel_id=1, source_target_pairs={{0,96},{32,0},{64,32},{96,64},{1,97},{33,1},{65,33},{97,65},{2,98}... | collective-permute-start | bytes 983048 | tf_op jit(solution)/shard_map/ppermute | solution.py:188
  148.1 8.4 %shard_map.98 = (bf16[576,1152]{1,0:T(8,128)(2,1)}, bf16[576,1152]{1,0:T(8,128)(2,1)}) custom-call(bf16[1152,768]{1,0:T(8,128)(2,1)} %get-tuple-element.28.refs_0_, bf16[1152,768]{1,0:T(8,128)(2,1)} %get-tuple-element.29.refs_1_, bf16[768,1152]{1,0:T(8,128)(2,1)} %constant_dynamic-update-slice_fusion.x_ref.refs_2_, ...), custom_call_target="tpu_custom_call" | custom-call | flops 3397386240 | bytes 12000000 | tf_op jit(solution)/shard_map/pallas_call | solution.py:277
  156.5 6.9 %collective-permute-done.8 = bf16[192,1280]{1,0:T(8,128)(2,1)S(1)} collective-permute-done((bf16[192,1280]{1,0:T(8,128)(2,1)S(1)}, bf16[192,1280]{1,0:T(8,128)(2,1)S(1)}, u32[]{:S(2)}, u32[]{:S(2)}) %collective-permute-start.8) | collective-permute-done | bytes 491552 | tf_op jit(solution)/shard_map/ppermute | solution.py:188
  163.4 5.3 %collective-permute-done.10 = bf16[192,1280]{1,0:T(8,128)(2,1)S(1)} collective-permute-done((bf16[192,1280]{1,0:T(8,128)(2,1)S(1)}, bf16[192,1280]{1,0:T(8,128)(2,1)S(1)}, u32[]{:S(2)}, u32[]{:S(2)}) %collective-permute-start.10) | collective-permute-done | bytes 491552 | tf_op jit(solution)/shard_map/ppermute | solution.py:188
  170.1 1.6 add_convert_fusion
  172.6 3.6 %all-to-all-start.2 = ((bf16[16,12,1280]{2,1,0:T(8,128)(2,1)}), bf16[16,12,1280]{2,1,0:T(8,128)(2,1)S(1)}, u32[]{:S(2)}, u32[]{:S(2)}) async-start(bf16[16,12,1280]{2,1,0:T(8,128)(2,1)} %all_to_all.39), calls=%async_computation.2 | async-start | bytes 1310720 | tf_op jit(solution)/shard_map/all_to_all | solution.py:192
  176.2 3.9 %collective-permute-done.13 = bf16[128,1280]{1,0:T(8,128)(2,1)} collective-permute-done((bf16[128,1280]{1,0:T(8,128)(2,1)}, bf16[128,1280]{1,0:T(8,128)(2,1)}, u32[]{:S(2)}, u32[]{:S(2)}) %collective-permute-start.13) | collective-permute-done | bytes 327712 | tf_op jit(solution)/shard_map/ppermute | solution.py:188
  180.1 2.2 %fusion = bf16[16,8,1280]{2,1,0:T(8,128)(2,1)} fusion(bf16[128,1280]{1,0:T(8,128)(2,1)} %collective-permute-done.13, bf16[128,1280]{1,0:T(8,128)(2,1)} %collective-permute-done.12, bf16[128,1280]{1,0:T(8,128)(2,1)} %collective-permute-done.11, bf16[512,1280]{1,0:T(8,128)(2,1)} %get-tuple-element.25), kind=kLoop, calls=%fused_computation.5 | loop fusion | flops 1310720 | bytes 1638400 | tf_op jit(solution)/shard_map/all_to_all | solution.py:192
  182.3 7.4 %all-to-all-done.2 = bf16[16,12,1280]{2,1,0:T(8,128)(2,1)S(1)} async-done(((bf16[16,12,1280]{2,1,0:T(8,128)(2,1)}), bf16[16,12,1280]{2,1,0:T(8,128)(2,1)S(1)}, u32[]{:S(2)}, u32[]{:S(2)}) %all-to-all-start.2) | async-done | bytes 491552 | tf_op jit(solution)/shard_map/all_to_all | solution.py:192
  189.7 4.2 %all-to-all-start.4 = ((bf16[16,8,1280]{2,1,0:T(8,128)(2,1)}), bf16[16,8,1280]{2,1,0:T(8,128)(2,1)}, u32[]{:S(2)}, u32[]{:S(2)}) async-start(bf16[16,8,1280]{2,1,0:T(8,128)(2,1)} %fusion), calls=%async_computation.4 | async-start | bytes 655360 | tf_op jit(solution)/shard_map/all_to_all | solution.py:192
  194.8 8.1 %all-to-all-done.4 = bf16[16,8,1280]{2,1,0:T(8,128)(2,1)} async-done(((bf16[16,8,1280]{2,1,0:T(8,128)(2,1)}), bf16[16,8,1280]{2,1,0:T(8,128)(2,1)}, u32[]{:S(2)}, u32[]{:S(2)}) %all-to-all-start.4) | async-done | bytes 327712 | tf_op jit(solution)/shard_map/all_to_all | solution.py:192
  203.0 2.5 %shard_map.97 = (bf16[128,1152]{1,0:T(8,128)(2,1)}, f32[2,128]{1,0:T(2,128)}) custom-call(s32[2,128]{1,0:T(2,128)} %bitcast.39, f32[2,128]{1,0:T(2,128)} %bitcast.41, bf16[192,1280]{1,0:T(8,128)(2,1)} %all_to_all.41.refs_2_, bf16[128,1280]{1,0:T(8,128)(2,1)} %bitcast.18.refs_3_), custom_call_target="tpu_custom_call" | custom-call | flops 94371840 | bytes 2000000 | tf_op jit(solution)/shard_map/pallas_call | solution.py:290
  207.7 8.8 %shard_map.99 = (bf16[576,1152]{1,0:T(8,128)(2,1)}, bf16[576,1152]{1,0:T(8,128)(2,1)}) custom-call(bf16[1152,768]{1,0:T(8,128)(2,1)} %get-tuple-element.28.refs_0_, bf16[1152,768]{1,0:T(8,128)(2,1)} %get-tuple-element.29.refs_1_, bf16[768,1152]{1,0:T(8,128)(2,1)} %constant_dynamic-update-slice_fusion.x_ref.refs_2_, ...), custom_call_target="tpu_custom_call" | custom-call | flops 3397386240 | bytes 12000000 | tf_op jit(solution)/shard_map/pallas_call | solution.py:277
  (83 shorter events, 30.4 us)
Async XLA Ops:
  3.2 10.2 %copy-start.12 = (bf16[144,1152]{1,0:T(8,128)(2,1)S(1)}, bf16[144,1152]{1,0:T(8,128)(2,1)}, u32[]{:S(2)}) copy-start(bf16[144,1152]{1,0:T(8,128)(2,1)} %get-tuple-element.21.refs_0_) | copy-start | bytes 995332
  5.3 35.7 %all-to-all-start = ((bf16[16,20,1152]{2,1,0:T(8,128)(2,1)}), bf16[16,20,1152]{2,1,0:T(8,128)(2,1)S(1)}, u32[]{:S(2)}, u32[]{:S(2)}) async-start(bf16[16,20,1152]{2,1,0:T(8,128)(2,1)} %all_to_all.34), calls=%async_computation | async-start | bytes 1769472 | tf_op jit(solution)/shard_map/all_to_all | solution.py:192
  13.3 39.7 %collective-permute-start.6 = (bf16[576,1152]{1,0:T(8,128)(2,1)}, bf16[576,1152]{1,0:T(8,128)(2,1)}, u32[]{:S(2)}, u32[]{:S(2)}) collective-permute-start(bf16[576,1152]{1,0:T(8,128)(2,1)} %bitcast.6), channel_id=1, source_target_pairs={{0,16},{16,0},{1,17},{17,1},{2,18},{18,2},{3,19},{19,3},{4,20},{20... | collective-permute-start | bytes 3981320 | tf_op jit(solution)/shard_map/ppermute | solution.py:188
  13.4 17.8 %collective-permute-start.5 = (bf16[144,1152]{1,0:T(8,128)(2,1)S(1)}, bf16[144,1152]{1,0:T(8,128)(2,1)S(1)}, u32[]{:S(2)}, u32[]{:S(2)}) collective-permute-start(bf16[144,1152]{1,0:T(8,128)(2,1)S(1)} %copy-done.12), channel_id=1, source_target_pairs={{0,96},{32,0},{64,32},{96,64},{1,97},{33,1},{65,33},{97,65},{2,98}... | collective-permute-start | bytes 995336 | tf_op jit(solution)/shard_map/ppermute | solution.py:188
  16.5 14.8 %collective-permute-start.4 = (bf16[144,1152]{1,0:T(8,128)(2,1)S(1)}, bf16[144,1152]{1,0:T(8,128)(2,1)S(1)}, u32[]{:S(2)}, u32[]{:S(2)}) collective-permute-start(bf16[144,1152]{1,0:T(8,128)(2,1)S(1)} %copy-done.12), channel_id=1, source_target_pairs={{0,64},{32,96},{64,0},{96,32},{1,65},{33,97},{65,1},{97,33},{2,66}... | collective-permute-start | bytes 995336 | tf_op jit(solution)/shard_map/ppermute | solution.py:188
  17.1 17.8 %collective-permute-start.3 = (bf16[144,1152]{1,0:T(8,128)(2,1)S(1)}, bf16[144,1152]{1,0:T(8,128)(2,1)S(1)}, u32[]{:S(2)}, u32[]{:S(2)}) collective-permute-start(bf16[144,1152]{1,0:T(8,128)(2,1)S(1)} %copy-done.12), channel_id=1, source_target_pairs={{0,32},{32,64},{64,96},{96,0},{1,33},{33,65},{65,97},{97,1},{2,34}... | collective-permute-start | bytes 995336 | tf_op jit(solution)/shard_map/ppermute | solution.py:188
  18.1 38.4 %collective-permute-start.7 = (bf16[576,1152]{1,0:T(8,128)(2,1)}, bf16[576,1152]{1,0:T(8,128)(2,1)}, u32[]{:S(2)}, u32[]{:S(2)}) collective-permute-start(bf16[576,1152]{1,0:T(8,128)(2,1)} %bitcast.8), channel_id=1, source_target_pairs={{0,16},{16,0},{1,17},{17,1},{2,18},{18,2},{3,19},{19,3},{4,20},{20... | collective-permute-start | bytes 3981320 | tf_op jit(solution)/shard_map/ppermute | solution.py:188
  31.2 3.7 %copy-start.13 = (bf16[144,1152]{1,0:T(8,128)(2,1)}, bf16[144,1152]{1,0:T(8,128)(2,1)S(1)}, u32[]{:S(2)}) copy-start(bf16[144,1152]{1,0:T(8,128)(2,1)S(1)} %collective-permute-done.5.refs_3_) | copy-start | bytes 995332
  31.3 3.7 %copy-start.14 = (bf16[144,1152]{1,0:T(8,128)(2,1)}, bf16[144,1152]{1,0:T(8,128)(2,1)S(1)}, u32[]{:S(2)}) copy-start(bf16[144,1152]{1,0:T(8,128)(2,1)S(1)} %collective-permute-done.4.refs_2_) | copy-start | bytes 995332
  41.0 49.4 %all-to-all-start.3 = ((bf16[16,32,1152]{2,1,0:T(8,128)(2,1)}), bf16[16,32,1152]{2,1,0:T(8,128)(2,1)S(1)}, u32[]{:S(2)}, u32[]{:S(2)}) async-start(bf16[16,32,1152]{2,1,0:T(8,128)(2,1)} %bitcast.37), calls=%async_computation.3 | async-start | bytes 2359296 | tf_op jit(solution)/shard_map/all_to_all | solution.py:192
  49.2 19.7 %collective-permute-start.2 = (bf16[320,1152]{1,0:T(8,128)(2,1)}, bf16[320,1152]{1,0:T(8,128)(2,1)}, u32[]{:S(2)}, u32[]{:S(2)}) collective-permute-start(bf16[320,1152]{1,0:T(8,128)(2,1)} %all_to_all.36), channel_id=1, source_target_pairs={{0,96},{32,0},{64,32},{96,64},{1,97},{33,1},{65,33},{97,65},{2,98}... | collective-permute-start | bytes 2211848 | tf_op jit(solution)/shard_map/ppermute | solution.py:188
  50.0 21.3 %collective-permute-start.1 = (bf16[320,1152]{1,0:T(8,128)(2,1)}, bf16[320,1152]{1,0:T(8,128)(2,1)}, u32[]{:S(2)}, u32[]{:S(2)}) collective-permute-start(bf16[320,1152]{1,0:T(8,128)(2,1)} %all_to_all.36), channel_id=1, source_target_pairs={{0,64},{32,96},{64,0},{96,32},{1,65},{33,97},{65,1},{97,33},{2,66}... | collective-permute-start | bytes 2211848 | tf_op jit(solution)/shard_map/ppermute | solution.py:188
  50.4 34.7 %collective-permute-start = (bf16[320,1152]{1,0:T(8,128)(2,1)}, bf16[320,1152]{1,0:T(8,128)(2,1)}, u32[]{:S(2)}, u32[]{:S(2)}) collective-permute-start(bf16[320,1152]{1,0:T(8,128)(2,1)} %all_to_all.36), channel_id=1, source_target_pairs={{0,32},{32,64},{64,96},{96,0},{1,33},{33,65},{65,97},{97,1},{2,34}... | collective-permute-start | bytes 2211848 | tf_op jit(solution)/shard_map/ppermute | solution.py:188
  72.6 13.8 %copy-start = (bf16[16,20,1152]{2,1,0:T(8,128)(2,1)}, bf16[16,20,1152]{2,1,0:T(8,128)(2,1)S(1)}, u32[]{:S(2)}) copy-start(bf16[16,20,1152]{2,1,0:T(8,128)(2,1)S(1)} %reshape.74) | copy-start | bytes 2211844
  86.4 2.2 %copy-start.1 = (bf16[16,20,1152]{2,1,0:T(8,128)(2,1)}, bf16[16,20,1152]{2,1,0:T(8,128)(2,1)S(1)}, u32[]{:S(2)}) copy-start(bf16[16,20,1152]{2,1,0:T(8,128)(2,1)S(1)} %reshape.72) | copy-start | bytes 2211844
  86.5 1.3 copy-start.4
  90.5 7.1 %copy-start.3 = (bf16[192,1152]{1,0:T(8,128)(2,1)S(1)}, bf16[192,1152]{1,0:T(8,128)(2,1)}, u32[]{:S(2)}) copy-start(bf16[192,1152]{1,0:T(8,128)(2,1)} %reshape.77) | copy-start | bytes 1327108
  90.5 34.6 %all-to-all-start.1 = ((bf16[16,48,1152]{2,1,0:T(8,128)(2,1)}), bf16[16,48,1152]{2,1,0:T(8,128)(2,1)S(1)}, u32[]{:S(2)}, u32[]{:S(2)}) async-start(bf16[16,48,1152]{2,1,0:T(8,128)(2,1)} %bitcast.36), calls=%async_computation.1 | async-start | bytes 3538944 | tf_op jit(solution)/shard_map/all_to_all | solution.py:192
  97.5 3.2 %copy-start.8 = (bf16[128,1152]{1,0:T(8,128)(2,1)S(1)}, bf16[128,1152]{1,0:T(8,128)(2,1)}, u32[]{:S(2)}) copy-start(bf16[128,1152]{1,0:T(8,128)(2,1)} %slice_bitcast_fusion.3) | copy-start | bytes 884740
  97.6 3.2 %copy-start.9 = (bf16[128,1152]{1,0:T(8,128)(2,1)S(1)}, bf16[128,1152]{1,0:T(8,128)(2,1)}, u32[]{:S(2)}) copy-start(bf16[128,1152]{1,0:T(8,128)(2,1)} %slice_bitcast_fusion) | copy-start | bytes 884740
  140.8 4.1 %copy-start.7 = (bf16[512,1280]{1,0:T(8,128)(2,1)S(1)}, bf16[512,1280]{1,0:T(8,128)(2,1)}, u32[]{:S(2)}) copy-start(bf16[512,1280]{1,0:T(8,128)(2,1)} %get-tuple-element.25) | copy-start | bytes 3932164
  142.4 21.1 %collective-permute-start.8 = (bf16[192,1280]{1,0:T(8,128)(2,1)S(1)}, bf16[192,1280]{1,0:T(8,128)(2,1)S(1)}, u32[]{:S(2)}, u32[]{:S(2)}) collective-permute-start(bf16[192,1280]{1,0:T(8,128)(2,1)S(1)} %get-tuple-element.36), channel_id=1, source_target_pairs={{0,96},{32,0},{64,32},{96,64},{1,97},{33,1},{65,33},{97,65},{2,98}... | collective-permute-start | bytes 1474568 | tf_op jit(solution)/shard_map/ppermute | solution.py:188
  142.8 25.9 %collective-permute-start.10 = (bf16[192,1280]{1,0:T(8,128)(2,1)S(1)}, bf16[192,1280]{1,0:T(8,128)(2,1)S(1)}, u32[]{:S(2)}, u32[]{:S(2)}) collective-permute-start(bf16[192,1280]{1,0:T(8,128)(2,1)S(1)} %get-tuple-element.37), channel_id=1, source_target_pairs={{0,32},{32,64},{64,96},{96,0},{1,33},{33,65},{65,97},{97,1},{2,34}... | collective-permute-start | bytes 1474568 | tf_op jit(solution)/shard_map/ppermute | solution.py:188
  144.5 24.3 %collective-permute-start.9 = (bf16[192,1280]{1,0:T(8,128)(2,1)S(1)}, bf16[192,1280]{1,0:T(8,128)(2,1)S(1)}, u32[]{:S(2)}, u32[]{:S(2)}) collective-permute-start(bf16[192,1280]{1,0:T(8,128)(2,1)S(1)} %get-tuple-element.38), channel_id=1, source_target_pairs={{0,64},{32,96},{64,0},{96,32},{1,65},{33,97},{65,1},{97,33},{2,66}... | collective-permute-start | bytes 1474568 | tf_op jit(solution)/shard_map/ppermute | solution.py:188
  145.9 30.3 %collective-permute-start.11 = (bf16[128,1280]{1,0:T(8,128)(2,1)}, bf16[128,1280]{1,0:T(8,128)(2,1)}, u32[]{:S(2)}, u32[]{:S(2)}) collective-permute-start(bf16[128,1280]{1,0:T(8,128)(2,1)} %get-tuple-element.39), channel_id=1, source_target_pairs={{0,96},{32,0},{64,32},{96,64},{1,97},{33,1},{65,33},{97,65},{2,98}... | collective-permute-start | bytes 983048 | tf_op jit(solution)/shard_map/ppermute | solution.py:188
  148.1 32.0 %collective-permute-start.13 = (bf16[128,1280]{1,0:T(8,128)(2,1)}, bf16[128,1280]{1,0:T(8,128)(2,1)}, u32[]{:S(2)}, u32[]{:S(2)}) collective-permute-start(bf16[128,1280]{1,0:T(8,128)(2,1)} %get-tuple-element.40), channel_id=1, source_target_pairs={{0,32},{32,64},{64,96},{96,0},{1,33},{33,65},{65,97},{97,1},{2,34}... | collective-permute-start | bytes 983048 | tf_op jit(solution)/shard_map/ppermute | solution.py:188
  163.4 16.7 %collective-permute-start.12 = (bf16[128,1280]{1,0:T(8,128)(2,1)}, bf16[128,1280]{1,0:T(8,128)(2,1)}, u32[]{:S(2)}, u32[]{:S(2)}) collective-permute-start(bf16[128,1280]{1,0:T(8,128)(2,1)} %get-tuple-element.41), channel_id=1, source_target_pairs={{0,64},{32,96},{64,0},{96,32},{1,65},{33,97},{65,1},{97,33},{2,66}... | collective-permute-start | bytes 983048 | tf_op jit(solution)/shard_map/ppermute | solution.py:188
  168.7 36.8 %collective-permute-start.14 = (bf16[576,1152]{1,0:T(8,128)(2,1)}, bf16[576,1152]{1,0:T(8,128)(2,1)S(1)}, u32[]{:S(2)}, u32[]{:S(2)}) collective-permute-start(bf16[576,1152]{1,0:T(8,128)(2,1)} %get-tuple-element.32), channel_id=1, source_target_pairs={{0,16},{16,0},{1,17},{17,1},{2,18},{18,2},{3,19},{19,3},{4,20},{20... | collective-permute-start | bytes 3981320 | tf_op jit(solution)/shard_map/ppermute | solution.py:188
  169.7 35.8 %collective-permute-start.15 = (bf16[576,1152]{1,0:T(8,128)(2,1)}, bf16[576,1152]{1,0:T(8,128)(2,1)S(1)}, u32[]{:S(2)}, u32[]{:S(2)}) collective-permute-start(bf16[576,1152]{1,0:T(8,128)(2,1)} %get-tuple-element.33), channel_id=1, source_target_pairs={{0,16},{16,0},{1,17},{17,1},{2,18},{18,2},{3,19},{19,3},{4,20},{20... | collective-permute-start | bytes 3981320 | tf_op jit(solution)/shard_map/ppermute | solution.py:188
  172.6 17.1 %all-to-all-start.2 = ((bf16[16,12,1280]{2,1,0:T(8,128)(2,1)}), bf16[16,12,1280]{2,1,0:T(8,128)(2,1)S(1)}, u32[]{:S(2)}, u32[]{:S(2)}) async-start(bf16[16,12,1280]{2,1,0:T(8,128)(2,1)} %all_to_all.39), calls=%async_computation.2 | async-start | bytes 1310720 | tf_op jit(solution)/shard_map/all_to_all | solution.py:192
  189.7 13.3 %all-to-all-start.4 = ((bf16[16,8,1280]{2,1,0:T(8,128)(2,1)}), bf16[16,8,1280]{2,1,0:T(8,128)(2,1)}, u32[]{:S(2)}, u32[]{:S(2)}) async-start(bf16[16,8,1280]{2,1,0:T(8,128)(2,1)} %fusion), calls=%async_computation.4 | async-start | bytes 655360 | tf_op jit(solution)/shard_map/all_to_all | solution.py:192
  205.5 1.1 copy-start.5
  (5 other events, 4.7 us)

commit v2 on v1

v2 whole, which is shorter than its diff:
```python
import functools
import math

import jax
import jax.numpy as jnp
from jax import lax
from jax.experimental import pallas as pl
from jax.experimental.pallas import tpu as pltpu
from jax.sharding import PartitionSpec as P

BF = jnp.bfloat16
F32 = jnp.float32
CHUNKS = (12, 8)
META = 16
LANES = 128
HBM = pl.BlockSpec(memory_space=pltpu.HBM)
MIB = 1024 * 1024


def mm(a, b, dims):
    return lax.dot_general(a, b, (dims, ((), ())), preferred_element_type=F32)


def ones(mask):
    return jnp.where(mask, 1.0, 0.0).astype(BF)


def eights(count):
    return -(-count // 8) * 8


NN = ((1,), (0,))
NT = ((1,), (1,))
TN = ((0,), (0,))


def positions(names, experts):
    tokens = names.shape[1]
    expert = lax.broadcasted_iota(jnp.int32, (experts, tokens), 0).astype(F32)
    member = (names[0:1] == expert) | (names[1:2] == expert)
    first = lax.broadcasted_iota(jnp.int32, (tokens, tokens), 0)
    second = lax.broadcasted_iota(jnp.int32, (tokens, tokens), 1)
    earlier = jnp.where(first < second, 1.0, 0.0).astype(BF)
    count = mm(jnp.where(member, 1.0, 0.0).astype(BF), earlier, NN)
    return jnp.where(member, count, -1.0)


def row_owner(experts, span):
    rows = experts * span
    row = lax.broadcasted_iota(jnp.int32, (rows, experts), 0)
    expert = lax.broadcasted_iota(jnp.int32, (rows, experts), 1)
    own = (row >= expert * span) & (row < (expert + 1) * span)
    number = jnp.sum(jnp.where(own, expert, 0).astype(F32), axis=1, keepdims=True)
    slot = row[:, 0:1].astype(F32) - number * span
    return jnp.where(own, 1.0, 0.0).astype(BF), number, slot


def message_kernel(dy_ref, names_ref, gates_ref, msg_ref):
    tokens, width = dy_ref.shape
    names = names_ref[...].astype(F32)
    gates = gates_ref[...]
    high = gates.astype(BF).astype(F32)
    low = gates - high
    msg_ref[0:tokens, :] = dy_ref[...]
    line = lax.broadcasted_iota(jnp.int32, (META, tokens), 0)
    meta = jnp.zeros((META, tokens), F32)
    for at, part in enumerate((names, high, low)):
        for k in range(2):
            meta = jnp.where(line == 2 * at + k, part[k : k + 1], meta)
    msg_ref[tokens:, :] = jnp.zeros((META, width), BF)
    msg_ref[tokens:, 0:tokens] = meta.astype(BF)


def pick_kernel(experts, x_ref, names_ref, xs_ref):
    pos = positions(names_ref[...].astype(F32), experts)
    own, _, slot = row_owner(experts, xs_ref.shape[0] // experts)
    picker = mm(own, pos.astype(BF), NN) == slot
    xs_ref[...] = mm(ones(picker), x_ref[...], NN).astype(BF)


def expand_kernel(experts, base, s, *refs):
    msgs, out = refs[:-1], refs[-1]
    blocks = len(msgs)
    tokens = msgs[0].shape[0] - META
    dy = jnp.concatenate([m[0:tokens, :] for m in msgs], axis=0)
    expert = lax.broadcasted_iota(jnp.int32, (experts, tokens), 0).astype(F32)
    here, gate = [], []
    for k, m in enumerate(msgs):
        meta = m[tokens:, 0:tokens].astype(F32)
        p = positions(meta[0:2], experts)
        here.append(jnp.where((p >= base) & (p < base + s), p - base + k * s, -1.0))
        both = meta[2:4] + meta[4:6]
        gate.append(
            jnp.where(meta[0:1] == expert, both[0:1], 0.0)
            + jnp.where(meta[1:2] == expert, both[1:2], 0.0)
        )
    gate = jnp.concatenate(gate, axis=1)
    here = jnp.concatenate(here, axis=1)
    high = gate.astype(BF)
    low = (gate - high.astype(F32)).astype(BF)
    own, _, slot = row_owner(experts, blocks * s)
    picker = mm(own, here.astype(BF), NN) == slot
    row_gate = jnp.sum(
        jnp.where(picker, mm(own, high, NN) + mm(own, low, NN), 0.0), axis=1, keepdims=True
    )
    out[...] = (mm(ones(picker), dy, NN) * row_gate).astype(BF)


def regroup(experts, span, base, count):
    _, number, slot = row_owner(experts, span)
    inside = (slot >= base) & (slot < base + count)
    want = jnp.where(inside, number * count + (slot - base), -1.0)
    shape = (experts * span, experts * count)
    return ones(lax.broadcasted_iota(jnp.int32, shape, 1).astype(F32) == want)


def gather(experts, count, span, base):
    _, number, slot = row_owner(experts, count)
    want = number * span + (base + slot)
    shape = (experts * count, experts * span)
    return ones(lax.broadcasted_iota(jnp.int32, shape, 1).astype(F32) == want)


def split_kernel(experts, chunks, got_ref, out_ref):
    span = got_ref.shape[0] // experts
    base = 0
    for s in chunks:
        rows = pl.ds(base * experts, s * experts)
        out_ref[rows, :] = mm(gather(experts, s, span, base), got_ref[...], NN).astype(BF)
        base += s


def rows_kernel(experts, blocks, base, s, *refs):
    xs, rest = refs[:blocks], refs[blocks:]
    got_ref, wi_mine, wi_other, wo_mine, wo_other, hid_out, dpre_out, dy_out = rest[:8]
    dxs, rest = rest[8 : 8 + blocks], rest[8 + blocks :]
    x_ref, got, dy_ref, wi_ref, wo_ref, hid_ref, dpre_ref, dx_ref, sems = rest
    width = x_ref.shape[1]
    block = experts * s
    units = wi_mine.shape[0]
    coeff = math.sqrt(2.0 / math.pi)
    copies = []

    def start(source, target):
        copies.append(pltpu.make_async_copy(source, target, sems.at[len(copies)]))
        copies[-1].start()
        return copies[-1]

    first = [start(got_ref, got)]
    second = [
        start(x.at[pl.ds(base * experts, block)], x_ref.at[pl.ds(k * block, block)])
        for k, x in enumerate(xs)
    ]
    for weight, mine, other in ((wi_ref, wi_mine, wi_other), (wo_ref, wo_mine, wo_other)):
        second.append(start(mine, weight.at[pl.ds(0, units)]))
        second.append(start(other, weight.at[pl.ds(units, units)]))
    for c in first:
        c.wait()
    for k in range(blocks):
        take = gather(experts, s, blocks * s, k * s)
        dy_ref[pl.ds(k * block, block), :] = mm(take, got[...], NN).astype(BF)
    for c in second:
        c.wait()
    last = [start(dy_ref, dy_out)]
    line = lax.broadcasted_iota(jnp.int32, (16, LANES), 0)
    lane = lax.broadcasted_iota(jnp.int32, (16, LANES), 1)
    tile = 256
    for at in range(0, blocks * block, tile):
        pre = mm(wi_ref[...], x_ref[at : at + tile, :], NT)
        back = mm(wo_ref[...], dy_ref[at : at + tile, :], NT)
        square = pre * pre
        tanh = jnp.tanh(coeff * pre * (1.0 + 0.044715 * square))
        half = 0.5 * (1.0 + tanh)
        hidden = (pre * half).astype(BF)
        slope = half + 0.5 * coeff * pre * (1.0 - tanh * tanh) * (1.0 + 3.0 * 0.044715 * square)
        hid_ref[:, at : at + tile] = hidden
        dpre_ref[:, at : at + tile] = (back * slope).astype(BF)
        prod = hidden.astype(F32) * back
        part = jnp.sum(prod.reshape(prod.shape[0] // 16, 16, tile), axis=0).astype(BF)
        dx_ref[at : at + tile, width:] = mm(part, ones(line == lane), TN).astype(BF)
        last.append(start(hid_ref.at[:, pl.ds(at, tile)], hid_out.at[:, pl.ds(at, tile)]))
        last.append(start(dpre_ref.at[:, pl.ds(at, tile)], dpre_out.at[:, pl.ds(at, tile)]))
    dx_ref[:, 0:width] = mm(dpre_ref[...], wi_ref[...], TN).astype(BF)
    for k in range(blocks):
        last.append(start(dx_ref.at[pl.ds(k * block, block)], dxs[k]))
    for c in last:
        c.wait()


def add_kernel(experts, blocks, chunks, *refs):
    out, base, laid = refs[-1], 0, None
    span = out.shape[0] // experts
    for c, s in enumerate(chunks):
        total = None
        for r in refs[c * blocks : (c + 1) * blocks]:
            part = r[...].astype(F32)
            total = part if total is None else total + part
        part = mm(regroup(experts, span, base, s), total.astype(BF), NN)
        laid = part if laid is None else laid + part
        base += s
    out[...] = laid.astype(BF)


def weights_kernel(blocks, first, *refs):
    hid, dpre, dy, *refs = refs
    xs, refs = refs[:blocks], refs[blocks:]
    held_hid, held_dpre, held_dy, held_x, out_o, out_i, out_other, sems = refs[-8:]
    outs, earlier = refs[-11:-8], refs[:-11]
    stored = (out_o, out_i, out_other)
    units = out_o.shape[0]
    copies = []

    def start(source, target):
        copies.append(pltpu.make_async_copy(source, target, sems.at[len(copies)]))
        copies[-1].start()
        return copies[-1]

    rows = held_x.shape[0] // blocks
    waits = [
        [start(hid, held_hid), start(dy, held_dy)],
        [start(dpre, held_dpre)]
        + [
            start(x.at[pl.ds(first, rows)], held_x.at[pl.ds(k * rows, rows)])
            for k, x in enumerate(xs)
        ],
    ]
    before = [start(e, s) for e, s in zip(earlier, stored)]
    last = []
    for which, (left, right) in enumerate(((held_hid, held_dy), (held_dpre, held_x))):
        for w in waits[which]:
            w.wait()
        for half in (1, 0):
            part = mm(left[pl.ds(half * units, units), :], right[...], NN)
            spot = pl.ds(which * units if half else 0, units)
            target = 2 if half else which
            if before:
                if which == 0 and half:
                    before[2].wait()
                if not half:
                    before[which].wait()
                part = part + stored[target][spot, :].astype(F32)
            stored[target][spot, :] = part.astype(BF)
            last.append(start(stored[target].at[spot], outs[target].at[spot]))
    for c in last:
        c.wait()


def combine_kernel(experts, names_ref, gates_ref, ret_ref, dx_ref, gate_ref):
    width = dx_ref.shape[1]
    names = names_ref[...].astype(F32)
    pos = positions(names, experts)
    own, number, slot = row_owner(experts, ret_ref.shape[0] // experts)
    picker = mm(own, pos.astype(BF), NN) == slot
    dx_ref[...] = mm(ones(picker), ret_ref[:, 0:width], TN).astype(BF)
    value = jnp.sum(ret_ref[:, width:].astype(F32), axis=1, keepdims=True)
    sums = [
        jnp.sum(jnp.where(picker & (names[k : k + 1] == number), value, 0.0), axis=0, keepdims=True)
        for k in range(2)
    ]
    line = lax.broadcasted_iota(jnp.int32, gate_ref.shape, 0)
    gate_ref[...] = jnp.where(line == 0, sums[0], sums[1]) / gates_ref[...]


def call(kernel, outs, flops, moved, **more):
    return pl.pallas_call(
        kernel,
        out_shape=outs,
        compiler_params=pltpu.CompilerParams(vmem_limit_bytes=60 * MIB),
        cost_estimate=pl.CostEstimate(flops=1, bytes_accessed=1, transcendentals=0),
        **more,
    )


def shift(value, axis, by):
    size = lax.axis_size(axis)
    return lax.ppermute(value, axis, [(i, (i + by) % size) for i in range(size)])


def exchange(value):
    return lax.all_to_all(value, "expert", split_axis=0, concat_axis=0, tiled=True)


def local(hidden_in, grad_out, combine, routes, w_in, w_out):
    tokens, width = hidden_in.shape
    units = w_out.shape[1]
    experts = lax.axis_size("expert")
    planes = lax.axis_size("dp")
    cap = sum(CHUNKS)
    names, gates = routes.T, combine.T
    wi, wo = w_in[0].T, w_out[0]
    hidden_units = 2 * units
    after = lax.optimization_barrier

    def arr(*shape, kind=BF):
        return jax.ShapeDtypeStruct(shape, kind)

    def ring(value, sign):
        return [shift(v, "dp", sign * k) for k, v in enumerate(value, 1)]

    msg = call(message_kernel, arr(tokens + META, width), 1e5, 6e5)(grad_out, names, gates)
    msgs = [msg] + ring([msg] * (planes - 1), 1)
    xs = call(
        functools.partial(pick_kernel, experts),
        arr(experts * eights(cap), width),
        2 * experts * cap * tokens * width,
        1e6,
    )(hidden_in, names)
    wi_other, wo_other = shift(wi, "seq", 1), shift(wo, "seq", 1)
    msgs, wi_other, wo_other = after((msgs, wi_other, wo_other))
    sent, base = [], 0
    for s in CHUNKS:
        count = planes * experts * s
        sent.append(
            call(
                functools.partial(expand_kernel, experts, base, s),
                arr(count, width),
                2 * count * planes * tokens * width,
                3e6,
            )(*msgs)
        )
        base += s
    xa = exchange(xs)
    xa = call(
        functools.partial(split_kernel, experts, CHUNKS),
        arr(experts * cap, width),
        2 * (experts * cap) ** 2 * width,
        2e6,
    )(xa)
    x = [xa] + ring([xa] * (planes - 1), 1)
    sent[0], xa = after((sent[0], xa))
    got = exchange(sent[0])
    sent[1], got = after((sent[1], got))
    got = [got, exchange(sent[1])]

    def rows_call(c):
        block = experts * CHUNKS[c]
        count = planes * block
        hid, dpre, dy, *dx = call(
            functools.partial(rows_kernel, experts, planes, sum(CHUNKS[:c]), CHUNKS[c]),
            [arr(hidden_units, count)] * 2
            + [arr(count, width)]
            + [arr(block, width + LANES)] * planes,
            6 * count * hidden_units * width,
            15e6,
            in_specs=[HBM] * (planes + 5),
            out_specs=[HBM] * (planes + 3),
            scratch_shapes=[pltpu.VMEM((count, width), BF)] * 3
            + [pltpu.VMEM((hidden_units, width), BF)] * 2
            + [pltpu.VMEM((hidden_units, count), BF)] * 2
            + [pltpu.VMEM((count, width + LANES), BF), pltpu.SemaphoreType.DMA((32,))],
        )(*x, got[c], wi, wi_other, wo, wo_other)
        return [hid, dpre, dy, *x], dx

    def weights_call(c, done, earlier):
        count = done[2].shape[0]
        grads = [(units, width)] * 2 + [(2 * units, width)]
        return call(
            functools.partial(weights_kernel, planes, experts * sum(CHUNKS[:c])),
            [arr(*g) for g in grads],
            4 * hidden_units * width * count,
            15e6,
            in_specs=[HBM] * (len(done) + len(earlier)),
            out_specs=[HBM] * 3,
            scratch_shapes=[pltpu.VMEM((hidden_units, count), BF)] * 2
            + [pltpu.VMEM((count, width), BF)] * 2
            + [pltpu.VMEM(g, BF) for g in grads]
            + [pltpu.SemaphoreType.DMA((32,))],
        )(*done, *earlier)

    done1, dx1 = rows_call(0)
    dx1[1:] = ring(dx1[1:], -1)
    grads = weights_call(0, done1, [])
    got[1], grads = after((got[1], grads))
    done2, dx2 = rows_call(1)
    dx2[1:] = ring(dx2[1:], -1)
    grads = weights_call(1, done2, grads)
    dx1, dx2, grads = after((dx1, dx2, grads))
    back = call(
        functools.partial(add_kernel, experts, planes, CHUNKS),
        arr(experts * eights(cap), width + LANES),
        1e6,
        6e6,
    )(*dx1, *dx2)
    mine_o, mine_i, theirs = grads
    theirs = shift(theirs, "seq", 1).astype(F32)
    grad_wo = (mine_o.astype(F32) + theirs[:units]).astype(BF)
    grad_wi = (mine_i.astype(F32) + theirs[units:]).astype(BF)
    back, grad_wo, grad_wi = after((exchange(back), grad_wo, grad_wi))
    grad_x, grad_gate = call(
        functools.partial(combine_kernel, experts),
        [arr(tokens, width), arr(2, tokens, kind=F32)],
        2 * experts * cap * tokens * width,
        2e6,
    )(names, gates, back)
    return grad_x, grad_gate.T, grad_wi.T[None], grad_wo[None]


def solution(mesh):
    rows = P(("dp", "seq", "expert"), None)
    first = P("expert", None, ("dp", "seq"))
    second = P("expert", ("dp", "seq"), None)
    return jax.shard_map(
        local,
        mesh=mesh,
        in_specs=(rows, rows, rows, rows, first, second),
        out_specs=(rows, rows, first, second),
        check_vma=False,
    )
```

time: 217 us -> 172 us (0.79)
  waiting for transfers between devices: 80.8 us -> 49.3 us
  local copies, waits for them, and re-layouts: 29.7 us -> 4.58 us
  Pallas kernels: 51.4 us -> 65.8 us
  other arithmetic: 11.8 us -> 4.33 us
  starting transfers between devices: 42 us -> 46.1 us
    ppermute x16 -> x15, waiting for transfers between devices: 53.5 us -> 12.7 us  [shift(): lax.ppermute(value, axis, [(i, (i + by) % size) for i in range(size)])]
    pallas_call x7 -> x11, Pallas kernels: 51.4 us -> 65.8 us  [the longest x2 25.5 us: rows_call(): call(functools.partial(rows_kernel, experts, planes, sum(CHUNKS[:c]), CHU...]
    reshape x12 -> x0, local copies, waits for them, and re-layouts: 12.5 us -> none  [the longest x11 11 us: local(): v.reshape(experts, cap, width)[:, base:base + s].reshape(experts * s, width)]
    all_to_all x5 -> x4, waiting for transfers between devices: 27.3 us -> 36.5 us  [exchange(): lax.all_to_all(value, 'expert', split_axis=0, concat_axis=0, tiled=True)]
    concatenate x3 -> x0, other arithmetic: 8.02 us -> none  [the longest x1 3.45 us: local(): wo = jnp.concatenate([wo, shift(wo, 'seq', 1)], axis=0)]
    ppermute x16 -> x15, starting transfers between devices: 12 us -> 19.4 us  [shift(): lax.ppermute(value, axis, [(i, (i + by) % size) for i in range(size)])]
    all_to_all x5 -> x0, local copies, waits for them, and re-layouts: 5.34 us -> none  [exchange(): lax.all_to_all(value, 'expert', split_axis=0, concat_axis=0, tiled=True)]
    all_to_all x5 -> x4, starting transfers between devices: 30 us -> 26.6 us  [exchange(): lax.all_to_all(value, 'expert', split_axis=0, concat_axis=0, tiled=True)]
  transfers between devices with their start and end apart: 21 -> 19, of which waited for: 11 -> 7; matrix products, arithmetic and copies ran while one was open for 13% -> 3% of each run, Pallas kernels for 12% -> 34%
where the time goes in v2:
time: 172 us; the launch traced here: 171 us
  Pallas kernels  65.8 us (38%)
  waiting for transfers between devices  49.3 us (29%)
  starting transfers between devices  46.1 us (27%)
  local copies, waits for them, and re-layouts  4.58 us (3%)
  other arithmetic  4.33 us (3%)
    all_to_all x4, waiting for transfers between devices, exchange(): lax.all_to_all(value, 'expert', split_axis=0, concat_axis=0, tiled=True)  36.5 us
    all_to_all x4, starting transfers between devices, exchange(): lax.all_to_all(value, 'expert', split_axis=0, concat_axis=0, tiled=True)  26.6 us
    pallas_call x2, Pallas kernels, rows_call(): call(functools.partial(rows_kernel, experts, planes, sum(CHUNKS[:c]), CHU...  25.5 us
    ppermute x15, starting transfers between devices, shift(): lax.ppermute(value, axis, [(i, (i + by) % size) for i in range(size)])  19.4 us
    pallas_call x2, Pallas kernels, weights_call(): call(functools.partial(weights_kernel, planes, experts * sum(CHUNKS[:c]))...  18 us
    ppermute x15, waiting for transfers between devices, shift(): lax.ppermute(value, axis, [(i, (i + by) % size) for i in range(size)])  12.7 us
    pallas_call x2, Pallas kernels, local(): call(functools.partial(expand_kernel, experts, base, s), arr(count, width...  9.02 us
    unnamed x32, local copies, waits for them, and re-layouts  4.58 us
  transfers between devices with their start and end apart: 19, of which 7 were waited for; matrix products, arithmetic and copies ran while one was open for 3% of the time, Pallas kernels for 34%

profile of v2, /device:TPU:0, one launch (start us, length us, event | category | flops | bytes accessed | tf_op | source)
XLA Modules:
  0.0 170.9 jit_solution(13292022114387136688)
XLA Ops:
  1.2 2.5 %shard_map.93 = bf16[384,1152]{1,0:T(8,128)(2,1)} custom-call(bf16[128,1152]{1,0:T(8,128)(2,1)} %x_ref.1, s32[2,128]{1,0:T(2,128)} %bitcast.33), custom_call_target="tpu_custom_call" | custom-call | flops 1 | bytes 1 | tf_op jit(solution)/shard_map/pallas_call | solution.py:302
  3.7 8.0 %all-to-all-start = ((bf16[16,24,1152]{2,1,0:T(8,128)(2,1)}), bf16[16,24,1152]{2,1,0:T(8,128)(2,1)S(1)}, u32[]{:S(2)}, u32[]{:S(2)}) async-start(bf16[16,24,1152]{2,1,0:T(8,128)(2,1)} %bitcast.30), calls=%async_computation | async-start | bytes 1769472 | tf_op jit(solution)/shard_map/all_to_all | solution.py:280
  11.7 1.7 %shard_map.95.refs_0_ = bf16[144,1152]{1,0:T(8,128)(2,1)} custom-call(bf16[128,1152]{1,0:T(8,128)(2,1)} %dy_ref.1, s32[2,128]{1,0:T(2,128)} %bitcast.34, f32[2,128]{1,0:T(2,128)} %bitcast.36), custom_call_target="tpu_custom_call" | custom-call | flops 1 | bytes 1 | tf_op jit(solution)/shard_map/pallas_call | solution.py:300
  13.4 1.6 collective-permute-start.3
  15.0 2.9 %collective-permute-start.4 = (bf16[144,1152]{1,0:T(8,128)(2,1)}, bf16[144,1152]{1,0:T(8,128)(2,1)}, u32[]{:S(2)}, u32[]{:S(2)}) collective-permute-start(bf16[144,1152]{1,0:T(8,128)(2,1)} %shard_map.95.refs_0_), channel_id=1, source_target_pairs={{0,64},{32,96},{64,0},{96,32},{1,65},{33,97},{65,1},{97,33},{2,66}... | collective-permute-start | bytes 995336 | tf_op jit(solution)/shard_map/ppermute | solution.py:276
  17.9 1.3 collective-permute-start.5
  19.3 8.3 %all-to-all-done = bf16[16,24,1152]{2,1,0:T(8,128)(2,1)S(1)} async-done(((bf16[16,24,1152]{2,1,0:T(8,128)(2,1)}), bf16[16,24,1152]{2,1,0:T(8,128)(2,1)S(1)}, u32[]{:S(2)}, u32[]{:S(2)}) %all-to-all-start) | async-done | bytes 884768 | tf_op jit(solution)/shard_map/all_to_all | solution.py:280
  28.4 2.7 %shard_map.94.refs_0_.refs_3_ = bf16[320,1152]{1,0:T(8,128)(2,1)} custom-call(bf16[384,1152]{1,0:T(8,128)(2,1)} %bitcast.29), custom_call_target="tpu_custom_call" | custom-call | flops 1 | bytes 1 | tf_op jit(solution)/shard_map/pallas_call | solution.py:323
  31.2 1.7 collective-permute-done.4.refs_2_
  32.9 5.4 %shard_map.97 = bf16[768,1152]{1,0:T(8,128)(2,1)} custom-call(bf16[144,1152]{1,0:T(8,128)(2,1)} %shard_map.95.refs_0_, bf16[144,1152]{1,0:T(8,128)(2,1)} %collective-permute-done.3.refs_1_, bf16[144,1152]{1,0:T(8,128)(2,1)} %collective-permute-done.4.refs_2_, bf16[144,1152]{1,0:T(8,128)(2,1)} %collective-permute-done.5.refs_3_), custom_call_target="tpu_custom_call" | custom-call | flops 1 | bytes 1 | tf_op jit(solution)/shard_map/pallas_call | solution.py:314
  38.3 7.1 %all-to-all-start.1 = ((bf16[16,48,1152]{2,1,0:T(8,128)(2,1)}), bf16[16,48,1152]{2,1,0:T(8,128)(2,1)}, u32[]{:S(2)}, u32[]{:S(2)}) async-start(bf16[16,48,1152]{2,1,0:T(8,128)(2,1)} %bitcast.19), calls=%async_computation.1 | async-start | bytes 3538944 | tf_op jit(solution)/shard_map/all_to_all | solution.py:280
  46.6 2.4 %collective-permute-start.1 = (bf16[320,1152]{1,0:T(8,128)(2,1)S(1)}, bf16[320,1152]{1,0:T(8,128)(2,1)S(1)}, u32[]{:S(2)}, u32[]{:S(2)}) collective-permute-start(bf16[320,1152]{1,0:T(8,128)(2,1)S(1)} %copy-done), channel_id=1, source_target_pairs={{0,64},{32,96},{64,0},{96,32},{1,65},{33,97},{65,1},{97,33},{2,66}... | collective-permute-start | bytes 2211848 | tf_op jit(solution)/shard_map/ppermute | solution.py:276
  49.0 1.7 collective-permute-start.2
  50.7 3.6 %shard_map.96 = bf16[512,1152]{1,0:T(8,128)(2,1)} custom-call(bf16[144,1152]{1,0:T(8,128)(2,1)} %shard_map.95.refs_0_, bf16[144,1152]{1,0:T(8,128)(2,1)} %collective-permute-done.3.refs_1_, bf16[144,1152]{1,0:T(8,128)(2,1)} %collective-permute-done.4.refs_2_, bf16[144,1152]{1,0:T(8,128)(2,1)} %collective-permute-done.5.refs_3_), custom_call_target="tpu_custom_call" | custom-call | flops 1 | bytes 1 | tf_op jit(solution)/shard_map/pallas_call | solution.py:314
  54.3 15.9 %all-to-all-done.1 = bf16[16,48,1152]{2,1,0:T(8,128)(2,1)} async-done(((bf16[16,48,1152]{2,1,0:T(8,128)(2,1)}), bf16[16,48,1152]{2,1,0:T(8,128)(2,1)}, u32[]{:S(2)}, u32[]{:S(2)}) %all-to-all-start.1) | async-done | bytes 1769504 | tf_op jit(solution)/shard_map/all_to_all | solution.py:280
  70.2 4.6 %all-to-all-start.2 = ((bf16[16,32,1152]{2,1,0:T(8,128)(2,1)}), bf16[16,32,1152]{2,1,0:T(8,128)(2,1)}, u32[]{:S(2)}, u32[]{:S(2)}) async-start(bf16[16,32,1152]{2,1,0:T(8,128)(2,1)} %bitcast.26), calls=%async_computation.2 | async-start | bytes 2359296 | tf_op jit(solution)/shard_map/all_to_all | solution.py:280
  74.8 6.1 %collective-permute-done.1.refs_2_.refs_5_ = bf16[320,1152]{1,0:T(8,128)(2,1)S(1)} collective-permute-done((bf16[320,1152]{1,0:T(8,128)(2,1)S(1)}, bf16[320,1152]{1,0:T(8,128)(2,1)S(1)}, u32[]{:S(2)}, u32[]{:S(2)}) %collective-permute-start.1) | collective-permute-done | bytes 737312 | tf_op jit(solution)/shard_map/ppermute | solution.py:276
  82.6 14.3 %shard_map.98 = (bf16[1152,768]{1,0:T(8,128)(2,1)}, bf16[1152,768]{1,0:T(8,128)(2,1)}, bf16[768,1152]{1,0:T(8,128)(2,1)}, bf16[192,1280]{1,0:T(8,128)(2,1)}, bf1...) custom-call(bf16[320,1152]{1,0:T(8,128)(2,1)} %shard_map.94.refs_0_.refs_3_, ...), custom_call_target="tpu_custom_call" | custom-call | flops 1 | bytes 1 | tf_op jit(solution)/shard_map/pallas_call | solution.py:338
  97.0 1.4 collective-permute-start.8
  99.3 8.3 %shard_map.99 = (bf16[576,1152]{1,0:T(8,128)(2,1)}, bf16[576,1152]{1,0:T(8,128)(2,1)}, bf16[1152,1152]{1,0:T(8,128)(2,1)}) custom-call(bf16[1152,768]{1,0:T(8,128)(2,1)} %get-tuple-element.66.refs_0_, bf16[1152,768]{1,0:T(8,128)(2,1)} %get-tuple-element.67.refs_1_, bf16[768,1152]{1,0:T(8,128)(2,1)} %get-tuple-element.68.refs_2_, ...), custom_call_target="tpu_custom_call" | custom-call | flops 1 | bytes 1 | tf_op jit(solution)/shard_map/pallas_call | solution.py:357
  107.6 11.2 %shard_map.100 = (bf16[1152,512]{1,0:T(8,128)(2,1)}, bf16[1152,512]{1,0:T(8,128)(2,1)}, bf16[512,1152]{1,0:T(8,128)(2,1)}, bf16[128,1280]{1,0:T(8,128)(2,1)}, bf...) custom-call(bf16[320,1152]{1,0:T(8,128)(2,1)} %shard_map.94.refs_0_.refs_3_, ...), custom_call_target="tpu_custom_call" | custom-call | flops 1 | bytes 1 | tf_op jit(solution)/shard_map/pallas_call | solution.py:338
  118.8 2.9 %collective-permute-start.11 = (bf16[128,1280]{1,0:T(8,128)(2,1)}, bf16[128,1280]{1,0:T(8,128)(2,1)S(1)}, u32[]{:S(2)}, u32[]{:S(2)}) collective-permute-start(bf16[128,1280]{1,0:T(8,128)(2,1)} %get-tuple-element.74), channel_id=1, source_target_pairs={{0,96},{32,0},{64,32},{96,64},{1,97},{33,1},{65,33},{97,65},{2,98}... | collective-permute-start | bytes 983048 | tf_op jit(solution)/shard_map/ppermute | solution.py:276
  121.6 1.8 %collective-permute-start.12 = (bf16[128,1280]{1,0:T(8,128)(2,1)}, bf16[128,1280]{1,0:T(8,128)(2,1)S(1)}, u32[]{:S(2)}, u32[]{:S(2)}) collective-permute-start(bf16[128,1280]{1,0:T(8,128)(2,1)} %get-tuple-element.75), channel_id=1, source_target_pairs={{0,64},{32,96},{64,0},{96,32},{1,65},{33,97},{65,1},{97,33},{2,66}... | collective-permute-start | bytes 983048 | tf_op jit(solution)/shard_map/ppermute | solution.py:276
  124.2 9.7 %shard_map.101 = (bf16[576,1152]{1,0:T(8,128)(2,1)}, bf16[576,1152]{1,0:T(8,128)(2,1)}, bf16[1152,1152]{1,0:T(8,128)(2,1)}) custom-call(bf16[1152,512]{1,0:T(8,128)(2,1)} %get-tuple-element.77.refs_0_, bf16[1152,512]{1,0:T(8,128)(2,1)} %get-tuple-element.78.refs_1_, bf16[512,1152]{1,0:T(8,128)(2,1)} %get-tuple-element.79.refs_2_, ...), custom_call_target="tpu_custom_call" | custom-call | flops 1 | bytes 1 | tf_op jit(solution)/shard_map/pallas_call | solution.py:357
  134.0 1.3 collective-permute-done.11.refs_5_
  135.3 3.6 %collective-permute-done.13.refs_7_ = bf16[128,1280]{1,0:T(8,128)(2,1)S(1)} collective-permute-done((bf16[128,1280]{1,0:T(8,128)(2,1)}, bf16[128,1280]{1,0:T(8,128)(2,1)S(1)}, u32[]{:S(2)}, u32[]{:S(2)}) %collective-permute-start.13) | collective-permute-done | bytes 327712 | tf_op jit(solution)/shard_map/ppermute | solution.py:276
  139.6 3.7 %shard_map.102 = bf16[384,1280]{1,0:T(8,128)(2,1)} custom-call(bf16[192,1280]{1,0:T(8,128)(2,1)} %get-tuple-element.86.refs_0_, bf16[192,1280]{1,0:T(8,128)(2,1)} %copy-done.10, bf16[192,1280]{1,0:T(8,128)(2,1)} %copy-done.11, bf16[192,1280]{1,0:T(8,128)(2,1)} %copy-done.12, bf16[128,1280]{1,0:T(8,128)(2,1)} %get-tuple-element.90.refs_4_, ...), custom_call_target="tpu_custom_call" | custom-call | flops 1 | bytes 1 | tf_op jit(solution)/shard_map/pallas_call | solution.py:378
  143.4 7.0 %all-to-all-start.3 = ((bf16[16,24,1280]{2,1,0:T(8,128)(2,1)}), bf16[16,24,1280]{2,1,0:T(8,128)(2,1)S(1)}, u32[]{:S(2)}, u32[]{:S(2)}) async-start(bf16[16,24,1280]{2,1,0:T(8,128)(2,1)} %bitcast.27), calls=%async_computation.3 | async-start | bytes 1966080 | tf_op jit(solution)/shard_map/all_to_all | solution.py:280
  150.4 2.2 %convert_element_type.16 = f32[1152,1152]{1,0:T(8,128)S(1)} convert(bf16[1152,1152]{1,0:T(8,128)(2,1)} %collective-permute-done.14) | non-fusion elementwise | flops 1327104 | bytes 7962624 | tf_op jit(solution)/shard_map/convert_element_type | solution.py:385
  152.9 2.1 %fusion = (bf16[576,1152]{1,0:T(8,128)(2,1)}, bf16[576,1152]{1,0:T(8,128)(2,1)}) fusion(f32[1152,1152]{1,0:T(8,128)S(1)} %convert_element_type.16, bf16[576,1152]{1,0:T(8,128)(2,1)S(1)} %copy-done.9, bf16[576,1152]{1,0:T(8,128)(2,1)S(1)} %copy-done.8), kind=kLoop, calls=%fused_computation.1 | loop fusion | flops 3981312 | bytes 10616832 | tf_op jit(solution)/shard_map/convert_element_type | solution.py:387
  155.0 12.4 %all-to-all-done.3 = bf16[16,24,1280]{2,1,0:T(8,128)(2,1)S(1)} async-done(((bf16[16,24,1280]{2,1,0:T(8,128)(2,1)}), bf16[16,24,1280]{2,1,0:T(8,128)(2,1)S(1)}, u32[]{:S(2)}, u32[]{:S(2)}) %all-to-all-start.3) | async-done | bytes 983072 | tf_op jit(solution)/shard_map/all_to_all | solution.py:280
  168.3 2.6 %shard_map.103 = (bf16[128,1152]{1,0:T(8,128)(2,1)}, f32[2,128]{1,0:T(2,128)}) custom-call(s32[2,128]{1,0:T(2,128)} %bitcast.35, f32[2,128]{1,0:T(2,128)} %bitcast.37, bf16[384,1280]{1,0:T(8,128)(2,1)} %bitcast.28), custom_call_target="tpu_custom_call" | custom-call | flops 1 | bytes 1 | tf_op jit(solution)/shard_map/pallas_call | solution.py:389
  (51 shorter events, 8.1 us)
Async XLA Ops:
  0.6 32.2 %collective-permute-start.6 = (bf16[576,1152]{1,0:T(8,128)(2,1)}, bf16[576,1152]{1,0:T(8,128)(2,1)S(1)}, u32[]{:S(2)}, u32[]{:S(2)}) collective-permute-start(bf16[576,1152]{1,0:T(8,128)(2,1)} %bitcast.20), channel_id=1, source_target_pairs={{0,16},{16,0},{1,17},{17,1},{2,18},{18,2},{3,19},{19,3},{4,20},{20... | collective-permute-start | bytes 3981320 | tf_op jit(solution)/shard_map/ppermute | solution.py:276
  0.7 32.1 %collective-permute-start.7 = (bf16[576,1152]{1,0:T(8,128)(2,1)}, bf16[576,1152]{1,0:T(8,128)(2,1)S(1)}, u32[]{:S(2)}, u32[]{:S(2)}) collective-permute-start(bf16[576,1152]{1,0:T(8,128)(2,1)} %bitcast.23), channel_id=1, source_target_pairs={{0,16},{16,0},{1,17},{17,1},{2,18},{18,2},{3,19},{19,3},{4,20},{20... | collective-permute-start | bytes 3981320 | tf_op jit(solution)/shard_map/ppermute | solution.py:276
  3.7 23.8 %all-to-all-start = ((bf16[16,24,1152]{2,1,0:T(8,128)(2,1)}), bf16[16,24,1152]{2,1,0:T(8,128)(2,1)S(1)}, u32[]{:S(2)}, u32[]{:S(2)}) async-start(bf16[16,24,1152]{2,1,0:T(8,128)(2,1)} %bitcast.30), calls=%async_computation | async-start | bytes 1769472 | tf_op jit(solution)/shard_map/all_to_all | solution.py:280
  13.4 17.7 %collective-permute-start.3 = (bf16[144,1152]{1,0:T(8,128)(2,1)}, bf16[144,1152]{1,0:T(8,128)(2,1)}, u32[]{:S(2)}, u32[]{:S(2)}) collective-permute-start(bf16[144,1152]{1,0:T(8,128)(2,1)} %shard_map.95.refs_0_), channel_id=1, source_target_pairs={{0,32},{32,64},{64,96},{96,0},{1,33},{33,65},{65,97},{97,1},{2,34}... | collective-permute-start | bytes 995336 | tf_op jit(solution)/shard_map/ppermute | solution.py:276
  15.0 17.8 %collective-permute-start.4 = (bf16[144,1152]{1,0:T(8,128)(2,1)}, bf16[144,1152]{1,0:T(8,128)(2,1)}, u32[]{:S(2)}, u32[]{:S(2)}) collective-permute-start(bf16[144,1152]{1,0:T(8,128)(2,1)} %shard_map.95.refs_0_), channel_id=1, source_target_pairs={{0,64},{32,96},{64,0},{96,32},{1,65},{33,97},{65,1},{97,33},{2,66}... | collective-permute-start | bytes 995336 | tf_op jit(solution)/shard_map/ppermute | solution.py:276
  17.9 14.9 %collective-permute-start.5 = (bf16[144,1152]{1,0:T(8,128)(2,1)}, bf16[144,1152]{1,0:T(8,128)(2,1)}, u32[]{:S(2)}, u32[]{:S(2)}) collective-permute-start(bf16[144,1152]{1,0:T(8,128)(2,1)} %shard_map.95.refs_0_), channel_id=1, source_target_pairs={{0,96},{32,0},{64,32},{96,64},{1,97},{33,1},{65,33},{97,65},{2,98}... | collective-permute-start | bytes 995336 | tf_op jit(solution)/shard_map/ppermute | solution.py:276
  27.5 0.9 copy-start.7
  32.8 5.4 %copy-start.4 = (bf16[576,1152]{1,0:T(8,128)(2,1)}, bf16[576,1152]{1,0:T(8,128)(2,1)S(1)}, u32[]{:S(2)}) copy-start(bf16[576,1152]{1,0:T(8,128)(2,1)S(1)} %collective-permute-done.6.refs_6_) | copy-start | bytes 3981316
  32.9 5.4 %copy-start.5 = (bf16[576,1152]{1,0:T(8,128)(2,1)}, bf16[576,1152]{1,0:T(8,128)(2,1)S(1)}, u32[]{:S(2)}) copy-start(bf16[576,1152]{1,0:T(8,128)(2,1)S(1)} %collective-permute-done.7.refs_8_) | copy-start | bytes 3981316
  38.3 7.1 %copy-start = (bf16[320,1152]{1,0:T(8,128)(2,1)S(1)}, bf16[320,1152]{1,0:T(8,128)(2,1)}, u32[]{:S(2)}) copy-start(bf16[320,1152]{1,0:T(8,128)(2,1)} %shard_map.94.refs_0_.refs_3_) | copy-start | bytes 2211844
  38.3 31.9 %all-to-all-start.1 = ((bf16[16,48,1152]{2,1,0:T(8,128)(2,1)}), bf16[16,48,1152]{2,1,0:T(8,128)(2,1)}, u32[]{:S(2)}, u32[]{:S(2)}) async-start(bf16[16,48,1152]{2,1,0:T(8,128)(2,1)} %bitcast.19), calls=%async_computation.1 | async-start | bytes 3538944 | tf_op jit(solution)/shard_map/all_to_all | solution.py:280
  45.4 29.4 %collective-permute-start = (bf16[320,1152]{1,0:T(8,128)(2,1)S(1)}, bf16[320,1152]{1,0:T(8,128)(2,1)S(1)}, u32[]{:S(2)}, u32[]{:S(2)}) collective-permute-start(bf16[320,1152]{1,0:T(8,128)(2,1)S(1)} %copy-done), channel_id=1, source_target_pairs={{0,32},{32,64},{64,96},{96,0},{1,33},{33,65},{65,97},{97,1},{2,34}... | collective-permute-start | bytes 2211848 | tf_op jit(solution)/shard_map/ppermute | solution.py:276
  46.6 34.3 %collective-permute-start.1 = (bf16[320,1152]{1,0:T(8,128)(2,1)S(1)}, bf16[320,1152]{1,0:T(8,128)(2,1)S(1)}, u32[]{:S(2)}, u32[]{:S(2)}) collective-permute-start(bf16[320,1152]{1,0:T(8,128)(2,1)S(1)} %copy-done), channel_id=1, source_target_pairs={{0,64},{32,96},{64,0},{96,32},{1,65},{33,97},{65,1},{97,33},{2,66}... | collective-permute-start | bytes 2211848 | tf_op jit(solution)/shard_map/ppermute | solution.py:276
  49.0 31.9 %collective-permute-start.2 = (bf16[320,1152]{1,0:T(8,128)(2,1)S(1)}, bf16[320,1152]{1,0:T(8,128)(2,1)S(1)}, u32[]{:S(2)}, u32[]{:S(2)}) collective-permute-start(bf16[320,1152]{1,0:T(8,128)(2,1)S(1)} %copy-done), channel_id=1, source_target_pairs={{0,96},{32,0},{64,32},{96,64},{1,97},{33,1},{65,33},{97,65},{2,98}... | collective-permute-start | bytes 2211848 | tf_op jit(solution)/shard_map/ppermute | solution.py:276
  70.2 37.4 %all-to-all-start.2 = ((bf16[16,32,1152]{2,1,0:T(8,128)(2,1)}), bf16[16,32,1152]{2,1,0:T(8,128)(2,1)}, u32[]{:S(2)}, u32[]{:S(2)}) async-start(bf16[16,32,1152]{2,1,0:T(8,128)(2,1)} %bitcast.26), calls=%async_computation.2 | async-start | bytes 2359296 | tf_op jit(solution)/shard_map/all_to_all | solution.py:280
  74.8 6.1 %copy-start.1 = (bf16[320,1152]{1,0:T(8,128)(2,1)}, bf16[320,1152]{1,0:T(8,128)(2,1)S(1)}, u32[]{:S(2)}) copy-start(bf16[320,1152]{1,0:T(8,128)(2,1)S(1)} %collective-permute-done.refs_1_.refs_4_) | copy-start | bytes 2211844
  97.0 26.5 %collective-permute-start.8 = (bf16[192,1280]{1,0:T(8,128)(2,1)}, bf16[192,1280]{1,0:T(8,128)(2,1)S(1)}, u32[]{:S(2)}, u32[]{:S(2)}) collective-permute-start(bf16[192,1280]{1,0:T(8,128)(2,1)} %get-tuple-element.62), channel_id=1, source_target_pairs={{0,96},{32,0},{64,32},{96,64},{1,97},{33,1},{65,33},{97,65},{2,98}... | collective-permute-start | bytes 1474568 | tf_op jit(solution)/shard_map/ppermute | solution.py:276
  98.3 35.6 %collective-permute-start.9 = (bf16[192,1280]{1,0:T(8,128)(2,1)}, bf16[192,1280]{1,0:T(8,128)(2,1)S(1)}, u32[]{:S(2)}, u32[]{:S(2)}) collective-permute-start(bf16[192,1280]{1,0:T(8,128)(2,1)} %get-tuple-element.63), channel_id=1, source_target_pairs={{0,64},{32,96},{64,0},{96,32},{1,65},{33,97},{65,1},{97,33},{2,66}... | collective-permute-start | bytes 1474568 | tf_op jit(solution)/shard_map/ppermute | solution.py:276
  98.9 35.1 %collective-permute-start.10 = (bf16[192,1280]{1,0:T(8,128)(2,1)}, bf16[192,1280]{1,0:T(8,128)(2,1)S(1)}, u32[]{:S(2)}, u32[]{:S(2)}) collective-permute-start(bf16[192,1280]{1,0:T(8,128)(2,1)} %get-tuple-element.64), channel_id=1, source_target_pairs={{0,32},{32,64},{64,96},{96,0},{1,33},{33,65},{65,97},{97,1},{2,34}... | collective-permute-start | bytes 1474568 | tf_op jit(solution)/shard_map/ppermute | solution.py:276
  118.8 16.6 %collective-permute-start.11 = (bf16[128,1280]{1,0:T(8,128)(2,1)}, bf16[128,1280]{1,0:T(8,128)(2,1)S(1)}, u32[]{:S(2)}, u32[]{:S(2)}) collective-permute-start(bf16[128,1280]{1,0:T(8,128)(2,1)} %get-tuple-element.74), channel_id=1, source_target_pairs={{0,96},{32,0},{64,32},{96,64},{1,97},{33,1},{65,33},{97,65},{2,98}... | collective-permute-start | bytes 983048 | tf_op jit(solution)/shard_map/ppermute | solution.py:276
  121.6 13.7 %collective-permute-start.12 = (bf16[128,1280]{1,0:T(8,128)(2,1)}, bf16[128,1280]{1,0:T(8,128)(2,1)S(1)}, u32[]{:S(2)}, u32[]{:S(2)}) collective-permute-start(bf16[128,1280]{1,0:T(8,128)(2,1)} %get-tuple-element.75), channel_id=1, source_target_pairs={{0,64},{32,96},{64,0},{96,32},{1,65},{33,97},{65,1},{97,33},{2,66}... | collective-permute-start | bytes 983048 | tf_op jit(solution)/shard_map/ppermute | solution.py:276
  123.4 10.5 %copy-start.10 = (bf16[192,1280]{1,0:T(8,128)(2,1)}, bf16[192,1280]{1,0:T(8,128)(2,1)S(1)}, u32[]{:S(2)}) copy-start(bf16[192,1280]{1,0:T(8,128)(2,1)S(1)} %collective-permute-done.8.refs_1_) | copy-start | bytes 1474564
  123.4 15.4 %collective-permute-start.13 = (bf16[128,1280]{1,0:T(8,128)(2,1)}, bf16[128,1280]{1,0:T(8,128)(2,1)S(1)}, u32[]{:S(2)}, u32[]{:S(2)}) collective-permute-start(bf16[128,1280]{1,0:T(8,128)(2,1)} %get-tuple-element.76), channel_id=1, source_target_pairs={{0,32},{32,64},{64,96},{96,0},{1,33},{33,65},{65,97},{97,1},{2,34}... | collective-permute-start | bytes 983048 | tf_op jit(solution)/shard_map/ppermute | solution.py:276
  133.9 5.0 %copy-start.11 = (bf16[192,1280]{1,0:T(8,128)(2,1)}, bf16[192,1280]{1,0:T(8,128)(2,1)S(1)}, u32[]{:S(2)}) copy-start(bf16[192,1280]{1,0:T(8,128)(2,1)S(1)} %collective-permute-done.9.refs_2_) | copy-start | bytes 1474564
  134.0 4.9 %copy-start.12 = (bf16[192,1280]{1,0:T(8,128)(2,1)}, bf16[192,1280]{1,0:T(8,128)(2,1)S(1)}, u32[]{:S(2)}) copy-start(bf16[192,1280]{1,0:T(8,128)(2,1)S(1)} %collective-permute-done.10.refs_3_) | copy-start | bytes 1474564
  135.3 3.6 %copy-start.13 = (bf16[128,1280]{1,0:T(8,128)(2,1)}, bf16[128,1280]{1,0:T(8,128)(2,1)S(1)}, u32[]{:S(2)}) copy-start(bf16[128,1280]{1,0:T(8,128)(2,1)S(1)} %collective-permute-done.11.refs_5_) | copy-start | bytes 983044
  135.3 3.6 %copy-start.14 = (bf16[128,1280]{1,0:T(8,128)(2,1)}, bf16[128,1280]{1,0:T(8,128)(2,1)S(1)}, u32[]{:S(2)}) copy-start(bf16[128,1280]{1,0:T(8,128)(2,1)S(1)} %collective-permute-done.12.refs_6_) | copy-start | bytes 983044
  138.9 11.5 %collective-permute-start.14 = (bf16[1152,1152]{1,0:T(8,128)(2,1)}, bf16[1152,1152]{1,0:T(8,128)(2,1)}, u32[]{:S(2)}, u32[]{:S(2)}) collective-permute-start(bf16[1152,1152]{1,0:T(8,128)(2,1)} %get-tuple-element.95), channel_id=1, source_target_pairs={{0,16},{16,0},{1,17},{17,1},{2,18},{18,2},{3,19},{19,3},{4,20},{20... | collective-permute-start | bytes 7962632 | tf_op jit(solution)/shard_map/ppermute | solution.py:276
  143.4 24.0 %all-to-all-start.3 = ((bf16[16,24,1280]{2,1,0:T(8,128)(2,1)}), bf16[16,24,1280]{2,1,0:T(8,128)(2,1)S(1)}, u32[]{:S(2)}, u32[]{:S(2)}) async-start(bf16[16,24,1280]{2,1,0:T(8,128)(2,1)} %bitcast.27), calls=%async_computation.3 | async-start | bytes 1966080 | tf_op jit(solution)/shard_map/all_to_all | solution.py:280
  150.4 2.3 %copy-start.8 = (bf16[576,1152]{1,0:T(8,128)(2,1)S(1)}, bf16[576,1152]{1,0:T(8,128)(2,1)}, u32[]{:S(2)}) copy-start(bf16[576,1152]{1,0:T(8,128)(2,1)} %get-tuple-element.94) | copy-start | bytes 3981316
  150.4 2.5 %copy-start.9 = (bf16[576,1152]{1,0:T(8,128)(2,1)S(1)}, bf16[576,1152]{1,0:T(8,128)(2,1)}, u32[]{:S(2)}) copy-start(bf16[576,1152]{1,0:T(8,128)(2,1)} %get-tuple-element.96) | copy-start | bytes 3981316
  167.4 1.0 copy-start.6
  (3 other events, 2.5 us)

commit v3 on v2

v3 whole, which is shorter than its diff:
```python
import functools
import math

import jax
import jax.numpy as jnp
from jax import lax
from jax.experimental import pallas as pl
from jax.experimental.pallas import tpu as pltpu
from jax.sharding import PartitionSpec as P

BF = jnp.bfloat16
F32 = jnp.float32
CAP = 20
GROUPS = ((1, 3), (2, 0))
META = 16
LANES = 128
HBM = pl.BlockSpec(memory_space=pltpu.HBM)
SMALL, LARGE = 12, 60
MIB = 1024 * 1024


def mm(a, b, dims):
    return lax.dot_general(a, b, (dims, ((), ())), preferred_element_type=F32)


def ones(mask):
    return jnp.where(mask, 1.0, 0.0).astype(BF)


def eights(count):
    return -(-count // 8) * 8


NN = ((1,), (0,))
NT = ((1,), (1,))
TN = ((0,), (0,))


def positions(names, experts):
    tokens = names.shape[1]
    expert = lax.broadcasted_iota(jnp.int32, (experts, tokens), 0).astype(F32)
    member = (names[0:1] == expert) | (names[1:2] == expert)
    first = lax.broadcasted_iota(jnp.int32, (tokens, tokens), 0)
    second = lax.broadcasted_iota(jnp.int32, (tokens, tokens), 1)
    earlier = jnp.where(first < second, 1.0, 0.0).astype(BF)
    count = mm(jnp.where(member, 1.0, 0.0).astype(BF), earlier, NN)
    return jnp.where(member, count, -1.0)


def row_owner(experts, span):
    rows = experts * span
    row = lax.broadcasted_iota(jnp.int32, (rows, experts), 0)
    expert = lax.broadcasted_iota(jnp.int32, (rows, experts), 1)
    own = (row >= expert * span) & (row < (expert + 1) * span)
    number = jnp.sum(jnp.where(own, expert, 0).astype(F32), axis=1, keepdims=True)
    slot = row[:, 0:1].astype(F32) - number * span
    return jnp.where(own, 1.0, 0.0).astype(BF), number, slot


def message_kernel(dy_ref, names_ref, gates_ref, msg_ref):
    tokens, width = dy_ref.shape
    names = names_ref[...].astype(F32)
    gates = gates_ref[...]
    high = gates.astype(BF).astype(F32)
    low = gates - high
    msg_ref[0:tokens, :] = dy_ref[...]
    line = lax.broadcasted_iota(jnp.int32, (META, tokens), 0)
    meta = jnp.zeros((META, tokens), F32)
    for at, part in enumerate((names, high, low)):
        for k in range(2):
            meta = jnp.where(line == 2 * at + k, part[k : k + 1], meta)
    msg_ref[tokens:, :] = jnp.zeros((META, width), BF)
    msg_ref[tokens:, 0:tokens] = meta.astype(BF)


def token_gates(names, gates, experts):
    expert = lax.broadcasted_iota(jnp.int32, (experts, names.shape[1]), 0).astype(F32)
    gate = jnp.where(names[0:1] == expert, gates[0:1], 0.0)
    gate = gate + jnp.where(names[1:2] == expert, gates[1:2], 0.0)
    high = gate.astype(BF)
    return high, (gate - high.astype(F32)).astype(BF)


def pick_kernel(experts, x_ref, names_ref, xs_ref):
    pos = positions(names_ref[...].astype(F32), experts)
    own, _, slot = row_owner(experts, xs_ref.shape[0] // experts)
    picker = mm(own, pos.astype(BF), NN) == slot
    xs_ref[...] = mm(ones(picker), x_ref[...], NN).astype(BF)


def expand_kernel(experts, cap, *refs):
    msgs, out = refs[:-1], refs[-1]
    tokens = msgs[0].shape[0] - META
    dy = jnp.concatenate([m[0:tokens, :] for m in msgs], axis=0)
    here, high, low = [], [], []
    for k, m in enumerate(msgs):
        meta = m[tokens:, 0:tokens].astype(F32)
        p = positions(meta[0:2], experts)
        here.append(jnp.where(p >= 0.0, p + k * cap, -1.0))
        parts = token_gates(meta[0:2], meta[2:4] + meta[4:6], experts)
        high.append(parts[0])
        low.append(parts[1])
    here, high, low = (jnp.concatenate(v, axis=1) for v in (here, high, low))
    own, _, slot = row_owner(experts, out.shape[0] // experts)
    picker = mm(own, here.astype(BF), NN) == slot
    gate = jnp.where(picker, mm(own, high, NN) + mm(own, low, NN), 0.0)
    gate = jnp.sum(gate, axis=1, keepdims=True)
    out[...] = (mm(ones(picker), dy, NN) * gate).astype(BF)


def regroup(experts, span, count):
    _, number, slot = row_owner(experts, span)
    want = jnp.where(slot < count, number * count + slot, -1.0)
    shape = (experts * span, experts * count)
    return ones(lax.broadcasted_iota(jnp.int32, shape, 1).astype(F32) == want)


def gather(experts, count, span, base):
    _, number, slot = row_owner(experts, count)
    want = number * span + (base + slot)
    shape = (experts * count, experts * span)
    return ones(lax.broadcasted_iota(jnp.int32, shape, 1).astype(F32) == want)


def split_kernel(experts, got_ref, out_ref):
    take = gather(experts, out_ref.shape[0] // experts, got_ref.shape[0] // experts, 0)
    out_ref[...] = mm(take, got_ref[...], NN).astype(BF)


def fill(start, parts, target):
    at, started = 0, []
    for part in parts:
        rows = part.shape[0]
        started.append(start(part, target.at[pl.ds(at, rows)]))
        at += rows
    return started


def rows_kernel(experts, parts, blocks, *refs):
    xs, refs = refs[:parts], refs[parts:]
    got_ref, wi_mine, wi_other, wo_mine, wo_other = refs[:5]
    hid_out, dpre_out, dy_out, *dxs = refs[5 : 8 + blocks]
    x_ref, got, dy_ref, wi_ref, wo_ref, hid_ref, dpre_ref, dx_ref, sems = refs[8 + blocks :]
    width = x_ref.shape[1]
    count = x_ref.shape[0]
    block = count // blocks
    units = wi_mine.shape[0]
    coeff = math.sqrt(2.0 / math.pi)
    copies = []

    def start(source, target):
        copies.append(pltpu.make_async_copy(source, target, sems.at[len(copies)]))
        copies[-1].start()
        return copies[-1]

    first = [start(got_ref, got)]
    second = fill(start, xs, x_ref)
    for weight, mine, other in ((wi_ref, wi_mine, wi_other), (wo_ref, wo_mine, wo_other)):
        second.append(start(mine, weight.at[pl.ds(0, units)]))
        second.append(start(other, weight.at[pl.ds(units, units)]))
    for c in first:
        c.wait()
    cap = block // experts
    for j in range(blocks):
        take = gather(experts, cap, blocks * cap, j * cap)
        dy_ref[pl.ds(j * block, block), :] = mm(take, got[...], NN).astype(BF)
    for c in second:
        c.wait()
    last = [start(dy_ref, dy_out)]
    line = lax.broadcasted_iota(jnp.int32, (16, LANES), 0)
    lane = lax.broadcasted_iota(jnp.int32, (16, LANES), 1)
    at = 0
    while at < count:
        tile = min(256, count - at)
        pre = mm(wi_ref[...], x_ref[at : at + tile, :], NT)
        back = mm(wo_ref[...], dy_ref[at : at + tile, :], NT)
        square = pre * pre
        tanh = jnp.tanh(coeff * pre * (1.0 + 0.044715 * square))
        half = 0.5 * (1.0 + tanh)
        hidden = (pre * half).astype(BF)
        slope = half + 0.5 * coeff * pre * (1.0 - tanh * tanh) * (1.0 + 3.0 * 0.044715 * square)
        hid_ref[:, at : at + tile] = hidden
        dpre_ref[:, at : at + tile] = (back * slope).astype(BF)
        prod = hidden.astype(F32) * back
        part = jnp.sum(prod.reshape(prod.shape[0] // 16, 16, tile), axis=0).astype(BF)
        dx_ref[at : at + tile, width:] = mm(part, ones(line == lane), TN).astype(BF)
        last.append(start(hid_ref.at[:, pl.ds(at, tile)], hid_out.at[:, pl.ds(at, tile)]))
        last.append(start(dpre_ref.at[:, pl.ds(at, tile)], dpre_out.at[:, pl.ds(at, tile)]))
        at += tile
    dx_ref[:, 0:width] = mm(dpre_ref[...], wi_ref[...], TN).astype(BF)
    for j in range(blocks):
        last.append(start(dx_ref.at[pl.ds(j * block, block)], dxs[j]))
    for c in last:
        c.wait()


def add_kernel(experts, *refs):
    total = refs[0][...].astype(F32)
    for r in refs[1:-1]:
        total = total + r[...].astype(F32)
    out = refs[-1]
    lay = regroup(experts, out.shape[0] // experts, total.shape[0] // experts)
    out[...] = mm(lay, total.astype(BF), NN).astype(BF)


def weights_kernel(groups, parts, *refs):
    ins, xs, refs = refs[: 3 * groups], refs[3 * groups :][:parts], refs[3 * groups + parts :]
    outs, (held_hid, held_dpre, held_dy, held_x), stored, sems = refs[:3], refs[3:7], refs[7:10], refs[10]
    units = stored[0].shape[0]
    copies = []

    def start(source, target):
        copies.append(pltpu.make_async_copy(source, target, sems.at[len(copies)]))
        copies[-1].start()
        return copies[-1]

    def columns(which, target):
        at, started = 0, []
        for part in ins[which::3]:
            count = part.shape[1]
            started.append(start(part, target.at[:, pl.ds(at, count)]))
            at += count
        return started

    waits = [columns(0, held_hid) + fill(start, ins[2::3], held_dy)]
    waits.append(columns(1, held_dpre) + fill(start, xs, held_x))
    last = []
    for which, (left, right) in enumerate(((held_hid, held_dy), (held_dpre, held_x))):
        for w in waits[which]:
            w.wait()
        for half in (1, 0):
            part = mm(left[pl.ds(half * units, units), :], right[...], NN).astype(BF)
            spot = pl.ds(which * units if half else 0, units)
            target = 2 if half else which
            stored[target][spot, :] = part
            last.append(start(stored[target].at[spot], outs[target].at[spot]))
    for c in last:
        c.wait()


def combine_kernel(experts, names_ref, gates_ref, ret_ref, dx_ref, gate_ref):
    width = dx_ref.shape[1]
    names = names_ref[...].astype(F32)
    pos = positions(names, experts)
    own, number, slot = row_owner(experts, ret_ref.shape[0] // experts)
    picker = mm(own, pos.astype(BF), NN) == slot
    dx_ref[...] = mm(ones(picker), ret_ref[:, 0:width], TN).astype(BF)
    value = jnp.sum(ret_ref[:, width:].astype(F32), axis=1, keepdims=True)
    sums = [
        jnp.sum(jnp.where(picker & (names[k : k + 1] == number), value, 0.0), axis=0, keepdims=True)
        for k in range(2)
    ]
    line = lax.broadcasted_iota(jnp.int32, gate_ref.shape, 0)
    gate_ref[...] = jnp.where(line == 0, sums[0], sums[1]) / gates_ref[...]


def call(kernel, outs, vmem, **more):
    return pl.pallas_call(
        kernel,
        out_shape=outs,
        compiler_params=pltpu.CompilerParams(vmem_limit_bytes=vmem * MIB),
        cost_estimate=pl.CostEstimate(flops=1, bytes_accessed=1, transcendentals=0),
        **more,
    )


def shift(value, axis, by):
    size = lax.axis_size(axis)
    return lax.ppermute(value, axis, [(i, (i + by) % size) for i in range(size)])


def exchange(value):
    return lax.all_to_all(value, "expert", split_axis=0, concat_axis=0, tiled=True)


def local(hidden_in, grad_out, combine, routes, w_in, w_out):
    tokens, width = hidden_in.shape
    units = w_out.shape[1]
    experts = lax.axis_size("expert")
    planes = lax.axis_size("dp")
    names, gates = routes.T, combine.T
    wi, wo = w_in[0].T, w_out[0]
    hidden_units = 2 * units
    block = experts * CAP
    after = lax.optimization_barrier

    def arr(*shape, kind=BF):
        return jax.ShapeDtypeStruct(shape, kind)

    msg = call(message_kernel, arr(tokens + META, width), SMALL)(grad_out, names, gates)
    msgs = {0: msg}
    for k in (1, 3, 2):
        msgs[k] = shift(msg, "dp", k)
    xs = call(functools.partial(pick_kernel, experts), arr(experts * eights(CAP), width), SMALL)(
        hidden_in, names
    )
    wi_other, wo_other = shift(wi, "seq", 1), shift(wo, "seq", 1)
    msgs[1], wi_other, wo_other = after((msgs[1], wi_other, wo_other))
    xa, msgs[1], msgs[3] = after((exchange(xs), msgs[1], msgs[3]))
    x = call(functools.partial(split_kernel, experts), arr(block, width), SMALL)(xa)
    x, msgs[1] = after((x, msgs[1]))
    half = block // 2
    near = [shift(x, "dp", 1), shift(x, "dp", -1)]
    def expand(g):
        return call(
            functools.partial(expand_kernel, experts, CAP),
            arr(block * len(GROUPS[g]), width),
            SMALL,
        )(*(msgs[k] for k in GROUPS[g]))

    sent, msgs[2] = after((expand(0), msgs[2]))
    got = exchange(sent)
    sent, got, near = after((expand(1), got, near))
    got = [got, exchange(sent)]
    xs = {0: [x], 1: near[:1], 3: near[1:]}
    xs[2] = [shift(xs[1][0][:half], "dp", 1), shift(xs[3][0][half:], "dp", -1)]

    def rows_call(g):
        blocks = len(GROUPS[g])
        count = blocks * block
        parts = sum((xs[k] for k in GROUPS[g]), [])
        hid, dpre, dy, *dx = call(
            functools.partial(rows_kernel, experts, len(parts), blocks),
            [arr(hidden_units, count)] * 2
            + [arr(count, width)]
            + [arr(block, width + LANES)] * blocks,
            LARGE,
            in_specs=[HBM] * (len(parts) + 5),
            out_specs=[HBM] * (3 + blocks),
            scratch_shapes=[pltpu.VMEM((count, width), BF)] * 3
            + [pltpu.VMEM((hidden_units, width), BF)] * 2
            + [pltpu.VMEM((hidden_units, count), BF)] * 2
            + [pltpu.VMEM((count, width + LANES), BF), pltpu.SemaphoreType.DMA((32,))],
        )(*parts, got[g], wi, wi_other, wo, wo_other)
        return [hid, dpre, dy], parts, dict(zip(GROUPS[g], dx))

    done_a, parts_a, dx = rows_call(0)
    dx = {k: shift(v, "dp", -k) for k, v in dx.items()}
    done_b, parts_b, dx_b = rows_call(1)
    dx[0], dx[2] = dx_b[0], shift(dx_b[2], "dp", 2)
    grads = [(units, width)] * 2 + [(2 * units, width)]
    total = planes * block
    ins = done_a + done_b + parts_a + parts_b
    mine_o, mine_i, theirs = call(
        functools.partial(weights_kernel, len(GROUPS), len(parts_a + parts_b)),
        [arr(*g) for g in grads],
        LARGE,
        in_specs=[HBM] * len(ins),
        out_specs=[HBM] * 3,
        scratch_shapes=[pltpu.VMEM((hidden_units, total), BF)] * 2
        + [pltpu.VMEM((total, width), BF)] * 2
        + [pltpu.VMEM(g, BF) for g in grads]
        + [pltpu.SemaphoreType.DMA((32,))],
    )(*ins)
    dx, theirs = after((dx, theirs))
    back = call(
        functools.partial(add_kernel, experts), arr(experts * eights(CAP), width + LANES), SMALL
    )(*(dx[k] for k in range(planes)))
    theirs = shift(theirs, "seq", 1).astype(F32)
    grad_wo = (mine_o.astype(F32) + theirs[:units]).astype(BF)
    grad_wi = (mine_i.astype(F32) + theirs[units:]).astype(BF)
    back, grad_wo, grad_wi = after((exchange(back), grad_wo, grad_wi))
    grad_x, grad_gate = call(
        functools.partial(combine_kernel, experts),
        [arr(tokens, width), arr(2, tokens, kind=F32)],
        SMALL,
    )(names, gates, back)
    return grad_x, grad_gate.T, grad_wi.T[None], grad_wo[None]


def solution(mesh):
    rows = P(("dp", "seq", "expert"), None)
    first = P("expert", None, ("dp", "seq"))
    second = P("expert", ("dp", "seq"), None)
    return jax.shard_map(
        local,
        mesh=mesh,
        in_specs=(rows, rows, rows, rows, first, second),
        out_specs=(rows, rows, first, second),
        check_vma=False,
    )
```

time: 172 us -> 147 us (0.85)
  Pallas kernels: 65.8 us -> 48 us
  starting transfers between devices: 46.1 us -> 42.1 us
  waiting for transfers between devices: 49.3 us -> 46.4 us
    all_to_all x4, waiting for transfers between devices: 36.5 us -> 16.9 us  [exchange(): lax.all_to_all(value, 'expert', split_axis=0, concat_axis=0, tiled=True)]
    ppermute x15 -> x13, waiting for transfers between devices: 12.7 us -> 29.5 us  [shift(): lax.ppermute(value, axis, [(i, (i + by) % size) for i in range(size)])]
    pallas_call x10 -> x9, Pallas kernels: 63.2 us -> 46.6 us  [the longest x2 26.3 us: rows_call(): call(functools.partial(rows_kernel, experts, len(parts), blocks), [arr(hi...]
    ppermute x15 -> x13, starting transfers between devices: 19.4 us -> 16.5 us  [shift(): lax.ppermute(value, axis, [(i, (i + by) % size) for i in range(size)])]
    slice x0 -> x2, local copies, waits for them, and re-layouts: none -> 1.78 us  [local(): xs[2] = [shift(xs[1][0][:half], 'dp', 1), shift(xs[3][0][half:], 'dp', -1)]]
    unnamed x32 -> x24, local copies, waits for them, and re-layouts: 4.58 us -> 3.01 us
  transfers between devices with their start and end apart: 19 -> 17, of which waited for: 7 -> 7; matrix products, arithmetic and copies ran while one was open for 3% -> 4% of each run, Pallas kernels for 34% -> 32%
where the time goes in v3:
time: 147 us; the launch traced here: 146 us
  Pallas kernels  48 us (33%)
  waiting for transfers between devices  46.4 us (32%)
  starting transfers between devices  42.1 us (29%)
  local copies, waits for them, and re-layouts  4.79 us (3%)
  other arithmetic  4.24 us (3%)
    ppermute x13, waiting for transfers between devices, shift(): lax.ppermute(value, axis, [(i, (i + by) % size) for i in range(size)])  29.5 us
    pallas_call x2, Pallas kernels, rows_call(): call(functools.partial(rows_kernel, experts, len(parts), blocks), [arr(hi...  26.3 us
    all_to_all x4, starting transfers between devices, exchange(): lax.all_to_all(value, 'expert', split_axis=0, concat_axis=0, tiled=True)  25.6 us
    all_to_all x4, waiting for transfers between devices, exchange(): lax.all_to_all(value, 'expert', split_axis=0, concat_axis=0, tiled=True)  16.9 us
    ppermute x13, starting transfers between devices, shift(): lax.ppermute(value, axis, [(i, (i + by) % size) for i in range(size)])  16.5 us
    pallas_call x1, Pallas kernels, local(): call(functools.partial(weights_kernel, len(GROUPS), len(parts_a + parts_b...  12.1 us
    pallas_call x2, Pallas kernels, expand(): call(functools.partial(expand_kernel, experts, CAP), arr(block * len(GROU...  4.18 us
    unnamed x24, local copies, waits for them, and re-layouts  3.01 us
  transfers between devices with their start and end apart: 17, of which 7 were waited for; matrix products, arithmetic and copies ran while one was open for 4% of the time, Pallas kernels for 32%

profile of v3, /device:TPU:0, one launch (start us, length us, event | category | flops | bytes accessed | tf_op | source)
XLA Modules:
  0.0 146.3 jit_solution(8309493660138388144)
XLA Ops:
  1.2 1.0 copy-done.3
  2.2 0.7 copy-done.4
  2.9 1.6 %shard_map.93 = bf16[384,1152]{1,0:T(8,128)(2,1)} custom-call(bf16[128,1152]{1,0:T(8,128)(2,1)S(1)} %copy-done.3, s32[2,128]{1,0:T(2,128)S(1)} %bitcast.21), custom_call_target="tpu_custom_call" | custom-call | flops 1 | bytes 1 | tf_op jit(solution)/shard_map/pallas_call | solution.py:294
  4.4 8.0 %all-to-all-start = ((bf16[16,24,1152]{2,1,0:T(8,128)(2,1)}), bf16[16,24,1152]{2,1,0:T(8,128)(2,1)S(1)}, u32[]{:S(2)}, u32[]{:S(2)}) async-start(bf16[16,24,1152]{2,1,0:T(8,128)(2,1)} %bitcast.2), calls=%async_computation | async-start | bytes 1769472 | tf_op jit(solution)/shard_map/all_to_all | solution.py:273
  12.5 1.6 %collective-permute-start = (bf16[144,1152]{1,0:T(8,128)(2,1)S(1)}, bf16[144,1152]{1,0:T(8,128)(2,1)S(1)}, u32[]{:S(2)}, u32[]{:S(2)}) collective-permute-start(bf16[144,1152]{1,0:T(8,128)(2,1)S(1)} %shard_map.94.refs_1_), channel_id=1, source_target_pairs={{0,32},{32,64},{64,96},{96,0},{1,33},{33,65},{65,97},{97,1},{2,34}... | collective-permute-start | bytes 995336 | tf_op jit(solution)/shard_map/ppermute | solution.py:269
  14.1 1.7 %collective-permute-start.3 = (bf16[144,1152]{1,0:T(8,128)(2,1)S(1)}, bf16[144,1152]{1,0:T(8,128)(2,1)S(1)}, u32[]{:S(2)}, u32[]{:S(2)}) collective-permute-start(bf16[144,1152]{1,0:T(8,128)(2,1)S(1)} %shard_map.94.refs_1_), channel_id=1, source_target_pairs={{0,96},{32,0},{64,32},{96,64},{1,97},{33,1},{65,33},{97,65},{2,98}... | collective-permute-start | bytes 995336 | tf_op jit(solution)/shard_map/ppermute | solution.py:269
  15.8 2.0 %collective-permute-start.4 = (bf16[144,1152]{1,0:T(8,128)(2,1)S(1)}, bf16[144,1152]{1,0:T(8,128)(2,1)S(1)}, u32[]{:S(2)}, u32[]{:S(2)}) collective-permute-start(bf16[144,1152]{1,0:T(8,128)(2,1)S(1)} %shard_map.94.refs_1_), channel_id=1, source_target_pairs={{0,64},{32,96},{64,0},{96,32},{1,65},{33,97},{65,1},{97,33},{2,66}... | collective-permute-start | bytes 995336 | tf_op jit(solution)/shard_map/ppermute | solution.py:269
  17.8 5.6 %collective-permute-done.refs_0_ = bf16[144,1152]{1,0:T(8,128)(2,1)S(1)} collective-permute-done((bf16[144,1152]{1,0:T(8,128)(2,1)S(1)}, bf16[144,1152]{1,0:T(8,128)(2,1)S(1)}, u32[]{:S(2)}, u32[]{:S(2)}) %collective-permute-start) | collective-permute-done | bytes 331808 | tf_op jit(solution)/shard_map/ppermute | solution.py:269
  23.3 6.5 %collective-permute-done.3.refs_1_ = bf16[144,1152]{1,0:T(8,128)(2,1)S(1)} collective-permute-done((bf16[144,1152]{1,0:T(8,128)(2,1)S(1)}, bf16[144,1152]{1,0:T(8,128)(2,1)S(1)}, u32[]{:S(2)}, u32[]{:S(2)}) %collective-permute-start.3) | collective-permute-done | bytes 331808 | tf_op jit(solution)/shard_map/ppermute | solution.py:269
  29.8 0.6 shard_map.95.refs_2_.refs_10_
  30.5 2.1 %shard_map.96 = bf16[640,1152]{1,0:T(8,128)(2,1)} custom-call(bf16[144,1152]{1,0:T(8,128)(2,1)S(1)} %collective-permute-done.refs_0_, bf16[144,1152]{1,0:T(8,128)(2,1)S(1)} %collective-permute-done.3.refs_1_), custom_call_target="tpu_custom_call" | custom-call | flops 1 | bytes 1 | tf_op jit(solution)/shard_map/pallas_call | solution.py:305
  32.6 7.0 %all-to-all-start.1 = ((bf16[16,40,1152]{2,1,0:T(8,128)(2,1)}), bf16[16,40,1152]{2,1,0:T(8,128)(2,1)}, u32[]{:S(2)}, u32[]{:S(2)}) async-start(bf16[16,40,1152]{2,1,0:T(8,128)(2,1)} %bitcast.7), calls=%async_computation.1 | async-start | bytes 2949120 | tf_op jit(solution)/shard_map/all_to_all | solution.py:273
  39.8 3.6 %collective-permute-start.6 = (bf16[320,1152]{1,0:T(8,128)(2,1)S(1)}, bf16[320,1152]{1,0:T(8,128)(2,1)}, u32[]{:S(2)}, u32[]{:S(2)}) collective-permute-start(bf16[320,1152]{1,0:T(8,128)(2,1)S(1)} %shard_map.95.refs_2_.refs_10_), channel_id=1, source_target_pairs={{0,96},{32,0},{64,32},{96,64},{1,97},{33,1},{65,33},{97,65},{2,98}... | collective-permute-start | bytes 2211848 | tf_op jit(solution)/shard_map/ppermute | solution.py:269
  43.4 2.1 %shard_map.97 = bf16[640,1152]{1,0:T(8,128)(2,1)} custom-call(bf16[144,1152]{1,0:T(8,128)(2,1)S(1)} %collective-permute-done.4.refs_0_, bf16[144,1152]{1,0:T(8,128)(2,1)S(1)} %shard_map.94.refs_1_), custom_call_target="tpu_custom_call" | custom-call | flops 1 | bytes 1 | tf_op jit(solution)/shard_map/pallas_call | solution.py:305
  45.5 11.2 %collective-permute-done.5.refs_0_.refs_6_ = bf16[320,1152]{1,0:T(8,128)(2,1)S(1)} collective-permute-done((bf16[320,1152]{1,0:T(8,128)(2,1)S(1)}, bf16[320,1152]{1,0:T(8,128)(2,1)S(1)}, u32[]{:S(2)}, u32[]{:S(2)}) %collective-permute-start.5) | collective-permute-done | bytes 737312 | tf_op jit(solution)/shard_map/ppermute | solution.py:269
  56.6 3.5 %all-to-all-done.1 = bf16[16,40,1152]{2,1,0:T(8,128)(2,1)} async-done(((bf16[16,40,1152]{2,1,0:T(8,128)(2,1)}), bf16[16,40,1152]{2,1,0:T(8,128)(2,1)}, u32[]{:S(2)}, u32[]{:S(2)}) %all-to-all-start.1) | async-done | bytes 1474592 | tf_op jit(solution)/shard_map/all_to_all | solution.py:273
  60.1 3.7 %all-to-all-start.2 = ((bf16[16,40,1152]{2,1,0:T(8,128)(2,1)}), bf16[16,40,1152]{2,1,0:T(8,128)(2,1)S(1)}, u32[]{:S(2)}, u32[]{:S(2)}) async-start(bf16[16,40,1152]{2,1,0:T(8,128)(2,1)} %bitcast.9), calls=%async_computation.2 | async-start | bytes 2949120 | tf_op jit(solution)/shard_map/all_to_all | solution.py:273
  64.5 1.8 %slice.13 = bf16[160,1152]{1,0:T(8,128)(2,1)} slice(bf16[320,1152]{1,0:T(8,128)(2,1)} %collective-permute-done.6.refs_1_.refs_7_), slice={[160:320], [0:1152]} | slice | bytes 737280 | tf_op jit(solution)/shard_map/slice | solution.py:316
  66.2 2.7 %collective-permute-start.8 = (bf16[160,1152]{1,0:T(8,128)(2,1)}, bf16[160,1152]{1,0:T(8,128)(2,1)}, u32[]{:S(2)}, u32[]{:S(2)}) collective-permute-start(bf16[160,1152]{1,0:T(8,128)(2,1)} %slice.13), channel_id=1, source_target_pairs={{0,96},{32,0},{64,32},{96,64},{1,97},{33,1},{65,33},{97,65},{2,98}... | collective-permute-start | bytes 1105928 | tf_op jit(solution)/shard_map/ppermute | solution.py:269
  68.9 13.1 %shard_map.99 = (bf16[1152,640]{1,0:T(8,128)(2,1)}, bf16[1152,640]{1,0:T(8,128)(2,1)}, bf16[640,1152]{1,0:T(8,128)(2,1)}, bf16[320,1280]{1,0:T(8,128)(2,1)}, bf16[320,1280]{1,0:T(8,128)(2,1)}) custom-call(bf16[320,1152]{1,0:T(8,128)(2,1)} %copy-done.8, bf16[320,1152]{1,0:T(8,128)(2,1)} %collective-permute-done.6.refs_1_.refs_7_, ...), custom_call_target="tpu_custom_call" | custom-call | flops 1 | bytes 1 | tf_op jit(solution)/shard_map/pallas_call | solution.py:322
  82.1 1.5 %collective-permute-start.9 = (bf16[320,1280]{1,0:T(8,128)(2,1)}, bf16[320,1280]{1,0:T(8,128)(2,1)S(1)}, u32[]{:S(2)}, u32[]{:S(2)}) collective-permute-start(bf16[320,1280]{1,0:T(8,128)(2,1)} %get-tuple-element.56), channel_id=1, source_target_pairs={{0,96},{32,0},{64,32},{96,64},{1,97},{33,1},{65,33},{97,65},{2,98}... | collective-permute-start | bytes 2457608 | tf_op jit(solution)/shard_map/ppermute | solution.py:269
  84.9 0.6 copy-done.7
  85.5 13.2 %shard_map.98 = (bf16[1152,640]{1,0:T(8,128)(2,1)}, bf16[1152,640]{1,0:T(8,128)(2,1)}, bf16[640,1152]{1,0:T(8,128)(2,1)}, bf16[320,1280]{1,0:T(8,128)(2,1)}, bf16[320,1280]{1,0:T(8,128)(2,1)}) custom-call(bf16[160,1152]{1,0:T(8,128)(2,1)} %copy-done.9, bf16[160,1152]{1,0:T(8,128)(2,1)} %collective-permute-done.8.refs_1_.refs_9_, bf16[320,1152]{1,0:T(8,128)(2,1)} %copy-done, ...), custom_call_target="tpu_custom_call" | custom-call | flops 1 | bytes 1 | tf_op jit(solution)/shard_map/pallas_call | solution.py:322
  98.7 1.4 collective-permute-start.10
  100.1 12.1 %shard_map.100 = (bf16[576,1152]{1,0:T(8,128)(2,1)}, bf16[576,1152]{1,0:T(8,128)(2,1)}, bf16[1152,1152]{1,0:T(8,128)(2,1)}) custom-call(bf16[1152,640]{1,0:T(8,128)(2,1)} %get-tuple-element.59.refs_0_, bf16[1152,640]{1,0:T(8,128)(2,1)} %get-tuple-element.60.refs_1_, bf16[640,1152]{1,0:T(8,128)(2,1)} %get-tuple-element.61.refs_2_, ...), custom_call_target="tpu_custom_call" | custom-call | flops 1 | bytes 1 | tf_op jit(solution)/shard_map/pallas_call | solution.py:344
  112.2 6.3 %collective-permute-done.11.refs_3_ = bf16[320,1280]{1,0:T(8,128)(2,1)S(1)} collective-permute-done((bf16[320,1280]{1,0:T(8,128)(2,1)}, bf16[320,1280]{1,0:T(8,128)(2,1)S(1)}, u32[]{:S(2)}, u32[]{:S(2)}) %collective-permute-start.11) | collective-permute-done | bytes 819232 | tf_op jit(solution)/shard_map/ppermute | solution.py:269
  118.5 1.8 %shard_map.101 = bf16[384,1280]{1,0:T(8,128)(2,1)} custom-call(bf16[320,1280]{1,0:T(8,128)(2,1)S(1)} %copy-done.1, bf16[320,1280]{1,0:T(8,128)(2,1)S(1)} %collective-permute-done.9.refs_1_, bf16[320,1280]{1,0:T(8,128)(2,1)S(1)} %collective-permute-done.10.refs_2_, bf16[320,1280]{1,0:T(8,128)(2,1)S(1)} %collective-permute-done.11.refs_3_), custom_call_target="tpu_custom_call" | custom-call | flops 1 | bytes 1 | tf_op jit(solution)/shard_map/pallas_call | solution.py:356
  120.3 6.9 %all-to-all-start.3 = ((bf16[16,24,1280]{2,1,0:T(8,128)(2,1)}), bf16[16,24,1280]{2,1,0:T(8,128)(2,1)S(1)}, u32[]{:S(2)}, u32[]{:S(2)}) async-start(bf16[16,24,1280]{2,1,0:T(8,128)(2,1)} %bitcast.12), calls=%async_computation.3 | async-start | bytes 1966080 | tf_op jit(solution)/shard_map/all_to_all | solution.py:273
  127.3 2.2 %convert_element_type.16 = f32[1152,1152]{1,0:T(8,128)S(1)} convert(bf16[1152,1152]{1,0:T(8,128)(2,1)} %collective-permute-done.12) | non-fusion elementwise | flops 1327104 | bytes 7962624 | tf_op jit(solution)/shard_map/convert_element_type | solution.py:359
  129.8 2.0 %fusion = (bf16[576,1152]{1,0:T(8,128)(2,1)}, bf16[576,1152]{1,0:T(8,128)(2,1)}) fusion(f32[1152,1152]{1,0:T(8,128)S(1)} %convert_element_type.16, bf16[576,1152]{1,0:T(8,128)(2,1)S(1)} %copy-done.11, bf16[576,1152]{1,0:T(8,128)(2,1)S(1)} %copy-done.10), kind=kLoop, calls=%fused_computation.1 | loop fusion | flops 3981312 | bytes 10616832 | tf_op jit(solution)/shard_map/convert_element_type | solution.py:361
  131.8 13.1 %all-to-all-done.3 = bf16[16,24,1280]{2,1,0:T(8,128)(2,1)S(1)} async-done(((bf16[16,24,1280]{2,1,0:T(8,128)(2,1)}), bf16[16,24,1280]{2,1,0:T(8,128)(2,1)S(1)}, u32[]{:S(2)}, u32[]{:S(2)}) %all-to-all-start.3) | async-done | bytes 983072 | tf_op jit(solution)/shard_map/all_to_all | solution.py:273
  145.0 1.4 shard_map.102
  (40 shorter events, 3.1 us)
Async XLA Ops:
  0.6 22.7 %collective-permute-start.1 = (bf16[576,1152]{1,0:T(8,128)(2,1)}, bf16[576,1152]{1,0:T(8,128)(2,1)}, u32[]{:S(2)}, u32[]{:S(2)}) collective-permute-start(bf16[576,1152]{1,0:T(8,128)(2,1)} %bitcast.27), channel_id=1, source_target_pairs={{0,16},{16,0},{1,17},{17,1},{2,18},{18,2},{3,19},{19,3},{4,20},{20... | collective-permute-start | bytes 3981320 | tf_op jit(solution)/shard_map/ppermute | solution.py:269
  0.7 22.6 %collective-permute-start.2 = (bf16[576,1152]{1,0:T(8,128)(2,1)}, bf16[576,1152]{1,0:T(8,128)(2,1)}, u32[]{:S(2)}, u32[]{:S(2)}) collective-permute-start(bf16[576,1152]{1,0:T(8,128)(2,1)} %bitcast.30), channel_id=1, source_target_pairs={{0,16},{16,0},{1,17},{17,1},{2,18},{18,2},{3,19},{19,3},{4,20},{20... | collective-permute-start | bytes 3981320 | tf_op jit(solution)/shard_map/ppermute | solution.py:269
  1.2 1.0 copy-start.3
  2.2 0.7 copy-start.4
  2.9 9.5 %copy-start.2 = (bf16[128,1152]{1,0:T(8,128)(2,1)S(1)}, bf16[128,1152]{1,0:T(8,128)(2,1)}, u32[]{:S(2)}) copy-start(bf16[128,1152]{1,0:T(8,128)(2,1)} %dy_ref.1) | copy-start | bytes 884740
  2.9 9.5 %copy-start.5 = (s32[128,2]{0,1:T(2,128)S(1)}, s32[128,2]{0,1:T(2,128)}, u32[]{:S(2)}) copy-start(s32[128,2]{0,1:T(2,128)} %param.9) | copy-start | bytes 3076
  2.9 9.5 %copy-start.6 = (f32[128,2]{0,1:T(2,128)S(1)}, f32[128,2]{0,1:T(2,128)}, u32[]{:S(2)}) copy-start(f32[128,2]{0,1:T(2,128)} %param.8) | copy-start | bytes 3076
  4.4 25.4 %all-to-all-start = ((bf16[16,24,1152]{2,1,0:T(8,128)(2,1)}), bf16[16,24,1152]{2,1,0:T(8,128)(2,1)S(1)}, u32[]{:S(2)}, u32[]{:S(2)}) async-start(bf16[16,24,1152]{2,1,0:T(8,128)(2,1)} %bitcast.2), calls=%async_computation | async-start | bytes 1769472 | tf_op jit(solution)/shard_map/all_to_all | solution.py:273
  12.5 10.9 %collective-permute-start = (bf16[144,1152]{1,0:T(8,128)(2,1)S(1)}, bf16[144,1152]{1,0:T(8,128)(2,1)S(1)}, u32[]{:S(2)}, u32[]{:S(2)}) collective-permute-start(bf16[144,1152]{1,0:T(8,128)(2,1)S(1)} %shard_map.94.refs_1_), channel_id=1, source_target_pairs={{0,32},{32,64},{64,96},{96,0},{1,33},{33,65},{65,97},{97,1},{2,34}... | collective-permute-start | bytes 995336 | tf_op jit(solution)/shard_map/ppermute | solution.py:269
  14.1 15.7 %collective-permute-start.3 = (bf16[144,1152]{1,0:T(8,128)(2,1)S(1)}, bf16[144,1152]{1,0:T(8,128)(2,1)S(1)}, u32[]{:S(2)}, u32[]{:S(2)}) collective-permute-start(bf16[144,1152]{1,0:T(8,128)(2,1)S(1)} %shard_map.94.refs_1_), channel_id=1, source_target_pairs={{0,96},{32,0},{64,32},{96,64},{1,97},{33,1},{65,33},{97,65},{2,98}... | collective-permute-start | bytes 995336 | tf_op jit(solution)/shard_map/ppermute | solution.py:269
  15.8 16.8 %collective-permute-start.4 = (bf16[144,1152]{1,0:T(8,128)(2,1)S(1)}, bf16[144,1152]{1,0:T(8,128)(2,1)S(1)}, u32[]{:S(2)}, u32[]{:S(2)}) collective-permute-start(bf16[144,1152]{1,0:T(8,128)(2,1)S(1)} %shard_map.94.refs_1_), channel_id=1, source_target_pairs={{0,64},{32,96},{64,0},{96,32},{1,65},{33,97},{65,1},{97,33},{2,66}... | collective-permute-start | bytes 995336 | tf_op jit(solution)/shard_map/ppermute | solution.py:269
  30.4 9.4 %copy-start = (bf16[320,1152]{1,0:T(8,128)(2,1)}, bf16[320,1152]{1,0:T(8,128)(2,1)S(1)}, u32[]{:S(2)}) copy-start(bf16[320,1152]{1,0:T(8,128)(2,1)S(1)} %shard_map.95.refs_2_.refs_10_) | copy-start | bytes 2211844
  32.6 27.5 %all-to-all-start.1 = ((bf16[16,40,1152]{2,1,0:T(8,128)(2,1)}), bf16[16,40,1152]{2,1,0:T(8,128)(2,1)}, u32[]{:S(2)}, u32[]{:S(2)}) async-start(bf16[16,40,1152]{2,1,0:T(8,128)(2,1)} %bitcast.7), calls=%async_computation.1 | async-start | bytes 2949120 | tf_op jit(solution)/shard_map/all_to_all | solution.py:273
  39.6 17.0 %collective-permute-start.5 = (bf16[320,1152]{1,0:T(8,128)(2,1)S(1)}, bf16[320,1152]{1,0:T(8,128)(2,1)S(1)}, u32[]{:S(2)}, u32[]{:S(2)}) collective-permute-start(bf16[320,1152]{1,0:T(8,128)(2,1)S(1)} %shard_map.95.refs_2_.refs_10_), channel_id=1, source_target_pairs={{0,32},{32,64},{64,96},{96,0},{1,33},{33,65},{65,97},{97,1},{2,34}... | collective-permute-start | bytes 2211848 | tf_op jit(solution)/shard_map/ppermute | solution.py:269
  39.8 16.8 %collective-permute-start.6 = (bf16[320,1152]{1,0:T(8,128)(2,1)S(1)}, bf16[320,1152]{1,0:T(8,128)(2,1)}, u32[]{:S(2)}, u32[]{:S(2)}) collective-permute-start(bf16[320,1152]{1,0:T(8,128)(2,1)S(1)} %shard_map.95.refs_2_.refs_10_), channel_id=1, source_target_pairs={{0,96},{32,0},{64,32},{96,64},{1,97},{33,1},{65,33},{97,65},{2,98}... | collective-permute-start | bytes 2211848 | tf_op jit(solution)/shard_map/ppermute | solution.py:269
  56.6 7.2 %copy-start.8 = (bf16[320,1152]{1,0:T(8,128)(2,1)}, bf16[320,1152]{1,0:T(8,128)(2,1)S(1)}, u32[]{:S(2)}) copy-start(bf16[320,1152]{1,0:T(8,128)(2,1)S(1)} %collective-permute-done.5.refs_0_.refs_6_) | copy-start | bytes 2211844
  60.1 24.3 %all-to-all-start.2 = ((bf16[16,40,1152]{2,1,0:T(8,128)(2,1)}), bf16[16,40,1152]{2,1,0:T(8,128)(2,1)S(1)}, u32[]{:S(2)}, u32[]{:S(2)}) async-start(bf16[16,40,1152]{2,1,0:T(8,128)(2,1)} %bitcast.9), calls=%async_computation.2 | async-start | bytes 2949120 | tf_op jit(solution)/shard_map/all_to_all | solution.py:273
  63.9 20.3 %collective-permute-start.7 = (bf16[160,1152]{1,0:T(8,128)(2,1)S(1)}, bf16[160,1152]{1,0:T(8,128)(2,1)S(1)}, u32[]{:S(2)}, u32[]{:S(2)}) collective-permute-start(bf16[160,1152]{1,0:T(8,128)(2,1)S(1)} %slice.12), channel_id=1, source_target_pairs={{0,32},{32,64},{64,96},{96,0},{1,33},{33,65},{65,97},{97,1},{2,34}... | collective-permute-start | bytes 1105928 | tf_op jit(solution)/shard_map/ppermute | solution.py:269
  66.2 17.9 %collective-permute-start.8 = (bf16[160,1152]{1,0:T(8,128)(2,1)}, bf16[160,1152]{1,0:T(8,128)(2,1)}, u32[]{:S(2)}, u32[]{:S(2)}) collective-permute-start(bf16[160,1152]{1,0:T(8,128)(2,1)} %slice.13), channel_id=1, source_target_pairs={{0,96},{32,0},{64,32},{96,64},{1,97},{33,1},{65,33},{97,65},{2,98}... | collective-permute-start | bytes 1105928 | tf_op jit(solution)/shard_map/ppermute | solution.py:269
  82.1 30.1 %collective-permute-start.9 = (bf16[320,1280]{1,0:T(8,128)(2,1)}, bf16[320,1280]{1,0:T(8,128)(2,1)S(1)}, u32[]{:S(2)}, u32[]{:S(2)}) collective-permute-start(bf16[320,1280]{1,0:T(8,128)(2,1)} %get-tuple-element.56), channel_id=1, source_target_pairs={{0,96},{32,0},{64,32},{96,64},{1,97},{33,1},{65,33},{97,65},{2,98}... | collective-permute-start | bytes 2457608 | tf_op jit(solution)/shard_map/ppermute | solution.py:269
  83.6 34.9 %collective-permute-start.11 = (bf16[320,1280]{1,0:T(8,128)(2,1)}, bf16[320,1280]{1,0:T(8,128)(2,1)S(1)}, u32[]{:S(2)}, u32[]{:S(2)}) collective-permute-start(bf16[320,1280]{1,0:T(8,128)(2,1)} %get-tuple-element.58), channel_id=1, source_target_pairs={{0,32},{32,64},{64,96},{96,0},{1,33},{33,65},{65,97},{97,1},{2,34}... | collective-permute-start | bytes 2457608 | tf_op jit(solution)/shard_map/ppermute | solution.py:269
  84.2 0.7 copy-start.9
  84.4 1.1 copy-start.7
  98.7 19.8 %collective-permute-start.10 = (bf16[320,1280]{1,0:T(8,128)(2,1)}, bf16[320,1280]{1,0:T(8,128)(2,1)S(1)}, u32[]{:S(2)}, u32[]{:S(2)}) collective-permute-start(bf16[320,1280]{1,0:T(8,128)(2,1)} %get-tuple-element.57), channel_id=1, source_target_pairs={{0,64},{32,96},{64,0},{96,32},{1,65},{33,97},{65,1},{97,33},{2,66}... | collective-permute-start | bytes 2457608 | tf_op jit(solution)/shard_map/ppermute | solution.py:269
  100.1 18.4 %copy-start.1 = (bf16[320,1280]{1,0:T(8,128)(2,1)S(1)}, bf16[320,1280]{1,0:T(8,128)(2,1)}, u32[]{:S(2)}) copy-start(bf16[320,1280]{1,0:T(8,128)(2,1)} %get-tuple-element.66.refs_0_) | copy-start | bytes 2457604
  118.5 8.8 %collective-permute-start.12 = (bf16[1152,1152]{1,0:T(8,128)(2,1)}, bf16[1152,1152]{1,0:T(8,128)(2,1)}, u32[]{:S(2)}, u32[]{:S(2)}) collective-permute-start(bf16[1152,1152]{1,0:T(8,128)(2,1)} %get-tuple-element.71), channel_id=1, source_target_pairs={{0,16},{16,0},{1,17},{17,1},{2,18},{18,2},{3,19},{19,3},{4,20},{20... | collective-permute-start | bytes 7962632 | tf_op jit(solution)/shard_map/ppermute | solution.py:269
  120.3 24.6 %all-to-all-start.3 = ((bf16[16,24,1280]{2,1,0:T(8,128)(2,1)}), bf16[16,24,1280]{2,1,0:T(8,128)(2,1)S(1)}, u32[]{:S(2)}, u32[]{:S(2)}) async-start(bf16[16,24,1280]{2,1,0:T(8,128)(2,1)} %bitcast.12), calls=%async_computation.3 | async-start | bytes 1966080 | tf_op jit(solution)/shard_map/all_to_all | solution.py:273
  127.3 2.3 %copy-start.10 = (bf16[576,1152]{1,0:T(8,128)(2,1)S(1)}, bf16[576,1152]{1,0:T(8,128)(2,1)}, u32[]{:S(2)}) copy-start(bf16[576,1152]{1,0:T(8,128)(2,1)} %get-tuple-element.70) | copy-start | bytes 3981316
  127.3 2.5 %copy-start.11 = (bf16[576,1152]{1,0:T(8,128)(2,1)S(1)}, bf16[576,1152]{1,0:T(8,128)(2,1)}, u32[]{:S(2)}) copy-start(bf16[576,1152]{1,0:T(8,128)(2,1)} %get-tuple-element.72) | copy-start | bytes 3981316

commit v4 on v3

--- a/solution.py
+++ b/solution.py
@@ -140,11 +140,12 @@
     xs, refs = refs[:parts], refs[parts:]
     got_ref, wi_mine, wi_other, wo_mine, wo_other = refs[:5]
     hid_out, dpre_out, dy_out, *dxs = refs[5 : 8 + blocks]
-    x_ref, got, dy_ref, wi_ref, wo_ref, hid_ref, dpre_ref, dx_ref, sems = refs[8 + blocks :]
+    x_ref, got, dy_ref, wi_ref, wo_ref, hid_ref, dpre_ref, dx_ref, gate_ref, sems = refs[8 + blocks :]
     width = x_ref.shape[1]
     count = x_ref.shape[0]
     block = count // blocks
     units = wi_mine.shape[0]
+    message = block + META
     coeff = math.sqrt(2.0 / math.pi)
     copies = []
 
@@ -153,54 +154,96 @@
         copies[-1].start()
         return copies[-1]
 
-    first = [start(got_ref, got)]
-    second = fill(start, xs, x_ref)
-    for weight, mine, other in ((wi_ref, wi_mine, wi_other), (wo_ref, wo_mine, wo_other)):
-        second.append(start(mine, weight.at[pl.ds(0, units)]))
-        second.append(start(other, weight.at[pl.ds(units, units)]))
-    for c in first:
-        c.wait()
-    cap = block // experts
+    mine, other = pl.ds(0, units), pl.ds(units, units)
+    loads = [
+        lambda: fill(start, xs, x_ref) + [start(wi_mine, wi_ref.at[mine])],
+        lambda: [start(got_ref, got), start(wo_mine, wo_ref.at[mine])],
+        lambda: [start(wi_other, wi_ref.at[other]), start(wo_other, wo_ref.at[other])],
+    ]
+    waits = [loads[0]()]
+
+    def arrived(at):
+        if at + 1 < len(loads):
+            waits.append(loads[at + 1]())
+        for c in waits[at]:
+            c.wait()
+
+    tiles = [(at, min(256, count - at)) for at in range(0, count, 256)]
+    sums = [0.0] * len(tiles)
+    last = []
+    for half in range(2):
+        spot = pl.ds(half * units, units)
+        arrived(2 if half else 0)
+        pres = [mm(wi_ref[spot, :], x_ref[at : at + size, :], NT) for at, size in tiles]
+        if half == 0:
+            arrived(1)
+            cap = block // experts
+            for j in range(blocks):
+                take = gather(experts, cap, blocks * cap, j * cap)
+                dy_ref[pl.ds(j * block, block), :] = mm(take, got[...], NN).astype(BF)
+            last.append(start(dy_ref, dy_out))
+        for i, (at, size) in enumerate(tiles):
+            pre = pres[i]
+            back = mm(wo_ref[spot, :], dy_ref[at : at + size, :], NT)
+            square = pre * pre
+            tanh = jnp.tanh(coeff * pre * (1.0 + 0.044715 * square))
+            gate = 0.5 * (1.0 + tanh)
+            hidden = (pre * gate).astype(BF)
+            slope = gate + 0.5 * coeff * pre * (1.0 - tanh * tanh) * (1.0 + 3.0 * 0.044715 * square)
+            hid_ref[spot, at : at + size] = hidden
+            dpre_ref[spot, at : at + size] = (back * slope).astype(BF)
+            prod = hidden.astype(F32) * back
+            sums[i] = sums[i] + jnp.sum(prod.reshape(units // META, META, size), axis=0)
+        last.append(start(hid_ref.at[spot], hid_out.at[spot]))
+        last.append(start(dpre_ref.at[spot], dpre_out.at[spot]))
+    for (at, size), part in zip(tiles, sums):
+        gate_ref[:, at : at + size] = part.astype(BF)
     for j in range(blocks):
-        take = gather(experts, cap, blocks * cap, j * cap)
-        dy_ref[pl.ds(j * block, block), :] = mm(take, got[...], NN).astype(BF)
-    for c in second:
-        c.wait()
-    last = [start(dy_ref, dy_out)]
-    line = lax.broadcasted_iota(jnp.int32, (16, LANES), 0)
-    lane = lax.broadcasted_iota(jnp.int32, (16, LANES), 1)
-    at = 0
-    while at < count:
-        tile = min(256, count - at)
-        pre = mm(wi_ref[...], x_ref[at : at + tile, :], NT)
-        back = mm(wo_ref[...], dy_ref[at : at + tile, :], NT)
-        square = pre * pre
-        tanh = jnp.tanh(coeff * pre * (1.0 + 0.044715 * square))
-        half = 0.5 * (1.0 + tanh)
-        hidden = (pre * half).astype(BF)
-        slope = half + 0.5 * coeff * pre * (1.0 - tanh * tanh) * (1.0 + 3.0 * 0.044715 * square)
-        hid_ref[:, at : at + tile] = hidden
-        dpre_ref[:, at : at + tile] = (back * slope).astype(BF)
-        prod = hidden.astype(F32) * back
-        part = jnp.sum(prod.reshape(prod.shape[0] // 16, 16, tile), axis=0).astype(BF)
-        dx_ref[at : at + tile, width:] = mm(part, ones(line == lane), TN).astype(BF)
-        last.append(start(hid_ref.at[:, pl.ds(at, tile)], hid_out.at[:, pl.ds(at, tile)]))
-        last.append(start(dpre_ref.at[:, pl.ds(at, tile)], dpre_out.at[:, pl.ds(at, tile)]))
-        at += tile
-    dx_ref[:, 0:width] = mm(dpre_ref[...], wi_ref[...], TN).astype(BF)
-    for j in range(blocks):
-        last.append(start(dx_ref.at[pl.ds(j * block, block)], dxs[j]))
+        at = j * message
+        dx_ref[at + block : at + message, :] = jnp.zeros((META, width), BF)
+        dx_ref[at + block : at + message, 0:block] = gate_ref[:, j * block : (j + 1) * block]
+    done = 0
+    for edge in (-(-block // LANES) * LANES, count):
+        dx = mm(dpre_ref[:, done:edge], wi_ref[...], TN).astype(BF)
+        for j in range(blocks):
+            low, high = max(done, j * block), min(edge, (j + 1) * block)
+            if low < high:
+                to = low + j * META
+                dx_ref[to : to + high - low, :] = dx[low - done : high - done]
+                if high == (j + 1) * block:
+                    last.append(start(dx_ref.at[pl.ds(j * message, message)], dxs[j]))
+        done = edge
     for c in last:
         c.wait()
 
 
-def add_kernel(experts, *refs):
+def spare(experts, span, at, across):
+    shape = (experts, experts * span) if across else (experts * span, experts)
+    row = lax.broadcasted_iota(jnp.int32, shape, 1 if across else 0)
+    expert = lax.broadcasted_iota(jnp.int32, shape, 0 if across else 1)
+    return ones(row == expert * span + at)
+
+
+def add_kernel(experts, cap, *refs):
+    out = refs[-1]
+    span = out.shape[0] // experts
+    block = experts * cap
     total = refs[0][...].astype(F32)
     for r in refs[1:-1]:
         total = total + r[...].astype(F32)
-    out = refs[-1]
-    lay = regroup(experts, out.shape[0] // experts, total.shape[0] // experts)
-    out[...] = mm(lay, total.astype(BF), NN).astype(BF)
+    sums = jnp.sum(total[block:, 0:block], axis=0, keepdims=True)
+    lane = lax.broadcasted_iota(jnp.int32, (experts, block), 1)
+    expert = lax.broadcasted_iota(jnp.int32, (experts, block), 0)
+    sums = jnp.where((lane >= expert * cap) & (lane < (expert + 1) * cap), sums, 0.0)
+    high = sums.astype(BF)
+    low = (sums - high.astype(F32)).astype(BF)
+    _, _, slot = row_owner(experts, cap)
+    column = ones(lax.broadcasted_iota(jnp.int32, (block, LANES), 1).astype(F32) == slot)
+    laid = mm(regroup(experts, span, cap), total[0:block].astype(BF), NN)
+    first = mm(spare(experts, span, cap, False), mm(high, column, NN).astype(BF), NN)
+    first = first + mm(spare(experts, span, cap + 1, False), mm(low, column, NN).astype(BF), NN)
+    out[...] = laid.astype(BF)
+    out[:, 0:LANES] = (laid[:, 0:LANES] + first).astype(BF)
 
 
 def weights_kernel(groups, parts, *refs):
@@ -238,16 +281,21 @@
         c.wait()
 
 
-def combine_kernel(experts, names_ref, gates_ref, ret_ref, dx_ref, gate_ref):
-    width = dx_ref.shape[1]
+def combine_kernel(experts, cap, names_ref, gates_ref, ret_ref, dx_ref, gate_ref):
     names = names_ref[...].astype(F32)
     pos = positions(names, experts)
-    own, number, slot = row_owner(experts, ret_ref.shape[0] // experts)
+    span = ret_ref.shape[0] // experts
+    own, _, slot = row_owner(experts, span)
     picker = mm(own, pos.astype(BF), NN) == slot
-    dx_ref[...] = mm(ones(picker), ret_ref[:, 0:width], TN).astype(BF)
-    value = jnp.sum(ret_ref[:, width:].astype(F32), axis=1, keepdims=True)
+    dx_ref[...] = mm(ones(picker), ret_ref[...], TN).astype(BF)
+    table = mm(spare(experts, span, cap, True), ret_ref[:, 0:LANES], NN)
+    table = table + mm(spare(experts, span, cap + 1, True), ret_ref[:, 0:LANES], NN)
+    value = jnp.zeros(pos.shape, F32)
+    for s in range(cap):
+        value = jnp.where(pos == float(s), table[:, s : s + 1], value)
+    expert = lax.broadcasted_iota(jnp.int32, pos.shape, 0).astype(F32)
     sums = [
-        jnp.sum(jnp.where(picker & (names[k : k + 1] == number), value, 0.0), axis=0, keepdims=True)
+        jnp.sum(jnp.where(expert == names[k : k + 1], value, 0.0), axis=0, keepdims=True)
         for k in range(2)
     ]
     line = lax.broadcasted_iota(jnp.int32, gate_ref.shape, 0)
@@ -291,7 +339,7 @@
     msgs = {0: msg}
     for k in (1, 3, 2):
         msgs[k] = shift(msg, "dp", k)
-    xs = call(functools.partial(pick_kernel, experts), arr(experts * eights(CAP), width), SMALL)(
+    xs = call(functools.partial(pick_kernel, experts), arr(experts * eights(CAP), width), LARGE)(
         hidden_in, names
     )
     wi_other, wo_other = shift(wi, "seq", 1), shift(wo, "seq", 1)
@@ -299,7 +347,6 @@
     xa, msgs[1], msgs[3] = after((exchange(xs), msgs[1], msgs[3]))
     x = call(functools.partial(split_kernel, experts), arr(block, width), SMALL)(xa)
     x, msgs[1] = after((x, msgs[1]))
-    half = block // 2
     near = [shift(x, "dp", 1), shift(x, "dp", -1)]
     def expand(g):
         return call(
@@ -312,8 +359,8 @@
     got = exchange(sent)
     sent, got, near = after((expand(1), got, near))
     got = [got, exchange(sent)]
-    xs = {0: [x], 1: near[:1], 3: near[1:]}
-    xs[2] = [shift(xs[1][0][:half], "dp", 1), shift(xs[3][0][half:], "dp", -1)]
+    far, near = after((x, near))
+    xs = {0: [x], 1: near[:1], 2: [shift(far, "dp", 2)], 3: near[1:]}
 
     def rows_call(g):
         blocks = len(GROUPS[g])
@@ -323,14 +370,15 @@
             functools.partial(rows_kernel, experts, len(parts), blocks),
             [arr(hidden_units, count)] * 2
             + [arr(count, width)]
-            + [arr(block, width + LANES)] * blocks,
+            + [arr(block + META, width)] * blocks,
             LARGE,
             in_specs=[HBM] * (len(parts) + 5),
             out_specs=[HBM] * (3 + blocks),
             scratch_shapes=[pltpu.VMEM((count, width), BF)] * 3
             + [pltpu.VMEM((hidden_units, width), BF)] * 2
             + [pltpu.VMEM((hidden_units, count), BF)] * 2
-            + [pltpu.VMEM((count, width + LANES), BF), pltpu.SemaphoreType.DMA((32,))],
+            + [pltpu.VMEM((count + META * blocks, width), BF), pltpu.VMEM((META, count), BF)]
+            + [pltpu.SemaphoreType.DMA((32,))],
         )(*parts, got[g], wi, wi_other, wo, wo_other)
         return [hid, dpre, dy], parts, dict(zip(GROUPS[g], dx))
 
@@ -354,14 +402,15 @@
     )(*ins)
     dx, theirs = after((dx, theirs))
     back = call(
-        functools.partial(add_kernel, experts), arr(experts * eights(CAP), width + LANES), SMALL
+        functools.partial(add_kernel, experts, CAP), arr(experts * eights(CAP), width), SMALL
     )(*(dx[k] for k in range(planes)))
+    theirs, back = after((theirs, back))
     theirs = shift(theirs, "seq", 1).astype(F32)
     grad_wo = (mine_o.astype(F32) + theirs[:units]).astype(BF)
     grad_wi = (mine_i.astype(F32) + theirs[units:]).astype(BF)
     back, grad_wo, grad_wi = after((exchange(back), grad_wo, grad_wi))
     grad_x, grad_gate = call(
-        functools.partial(combine_kernel, experts),
+        functools.partial(combine_kernel, experts, CAP),
         [arr(tokens, width), arr(2, tokens, kind=F32)],
         SMALL,
     )(names, gates, back)

time: 147 us -> 142 us (0.966)
  local copies, waits for them, and re-layouts: 4.79 us -> 1.38 us
  other arithmetic: 4.24 us -> 2.34 us
  waiting for transfers between devices: 46.4 us -> 48.1 us
  starting transfers between devices: 42.1 us -> 40.5 us
    ppermute x13 -> x12, starting transfers between devices: 16.5 us -> 14.2 us  [shift(): lax.ppermute(value, axis, [(i, (i + by) % size) for i in range(size)])]
    convert_element_type x1, other arithmetic: 2.24 us -> 0.34 us  [local(): theirs = shift(theirs, 'seq', 1).astype(F32)]
    slice x2 -> x0, local copies, waits for them, and re-layouts: 1.78 us -> none  [local(): xs[2] = [shift(xs[1][0][:half], 'dp', 1), shift(xs[3][0][half:], 'dp', -1)]]
    unnamed x24 -> x20, local copies, waits for them, and re-layouts: 3.01 us -> 1.38 us
    ppermute x13 -> x12, waiting for transfers between devices: 29.5 us -> 30.1 us  [shift(): lax.ppermute(value, axis, [(i, (i + by) % size) for i in range(size)])]
  transfers between devices with their start and end apart: 17 -> 16, of which waited for: 7 -> 9; matrix products, arithmetic and copies ran while one was open for 4% -> 2% of each run, Pallas kernels for 32% -> 32%
where the time goes in v4:
time: 142 us; the launch traced here: 141 us
  waiting for transfers between devices  48.1 us (34%)
  Pallas kernels  48 us (34%)
  starting transfers between devices  40.5 us (29%)
  other arithmetic  2.34 us (2%)
    ppermute x12, waiting for transfers between devices, shift(): lax.ppermute(value, axis, [(i, (i + by) % size) for i in range(size)])  30.1 us
    all_to_all x4, starting transfers between devices, exchange(): lax.all_to_all(value, 'expert', split_axis=0, concat_axis=0, tiled=True)  26.3 us
    pallas_call x2, Pallas kernels, rows_call(): call(functools.partial(rows_kernel, experts, len(parts), blocks), [arr(hi...  25.2 us
    all_to_all x4, waiting for transfers between devices, exchange(): lax.all_to_all(value, 'expert', split_axis=0, concat_axis=0, tiled=True)  18 us
    ppermute x12, starting transfers between devices, shift(): lax.ppermute(value, axis, [(i, (i + by) % size) for i in range(size)])  14.2 us
    pallas_call x1, Pallas kernels, local(): call(functools.partial(weights_kernel, len(GROUPS), len(parts_a + parts_b...  12.1 us
    pallas_call x2, Pallas kernels, expand(): call(functools.partial(expand_kernel, experts, CAP), arr(block * len(GROU...  4.19 us
  transfers between devices with their start and end apart: 16, of which 9 were waited for; matrix products, arithmetic and copies ran while one was open for 2% of the time, Pallas kernels for 32%

profile of v4, /device:TPU:0, one launch (start us, length us, event | category | flops | bytes accessed | tf_op | source)
XLA Modules:
  0.0 141.2 jit_solution(8066366545888152080)
XLA Ops:
  0.7 0.5 collective-permute-start.2
  1.2 2.6 %shard_map.93 = bf16[384,1152]{1,0:T(8,128)(2,1)} custom-call(bf16[128,1152]{1,0:T(8,128)(2,1)} %x_ref.1, s32[2,128]{1,0:T(2,128)} %bitcast.21), custom_call_target="tpu_custom_call" | custom-call | flops 1 | bytes 1 | tf_op jit(solution)/shard_map/pallas_call | solution.py:342
  3.8 8.0 %all-to-all-start = ((bf16[16,24,1152]{2,1,0:T(8,128)(2,1)}), bf16[16,24,1152]{2,1,0:T(8,128)(2,1)S(1)}, u32[]{:S(2)}, u32[]{:S(2)}) async-start(bf16[16,24,1152]{2,1,0:T(8,128)(2,1)} %bitcast.32), calls=%async_computation | async-start | bytes 1769472 | tf_op jit(solution)/shard_map/all_to_all | solution.py:321
  11.8 1.6 %collective-permute-start = (bf16[144,1152]{1,0:T(8,128)(2,1)S(1)}, bf16[144,1152]{1,0:T(8,128)(2,1)S(1)}, u32[]{:S(2)}, u32[]{:S(2)}) collective-permute-start(bf16[144,1152]{1,0:T(8,128)(2,1)S(1)} %shard_map.94.refs_1_), channel_id=1, source_target_pairs={{0,32},{32,64},{64,96},{96,0},{1,33},{33,65},{65,97},{97,1},{2,34}... | collective-permute-start | bytes 995336 | tf_op jit(solution)/shard_map/ppermute | solution.py:317
  13.5 1.7 %collective-permute-start.3 = (bf16[144,1152]{1,0:T(8,128)(2,1)S(1)}, bf16[144,1152]{1,0:T(8,128)(2,1)S(1)}, u32[]{:S(2)}, u32[]{:S(2)}) collective-permute-start(bf16[144,1152]{1,0:T(8,128)(2,1)S(1)} %shard_map.94.refs_1_), channel_id=1, source_target_pairs={{0,96},{32,0},{64,32},{96,64},{1,97},{33,1},{65,33},{97,65},{2,98}... | collective-permute-start | bytes 995336 | tf_op jit(solution)/shard_map/ppermute | solution.py:317
  15.1 2.0 %collective-permute-start.4 = (bf16[144,1152]{1,0:T(8,128)(2,1)S(1)}, bf16[144,1152]{1,0:T(8,128)(2,1)S(1)}, u32[]{:S(2)}, u32[]{:S(2)}) collective-permute-start(bf16[144,1152]{1,0:T(8,128)(2,1)S(1)} %shard_map.94.refs_1_), channel_id=1, source_target_pairs={{0,64},{32,96},{64,0},{96,32},{1,65},{33,97},{65,1},{97,33},{2,66}... | collective-permute-start | bytes 995336 | tf_op jit(solution)/shard_map/ppermute | solution.py:317
  17.1 5.6 %collective-permute-done.refs_0_ = bf16[144,1152]{1,0:T(8,128)(2,1)S(1)} collective-permute-done((bf16[144,1152]{1,0:T(8,128)(2,1)S(1)}, bf16[144,1152]{1,0:T(8,128)(2,1)S(1)}, u32[]{:S(2)}, u32[]{:S(2)}) %collective-permute-start) | collective-permute-done | bytes 331808 | tf_op jit(solution)/shard_map/ppermute | solution.py:317
  22.7 6.5 %collective-permute-done.3.refs_1_ = bf16[144,1152]{1,0:T(8,128)(2,1)S(1)} collective-permute-done((bf16[144,1152]{1,0:T(8,128)(2,1)S(1)}, bf16[144,1152]{1,0:T(8,128)(2,1)S(1)}, u32[]{:S(2)}, u32[]{:S(2)}) %collective-permute-start.3) | collective-permute-done | bytes 331808 | tf_op jit(solution)/shard_map/ppermute | solution.py:317
  29.2 0.6 shard_map.95.refs_1_.refs_9_
  29.8 2.1 %shard_map.96 = bf16[640,1152]{1,0:T(8,128)(2,1)} custom-call(bf16[144,1152]{1,0:T(8,128)(2,1)S(1)} %collective-permute-done.refs_0_, bf16[144,1152]{1,0:T(8,128)(2,1)S(1)} %collective-permute-done.3.refs_1_), custom_call_target="tpu_custom_call" | custom-call | flops 1 | bytes 1 | tf_op jit(solution)/shard_map/pallas_call | solution.py:352
  31.9 7.0 %all-to-all-start.1 = ((bf16[16,40,1152]{2,1,0:T(8,128)(2,1)}), bf16[16,40,1152]{2,1,0:T(8,128)(2,1)}, u32[]{:S(2)}, u32[]{:S(2)}) async-start(bf16[16,40,1152]{2,1,0:T(8,128)(2,1)} %bitcast.7), calls=%async_computation.1 | async-start | bytes 2949120 | tf_op jit(solution)/shard_map/all_to_all | solution.py:321
  39.2 3.5 %collective-permute-start.6 = (bf16[320,1152]{1,0:T(8,128)(2,1)S(1)}, bf16[320,1152]{1,0:T(8,128)(2,1)S(1)}, u32[]{:S(2)}, u32[]{:S(2)}) collective-permute-start(bf16[320,1152]{1,0:T(8,128)(2,1)S(1)} %shard_map.95.refs_1_.refs_9_), channel_id=1, source_target_pairs={{0,96},{32,0},{64,32},{96,64},{1,97},{33,1},{65,33},{97,65},{2,98}... | collective-permute-start | bytes 2211848 | tf_op jit(solution)/shard_map/ppermute | solution.py:317
  42.7 2.1 %shard_map.97 = bf16[640,1152]{1,0:T(8,128)(2,1)} custom-call(bf16[144,1152]{1,0:T(8,128)(2,1)S(1)} %collective-permute-done.4.refs_0_, bf16[144,1152]{1,0:T(8,128)(2,1)S(1)} %shard_map.94.refs_1_), custom_call_target="tpu_custom_call" | custom-call | flops 1 | bytes 1 | tf_op jit(solution)/shard_map/pallas_call | solution.py:352
  44.8 11.2 %collective-permute-done.5.refs_0_.refs_6_ = bf16[320,1152]{1,0:T(8,128)(2,1)S(1)} collective-permute-done((bf16[320,1152]{1,0:T(8,128)(2,1)S(1)}, bf16[320,1152]{1,0:T(8,128)(2,1)S(1)}, u32[]{:S(2)}, u32[]{:S(2)}) %collective-permute-start.5) | collective-permute-done | bytes 737312 | tf_op jit(solution)/shard_map/ppermute | solution.py:317
  56.0 3.5 %all-to-all-done.1 = bf16[16,40,1152]{2,1,0:T(8,128)(2,1)} async-done(((bf16[16,40,1152]{2,1,0:T(8,128)(2,1)}), bf16[16,40,1152]{2,1,0:T(8,128)(2,1)}, u32[]{:S(2)}, u32[]{:S(2)}) %all-to-all-start.1) | async-done | bytes 1474592 | tf_op jit(solution)/shard_map/all_to_all | solution.py:321
  59.5 4.5 %all-to-all-start.2 = ((bf16[16,40,1152]{2,1,0:T(8,128)(2,1)}), bf16[16,40,1152]{2,1,0:T(8,128)(2,1)}, u32[]{:S(2)}, u32[]{:S(2)}) async-start(bf16[16,40,1152]{2,1,0:T(8,128)(2,1)} %bitcast.9), calls=%async_computation.2 | async-start | bytes 2949120 | tf_op jit(solution)/shard_map/all_to_all | solution.py:321
  64.0 1.5 %collective-permute-start.7 = (bf16[320,1152]{1,0:T(8,128)(2,1)S(1)}, bf16[320,1152]{1,0:T(8,128)(2,1)S(1)}, u32[]{:S(2)}, u32[]{:S(2)}) collective-permute-start(bf16[320,1152]{1,0:T(8,128)(2,1)S(1)} %shard_map.95.refs_1_.refs_9_), channel_id=1, source_target_pairs={{0,64},{32,96},{64,0},{96,32},{1,65},{33,97},{65,1},{97,33},{2,66}... | collective-permute-start | bytes 2211848 | tf_op jit(solution)/shard_map/ppermute | solution.py:317
  65.5 12.6 %shard_map.99 = (bf16[1152,640]{1,0:T(8,128)(2,1)}, bf16[1152,640]{1,0:T(8,128)(2,1)}, bf16[640,1152]{1,0:T(8,128)(2,1)}, bf16[336,1152]{1,0:T(8,128)(2,1)}, bf16[336,1152]{1,0:T(8,128)(2,1)}) custom-call(bf16[320,1152]{1,0:T(8,128)(2,1)} %copy-done.5, bf16[320,1152]{1,0:T(8,128)(2,1)} %copy-done.6, bf16[640,1152]{1,0:T(8,128)(2,1)} %bitcast.8.refs_2_, ...), custom_call_target="tpu_custom_call" | custom-call | flops 1 | bytes 1 | tf_op jit(solution)/shard_map/pallas_call | solution.py:369
  78.1 1.9 %collective-permute-start.8 = (bf16[336,1152]{1,0:T(8,128)(2,1)}, bf16[336,1152]{1,0:T(8,128)(2,1)S(1)}, u32[]{:S(2)}, u32[]{:S(2)}) collective-permute-start(bf16[336,1152]{1,0:T(8,128)(2,1)} %get-tuple-element.64), channel_id=1, source_target_pairs={{0,96},{32,0},{64,32},{96,64},{1,97},{33,1},{65,33},{97,65},{2,98}... | collective-permute-start | bytes 2322440 | tf_op jit(solution)/shard_map/ppermute | solution.py:317
  80.1 0.7 collective-permute-start.10
  80.8 1.2 collective-permute-done.7.refs_0_.refs_8_
  82.0 1.9 %all-to-all-done.2 = bf16[16,40,1152]{2,1,0:T(8,128)(2,1)} async-done(((bf16[16,40,1152]{2,1,0:T(8,128)(2,1)}), bf16[16,40,1152]{2,1,0:T(8,128)(2,1)}, u32[]{:S(2)}, u32[]{:S(2)}) %all-to-all-start.2) | async-done | bytes 1474592 | tf_op jit(solution)/shard_map/all_to_all | solution.py:321
  84.0 12.6 %shard_map.98 = (bf16[1152,640]{1,0:T(8,128)(2,1)}, bf16[1152,640]{1,0:T(8,128)(2,1)}, bf16[640,1152]{1,0:T(8,128)(2,1)}, bf16[336,1152]{1,0:T(8,128)(2,1)}, bf16[336,1152]{1,0:T(8,128)(2,1)}) custom-call(bf16[320,1152]{1,0:T(8,128)(2,1)} %copy-done.7, bf16[320,1152]{1,0:T(8,128)(2,1)} %copy-done, bf16[640,1152]{1,0:T(8,128)(2,1)} %bitcast.10.refs_2_, ...), custom_call_target="tpu_custom_call" | custom-call | flops 1 | bytes 1 | tf_op jit(solution)/shard_map/pallas_call | solution.py:369
  96.9 12.1 %shard_map.100 = (bf16[576,1152]{1,0:T(8,128)(2,1)}, bf16[576,1152]{1,0:T(8,128)(2,1)}, bf16[1152,1152]{1,0:T(8,128)(2,1)}) custom-call(bf16[1152,640]{1,0:T(8,128)(2,1)} %get-tuple-element.67.refs_0_, bf16[1152,640]{1,0:T(8,128)(2,1)} %get-tuple-element.68.refs_1_, bf16[640,1152]{1,0:T(8,128)(2,1)} %get-tuple-element.69.refs_2_, ...), custom_call_target="tpu_custom_call" | custom-call | flops 1 | bytes 1 | tf_op jit(solution)/shard_map/pallas_call | solution.py:392
  109.0 3.7 %collective-permute-done.8.refs_1_ = bf16[336,1152]{1,0:T(8,128)(2,1)S(1)} collective-permute-done((bf16[336,1152]{1,0:T(8,128)(2,1)}, bf16[336,1152]{1,0:T(8,128)(2,1)S(1)}, u32[]{:S(2)}, u32[]{:S(2)}) %collective-permute-start.8) | collective-permute-done | bytes 774176 | tf_op jit(solution)/shard_map/ppermute | solution.py:317
  112.7 2.0 %collective-permute-done.10.refs_3_ = bf16[336,1152]{1,0:T(8,128)(2,1)S(1)} collective-permute-done((bf16[336,1152]{1,0:T(8,128)(2,1)}, bf16[336,1152]{1,0:T(8,128)(2,1)S(1)}, u32[]{:S(2)}, u32[]{:S(2)}) %collective-permute-start.10) | collective-permute-done | bytes 774176 | tf_op jit(solution)/shard_map/ppermute | solution.py:317
  114.7 2.0 %shard_map.101 = bf16[384,1152]{1,0:T(8,128)(2,1)} custom-call(bf16[336,1152]{1,0:T(8,128)(2,1)S(1)} %copy-done.1, bf16[336,1152]{1,0:T(8,128)(2,1)S(1)} %collective-permute-done.8.refs_1_, bf16[336,1152]{1,0:T(8,128)(2,1)S(1)} %collective-permute-done.9.refs_2_, bf16[336,1152]{1,0:T(8,128)(2,1)S(1)} %collective-permute-done.10.refs_3_), custom_call_target="tpu_custom_call" | custom-call | flops 1 | bytes 1 | tf_op jit(solution)/shard_map/pallas_call | solution.py:404
  116.7 6.9 %all-to-all-start.3 = ((bf16[16,24,1152]{2,1,0:T(8,128)(2,1)}), bf16[16,24,1152]{2,1,0:T(8,128)(2,1)S(1)}, u32[]{:S(2)}, u32[]{:S(2)}) async-start(bf16[16,24,1152]{2,1,0:T(8,128)(2,1)} %bitcast.12), calls=%async_computation.3 | async-start | bytes 1769472 | tf_op jit(solution)/shard_map/all_to_all | solution.py:321
  124.0 0.9 copy-done.8
  125.3 2.0 %fusion = (bf16[576,1152]{1,0:T(8,128)(2,1)}, bf16[576,1152]{1,0:T(8,128)(2,1)}) fusion(f32[1152,1152]{1,0:T(8,128)S(1)} %convert_element_type.16, bf16[576,1152]{1,0:T(8,128)(2,1)S(1)} %copy-done.9, bf16[576,1152]{1,0:T(8,128)(2,1)S(1)} %copy-done.8), kind=kLoop, calls=%fused_computation.1 | loop fusion | flops 3981312 | bytes 10616832 | tf_op jit(solution)/shard_map/convert_element_type | solution.py:410
  127.3 12.6 %all-to-all-done.3 = bf16[16,24,1152]{2,1,0:T(8,128)(2,1)S(1)} async-done(((bf16[16,24,1152]{2,1,0:T(8,128)(2,1)}), bf16[16,24,1152]{2,1,0:T(8,128)(2,1)S(1)}, u32[]{:S(2)}, u32[]{:S(2)}) %all-to-all-start.3) | async-done | bytes 884768 | tf_op jit(solution)/shard_map/all_to_all | solution.py:321
  139.9 1.4 shard_map.102
  (32 shorter events, 1.5 us)
Async XLA Ops:
  0.6 22.1 %collective-permute-start.1 = (bf16[576,1152]{1,0:T(8,128)(2,1)}, bf16[576,1152]{1,0:T(8,128)(2,1)}, u32[]{:S(2)}, u32[]{:S(2)}) collective-permute-start(bf16[576,1152]{1,0:T(8,128)(2,1)} %bitcast.26), channel_id=1, source_target_pairs={{0,16},{16,0},{1,17},{17,1},{2,18},{18,2},{3,19},{19,3},{4,20},{20... | collective-permute-start | bytes 3981320 | tf_op jit(solution)/shard_map/ppermute | solution.py:317
  0.7 22.0 %collective-permute-start.2 = (bf16[576,1152]{1,0:T(8,128)(2,1)}, bf16[576,1152]{1,0:T(8,128)(2,1)}, u32[]{:S(2)}, u32[]{:S(2)}) collective-permute-start(bf16[576,1152]{1,0:T(8,128)(2,1)} %bitcast.29), channel_id=1, source_target_pairs={{0,16},{16,0},{1,17},{17,1},{2,18},{18,2},{3,19},{19,3},{4,20},{20... | collective-permute-start | bytes 3981320 | tf_op jit(solution)/shard_map/ppermute | solution.py:317
  1.2 10.5 %copy-start.2 = (bf16[128,1152]{1,0:T(8,128)(2,1)S(1)}, bf16[128,1152]{1,0:T(8,128)(2,1)}, u32[]{:S(2)}) copy-start(bf16[128,1152]{1,0:T(8,128)(2,1)} %dy_ref.1) | copy-start | bytes 884740
  1.2 10.5 %copy-start.3 = (s32[128,2]{0,1:T(2,128)S(1)}, s32[128,2]{0,1:T(2,128)}, u32[]{:S(2)}) copy-start(s32[128,2]{0,1:T(2,128)} %param.9) | copy-start | bytes 3076
  1.2 10.6 %copy-start.4 = (f32[128,2]{0,1:T(2,128)S(1)}, f32[128,2]{0,1:T(2,128)}, u32[]{:S(2)}) copy-start(f32[128,2]{0,1:T(2,128)} %param.8) | copy-start | bytes 3076
  3.8 25.4 %all-to-all-start = ((bf16[16,24,1152]{2,1,0:T(8,128)(2,1)}), bf16[16,24,1152]{2,1,0:T(8,128)(2,1)S(1)}, u32[]{:S(2)}, u32[]{:S(2)}) async-start(bf16[16,24,1152]{2,1,0:T(8,128)(2,1)} %bitcast.32), calls=%async_computation | async-start | bytes 1769472 | tf_op jit(solution)/shard_map/all_to_all | solution.py:321
  11.8 10.9 %collective-permute-start = (bf16[144,1152]{1,0:T(8,128)(2,1)S(1)}, bf16[144,1152]{1,0:T(8,128)(2,1)S(1)}, u32[]{:S(2)}, u32[]{:S(2)}) collective-permute-start(bf16[144,1152]{1,0:T(8,128)(2,1)S(1)} %shard_map.94.refs_1_), channel_id=1, source_target_pairs={{0,32},{32,64},{64,96},{96,0},{1,33},{33,65},{65,97},{97,1},{2,34}... | collective-permute-start | bytes 995336 | tf_op jit(solution)/shard_map/ppermute | solution.py:317
  13.5 15.7 %collective-permute-start.3 = (bf16[144,1152]{1,0:T(8,128)(2,1)S(1)}, bf16[144,1152]{1,0:T(8,128)(2,1)S(1)}, u32[]{:S(2)}, u32[]{:S(2)}) collective-permute-start(bf16[144,1152]{1,0:T(8,128)(2,1)S(1)} %shard_map.94.refs_1_), channel_id=1, source_target_pairs={{0,96},{32,0},{64,32},{96,64},{1,97},{33,1},{65,33},{97,65},{2,98}... | collective-permute-start | bytes 995336 | tf_op jit(solution)/shard_map/ppermute | solution.py:317
  15.1 16.8 %collective-permute-start.4 = (bf16[144,1152]{1,0:T(8,128)(2,1)S(1)}, bf16[144,1152]{1,0:T(8,128)(2,1)S(1)}, u32[]{:S(2)}, u32[]{:S(2)}) collective-permute-start(bf16[144,1152]{1,0:T(8,128)(2,1)S(1)} %shard_map.94.refs_1_), channel_id=1, source_target_pairs={{0,64},{32,96},{64,0},{96,32},{1,65},{33,97},{65,1},{97,33},{2,66}... | collective-permute-start | bytes 995336 | tf_op jit(solution)/shard_map/ppermute | solution.py:317
  29.8 34.2 %copy-start = (bf16[320,1152]{1,0:T(8,128)(2,1)}, bf16[320,1152]{1,0:T(8,128)(2,1)S(1)}, u32[]{:S(2)}) copy-start(bf16[320,1152]{1,0:T(8,128)(2,1)S(1)} %shard_map.95.refs_1_.refs_9_) | copy-start | bytes 2211844
  31.9 27.6 %all-to-all-start.1 = ((bf16[16,40,1152]{2,1,0:T(8,128)(2,1)}), bf16[16,40,1152]{2,1,0:T(8,128)(2,1)}, u32[]{:S(2)}, u32[]{:S(2)}) async-start(bf16[16,40,1152]{2,1,0:T(8,128)(2,1)} %bitcast.7), calls=%async_computation.1 | async-start | bytes 2949120 | tf_op jit(solution)/shard_map/all_to_all | solution.py:321
  38.9 17.1 %collective-permute-start.5 = (bf16[320,1152]{1,0:T(8,128)(2,1)S(1)}, bf16[320,1152]{1,0:T(8,128)(2,1)S(1)}, u32[]{:S(2)}, u32[]{:S(2)}) collective-permute-start(bf16[320,1152]{1,0:T(8,128)(2,1)S(1)} %shard_map.95.refs_1_.refs_9_), channel_id=1, source_target_pairs={{0,32},{32,64},{64,96},{96,0},{1,33},{33,65},{65,97},{97,1},{2,34}... | collective-permute-start | bytes 2211848 | tf_op jit(solution)/shard_map/ppermute | solution.py:317
  39.2 16.8 %collective-permute-start.6 = (bf16[320,1152]{1,0:T(8,128)(2,1)S(1)}, bf16[320,1152]{1,0:T(8,128)(2,1)S(1)}, u32[]{:S(2)}, u32[]{:S(2)}) collective-permute-start(bf16[320,1152]{1,0:T(8,128)(2,1)S(1)} %shard_map.95.refs_1_.refs_9_), channel_id=1, source_target_pairs={{0,96},{32,0},{64,32},{96,64},{1,97},{33,1},{65,33},{97,65},{2,98}... | collective-permute-start | bytes 2211848 | tf_op jit(solution)/shard_map/ppermute | solution.py:317
  56.0 3.5 %copy-start.5 = (bf16[320,1152]{1,0:T(8,128)(2,1)}, bf16[320,1152]{1,0:T(8,128)(2,1)S(1)}, u32[]{:S(2)}) copy-start(bf16[320,1152]{1,0:T(8,128)(2,1)S(1)} %collective-permute-done.5.refs_0_.refs_6_) | copy-start | bytes 2211844
  56.0 3.5 %copy-start.6 = (bf16[320,1152]{1,0:T(8,128)(2,1)}, bf16[320,1152]{1,0:T(8,128)(2,1)S(1)}, u32[]{:S(2)}) copy-start(bf16[320,1152]{1,0:T(8,128)(2,1)S(1)} %collective-permute-done.6.refs_1_.refs_7_) | copy-start | bytes 2211844
  59.5 24.5 %all-to-all-start.2 = ((bf16[16,40,1152]{2,1,0:T(8,128)(2,1)}), bf16[16,40,1152]{2,1,0:T(8,128)(2,1)}, u32[]{:S(2)}, u32[]{:S(2)}) async-start(bf16[16,40,1152]{2,1,0:T(8,128)(2,1)} %bitcast.9), calls=%async_computation.2 | async-start | bytes 2949120 | tf_op jit(solution)/shard_map/all_to_all | solution.py:321
  64.0 18.0 %collective-permute-start.7 = (bf16[320,1152]{1,0:T(8,128)(2,1)S(1)}, bf16[320,1152]{1,0:T(8,128)(2,1)S(1)}, u32[]{:S(2)}, u32[]{:S(2)}) collective-permute-start(bf16[320,1152]{1,0:T(8,128)(2,1)S(1)} %shard_map.95.refs_1_.refs_9_), channel_id=1, source_target_pairs={{0,64},{32,96},{64,0},{96,32},{1,65},{33,97},{65,1},{97,33},{2,66}... | collective-permute-start | bytes 2211848 | tf_op jit(solution)/shard_map/ppermute | solution.py:317
  78.1 34.6 %collective-permute-start.8 = (bf16[336,1152]{1,0:T(8,128)(2,1)}, bf16[336,1152]{1,0:T(8,128)(2,1)S(1)}, u32[]{:S(2)}, u32[]{:S(2)}) collective-permute-start(bf16[336,1152]{1,0:T(8,128)(2,1)} %get-tuple-element.64), channel_id=1, source_target_pairs={{0,96},{32,0},{64,32},{96,64},{1,97},{33,1},{65,33},{97,65},{2,98}... | collective-permute-start | bytes 2322440 | tf_op jit(solution)/shard_map/ppermute | solution.py:317
  80.1 34.6 %collective-permute-start.10 = (bf16[336,1152]{1,0:T(8,128)(2,1)}, bf16[336,1152]{1,0:T(8,128)(2,1)S(1)}, u32[]{:S(2)}, u32[]{:S(2)}) collective-permute-start(bf16[336,1152]{1,0:T(8,128)(2,1)} %get-tuple-element.66), channel_id=1, source_target_pairs={{0,32},{32,64},{64,96},{96,0},{1,33},{33,65},{65,97},{97,1},{2,34}... | collective-permute-start | bytes 2322440 | tf_op jit(solution)/shard_map/ppermute | solution.py:317
  82.0 1.9 %copy-start.7 = (bf16[320,1152]{1,0:T(8,128)(2,1)}, bf16[320,1152]{1,0:T(8,128)(2,1)S(1)}, u32[]{:S(2)}) copy-start(bf16[320,1152]{1,0:T(8,128)(2,1)S(1)} %collective-permute-done.7.refs_0_.refs_8_) | copy-start | bytes 2211844
  96.6 18.1 %collective-permute-start.9 = (bf16[336,1152]{1,0:T(8,128)(2,1)}, bf16[336,1152]{1,0:T(8,128)(2,1)S(1)}, u32[]{:S(2)}, u32[]{:S(2)}) collective-permute-start(bf16[336,1152]{1,0:T(8,128)(2,1)} %get-tuple-element.65), channel_id=1, source_target_pairs={{0,64},{32,96},{64,0},{96,32},{1,65},{33,97},{65,1},{97,33},{2,66}... | collective-permute-start | bytes 2322440 | tf_op jit(solution)/shard_map/ppermute | solution.py:317
  96.9 17.8 %copy-start.1 = (bf16[336,1152]{1,0:T(8,128)(2,1)S(1)}, bf16[336,1152]{1,0:T(8,128)(2,1)}, u32[]{:S(2)}) copy-start(bf16[336,1152]{1,0:T(8,128)(2,1)} %get-tuple-element.75.refs_0_) | copy-start | bytes 2322436
  116.7 6.9 %collective-permute-start.11 = (bf16[1152,1152]{1,0:T(8,128)(2,1)}, bf16[1152,1152]{1,0:T(8,128)(2,1)S(1)}, u32[]{:S(2)}, u32[]{:S(2)}) collective-permute-start(bf16[1152,1152]{1,0:T(8,128)(2,1)} %get-tuple-element.81), channel_id=1, source_target_pairs={{0,16},{16,0},{1,17},{17,1},{2,18},{18,2},{3,19},{19,3},{4,20},{20... | collective-permute-start | bytes 7962632 | tf_op jit(solution)/shard_map/ppermute | solution.py:317
  116.7 23.2 %all-to-all-start.3 = ((bf16[16,24,1152]{2,1,0:T(8,128)(2,1)}), bf16[16,24,1152]{2,1,0:T(8,128)(2,1)S(1)}, u32[]{:S(2)}, u32[]{:S(2)}) async-start(bf16[16,24,1152]{2,1,0:T(8,128)(2,1)} %bitcast.12), calls=%async_computation.3 | async-start | bytes 1769472 | tf_op jit(solution)/shard_map/all_to_all | solution.py:321
  123.6 1.3 copy-start.8
  123.6 1.7 %copy-start.9 = (bf16[576,1152]{1,0:T(8,128)(2,1)S(1)}, bf16[576,1152]{1,0:T(8,128)(2,1)}, u32[]{:S(2)}) copy-start(bf16[576,1152]{1,0:T(8,128)(2,1)} %get-tuple-element.82) | copy-start | bytes 3981316

commit v5 on v4

--- a/solution.py
+++ b/solution.py
@@ -342,6 +342,7 @@
     xs = call(functools.partial(pick_kernel, experts), arr(experts * eights(CAP), width), LARGE)(
         hidden_in, names
     )
+    wi, wo, _ = after((wi, wo, xs))
     wi_other, wo_other = shift(wi, "seq", 1), shift(wo, "seq", 1)
     msgs[1], wi_other, wo_other = after((msgs[1], wi_other, wo_other))
     xa, msgs[1], msgs[3] = after((exchange(xs), msgs[1], msgs[3]))

time: 142 us -> 141 us (level)
  transfers between devices with their start and end apart: 16 -> 16, of which waited for: 9 -> 9; matrix products, arithmetic and copies ran while one was open for 2% -> 2% of each run, Pallas kernels for 32% -> 30%
where the time goes in v5:
time: 141 us
  Pallas kernels  48 us (34%)
  waiting for transfers between devices  47.9 us (34%)
  starting transfers between devices  40.5 us (29%)
  other arithmetic  2.34 us (2%)
    ppermute x12, waiting for transfers between devices, shift(): lax.ppermute(value, axis, [(i, (i + by) % size) for i in range(size)])  29.7 us
    all_to_all x4, starting transfers between devices, exchange(): lax.all_to_all(value, 'expert', split_axis=0, concat_axis=0, tiled=True)  26.3 us
    pallas_call x2, Pallas kernels, rows_call(): call(functools.partial(rows_kernel, experts, len(parts), blocks), [arr(hi...  25.2 us
    all_to_all x4, waiting for transfers between devices, exchange(): lax.all_to_all(value, 'expert', split_axis=0, concat_axis=0, tiled=True)  18.2 us
    ppermute x12, starting transfers between devices, shift(): lax.ppermute(value, axis, [(i, (i + by) % size) for i in range(size)])  14.1 us
    pallas_call x1, Pallas kernels, local(): call(functools.partial(weights_kernel, len(GROUPS), len(parts_a + parts_b...  12.1 us
    pallas_call x2, Pallas kernels, expand(): call(functools.partial(expand_kernel, experts, CAP), arr(block * len(GROU...  4.19 us
  transfers between devices with their start and end apart: 16, of which 9 were waited for; matrix products, arithmetic and copies ran while one was open for 2% of the time, Pallas kernels for 30%

profile of v5, /device:TPU:0, one launch (start us, length us, event | category | flops | bytes accessed | tf_op | source)
XLA Modules:
  0.0 140.9 jit_solution(7087723595067910988)
XLA Ops:
  0.7 2.6 %shard_map.93 = bf16[384,1152]{1,0:T(8,128)(2,1)} custom-call(bf16[128,1152]{1,0:T(8,128)(2,1)} %x_ref.1, s32[2,128]{1,0:T(2,128)} %bitcast.21), custom_call_target="tpu_custom_call" | custom-call | flops 1 | bytes 1 | tf_op jit(solution)/shard_map/pallas_call | solution.py:342
  3.2 0.5 collective-permute-start.2
  3.7 8.0 %all-to-all-start = ((bf16[16,24,1152]{2,1,0:T(8,128)(2,1)}), bf16[16,24,1152]{2,1,0:T(8,128)(2,1)S(1)}, u32[]{:S(2)}, u32[]{:S(2)}) async-start(bf16[16,24,1152]{2,1,0:T(8,128)(2,1)} %bitcast.32), calls=%async_computation | async-start | bytes 1769472 | tf_op jit(solution)/shard_map/all_to_all | solution.py:321
  11.8 1.6 %collective-permute-start = (bf16[144,1152]{1,0:T(8,128)(2,1)S(1)}, bf16[144,1152]{1,0:T(8,128)(2,1)S(1)}, u32[]{:S(2)}, u32[]{:S(2)}) collective-permute-start(bf16[144,1152]{1,0:T(8,128)(2,1)S(1)} %shard_map.94.refs_1_), channel_id=1, source_target_pairs={{0,32},{32,64},{64,96},{96,0},{1,33},{33,65},{65,97},{97,1},{2,34}... | collective-permute-start | bytes 995336 | tf_op jit(solution)/shard_map/ppermute | solution.py:317
  13.4 1.7 %collective-permute-start.3 = (bf16[144,1152]{1,0:T(8,128)(2,1)S(1)}, bf16[144,1152]{1,0:T(8,128)(2,1)S(1)}, u32[]{:S(2)}, u32[]{:S(2)}) collective-permute-start(bf16[144,1152]{1,0:T(8,128)(2,1)S(1)} %shard_map.94.refs_1_), channel_id=1, source_target_pairs={{0,96},{32,0},{64,32},{96,64},{1,97},{33,1},{65,33},{97,65},{2,98}... | collective-permute-start | bytes 995336 | tf_op jit(solution)/shard_map/ppermute | solution.py:317
  15.1 2.0 %collective-permute-start.4 = (bf16[144,1152]{1,0:T(8,128)(2,1)S(1)}, bf16[144,1152]{1,0:T(8,128)(2,1)S(1)}, u32[]{:S(2)}, u32[]{:S(2)}) collective-permute-start(bf16[144,1152]{1,0:T(8,128)(2,1)S(1)} %shard_map.94.refs_1_), channel_id=1, source_target_pairs={{0,64},{32,96},{64,0},{96,32},{1,65},{33,97},{65,1},{97,33},{2,66}... | collective-permute-start | bytes 995336 | tf_op jit(solution)/shard_map/ppermute | solution.py:317
  17.1 5.6 %collective-permute-done.refs_0_ = bf16[144,1152]{1,0:T(8,128)(2,1)S(1)} collective-permute-done((bf16[144,1152]{1,0:T(8,128)(2,1)S(1)}, bf16[144,1152]{1,0:T(8,128)(2,1)S(1)}, u32[]{:S(2)}, u32[]{:S(2)}) %collective-permute-start) | collective-permute-done | bytes 331808 | tf_op jit(solution)/shard_map/ppermute | solution.py:317
  22.6 6.4 %collective-permute-done.3.refs_1_ = bf16[144,1152]{1,0:T(8,128)(2,1)S(1)} collective-permute-done((bf16[144,1152]{1,0:T(8,128)(2,1)S(1)}, bf16[144,1152]{1,0:T(8,128)(2,1)S(1)}, u32[]{:S(2)}, u32[]{:S(2)}) %collective-permute-start.3) | collective-permute-done | bytes 331808 | tf_op jit(solution)/shard_map/ppermute | solution.py:317
  29.0 0.6 shard_map.95.refs_1_.refs_9_
  29.7 2.1 %shard_map.96 = bf16[640,1152]{1,0:T(8,128)(2,1)} custom-call(bf16[144,1152]{1,0:T(8,128)(2,1)S(1)} %collective-permute-done.refs_0_, bf16[144,1152]{1,0:T(8,128)(2,1)S(1)} %collective-permute-done.3.refs_1_), custom_call_target="tpu_custom_call" | custom-call | flops 1 | bytes 1 | tf_op jit(solution)/shard_map/pallas_call | solution.py:353
  31.8 7.0 %all-to-all-start.1 = ((bf16[16,40,1152]{2,1,0:T(8,128)(2,1)}), bf16[16,40,1152]{2,1,0:T(8,128)(2,1)}, u32[]{:S(2)}, u32[]{:S(2)}) async-start(bf16[16,40,1152]{2,1,0:T(8,128)(2,1)} %bitcast.7), calls=%async_computation.1 | async-start | bytes 2949120 | tf_op jit(solution)/shard_map/all_to_all | solution.py:321
  39.0 3.5 %collective-permute-start.6 = (bf16[320,1152]{1,0:T(8,128)(2,1)S(1)}, bf16[320,1152]{1,0:T(8,128)(2,1)S(1)}, u32[]{:S(2)}, u32[]{:S(2)}) collective-permute-start(bf16[320,1152]{1,0:T(8,128)(2,1)S(1)} %shard_map.95.refs_1_.refs_9_), channel_id=1, source_target_pairs={{0,96},{32,0},{64,32},{96,64},{1,97},{33,1},{65,33},{97,65},{2,98}... | collective-permute-start | bytes 2211848 | tf_op jit(solution)/shard_map/ppermute | solution.py:317
  42.6 2.1 %shard_map.97 = bf16[640,1152]{1,0:T(8,128)(2,1)} custom-call(bf16[144,1152]{1,0:T(8,128)(2,1)S(1)} %collective-permute-done.4.refs_0_, bf16[144,1152]{1,0:T(8,128)(2,1)S(1)} %shard_map.94.refs_1_), custom_call_target="tpu_custom_call" | custom-call | flops 1 | bytes 1 | tf_op jit(solution)/shard_map/pallas_call | solution.py:353
  44.7 11.1 %collective-permute-done.5.refs_0_.refs_6_ = bf16[320,1152]{1,0:T(8,128)(2,1)S(1)} collective-permute-done((bf16[320,1152]{1,0:T(8,128)(2,1)S(1)}, bf16[320,1152]{1,0:T(8,128)(2,1)S(1)}, u32[]{:S(2)}, u32[]{:S(2)}) %collective-permute-start.5) | collective-permute-done | bytes 737312 | tf_op jit(solution)/shard_map/ppermute | solution.py:317
  55.7 3.5 %all-to-all-done.1 = bf16[16,40,1152]{2,1,0:T(8,128)(2,1)} async-done(((bf16[16,40,1152]{2,1,0:T(8,128)(2,1)}), bf16[16,40,1152]{2,1,0:T(8,128)(2,1)}, u32[]{:S(2)}, u32[]{:S(2)}) %all-to-all-start.1) | async-done | bytes 1474592 | tf_op jit(solution)/shard_map/all_to_all | solution.py:321
  59.2 4.5 %all-to-all-start.2 = ((bf16[16,40,1152]{2,1,0:T(8,128)(2,1)}), bf16[16,40,1152]{2,1,0:T(8,128)(2,1)}, u32[]{:S(2)}, u32[]{:S(2)}) async-start(bf16[16,40,1152]{2,1,0:T(8,128)(2,1)} %bitcast.9), calls=%async_computation.2 | async-start | bytes 2949120 | tf_op jit(solution)/shard_map/all_to_all | solution.py:321
  63.8 1.5 %collective-permute-start.7 = (bf16[320,1152]{1,0:T(8,128)(2,1)S(1)}, bf16[320,1152]{1,0:T(8,128)(2,1)S(1)}, u32[]{:S(2)}, u32[]{:S(2)}) collective-permute-start(bf16[320,1152]{1,0:T(8,128)(2,1)S(1)} %shard_map.95.refs_1_.refs_9_), channel_id=1, source_target_pairs={{0,64},{32,96},{64,0},{96,32},{1,65},{33,97},{65,1},{97,33},{2,66}... | collective-permute-start | bytes 2211848 | tf_op jit(solution)/shard_map/ppermute | solution.py:317
  65.3 12.6 %shard_map.99 = (bf16[1152,640]{1,0:T(8,128)(2,1)}, bf16[1152,640]{1,0:T(8,128)(2,1)}, bf16[640,1152]{1,0:T(8,128)(2,1)}, bf16[336,1152]{1,0:T(8,128)(2,1)}, bf16[336,1152]{1,0:T(8,128)(2,1)}) custom-call(bf16[320,1152]{1,0:T(8,128)(2,1)} %copy-done.5, bf16[320,1152]{1,0:T(8,128)(2,1)} %copy-done.6, bf16[640,1152]{1,0:T(8,128)(2,1)} %bitcast.8.refs_2_, ...), custom_call_target="tpu_custom_call" | custom-call | flops 1 | bytes 1 | tf_op jit(solution)/shard_map/pallas_call | solution.py:370
  77.9 2.0 %collective-permute-start.8 = (bf16[336,1152]{1,0:T(8,128)(2,1)}, bf16[336,1152]{1,0:T(8,128)(2,1)S(1)}, u32[]{:S(2)}, u32[]{:S(2)}) collective-permute-start(bf16[336,1152]{1,0:T(8,128)(2,1)} %get-tuple-element.68), channel_id=1, source_target_pairs={{0,96},{32,0},{64,32},{96,64},{1,97},{33,1},{65,33},{97,65},{2,98}... | collective-permute-start | bytes 2322440 | tf_op jit(solution)/shard_map/ppermute | solution.py:317
  79.9 0.7 collective-permute-start.10
  80.5 1.0 collective-permute-done.7.refs_0_.refs_8_
  81.5 2.1 %all-to-all-done.2 = bf16[16,40,1152]{2,1,0:T(8,128)(2,1)} async-done(((bf16[16,40,1152]{2,1,0:T(8,128)(2,1)}), bf16[16,40,1152]{2,1,0:T(8,128)(2,1)}, u32[]{:S(2)}, u32[]{:S(2)}) %all-to-all-start.2) | async-done | bytes 1474592 | tf_op jit(solution)/shard_map/all_to_all | solution.py:321
  83.6 12.6 %shard_map.98 = (bf16[1152,640]{1,0:T(8,128)(2,1)}, bf16[1152,640]{1,0:T(8,128)(2,1)}, bf16[640,1152]{1,0:T(8,128)(2,1)}, bf16[336,1152]{1,0:T(8,128)(2,1)}, bf16[336,1152]{1,0:T(8,128)(2,1)}) custom-call(bf16[320,1152]{1,0:T(8,128)(2,1)} %copy-done.7, bf16[320,1152]{1,0:T(8,128)(2,1)} %copy-done, bf16[640,1152]{1,0:T(8,128)(2,1)} %bitcast.10.refs_2_, ...), custom_call_target="tpu_custom_call" | custom-call | flops 1 | bytes 1 | tf_op jit(solution)/shard_map/pallas_call | solution.py:370
  96.6 12.1 %shard_map.100 = (bf16[576,1152]{1,0:T(8,128)(2,1)}, bf16[576,1152]{1,0:T(8,128)(2,1)}, bf16[1152,1152]{1,0:T(8,128)(2,1)}) custom-call(bf16[1152,640]{1,0:T(8,128)(2,1)} %get-tuple-element.71.refs_0_, bf16[1152,640]{1,0:T(8,128)(2,1)} %get-tuple-element.72.refs_1_, bf16[640,1152]{1,0:T(8,128)(2,1)} %get-tuple-element.73.refs_2_, ...), custom_call_target="tpu_custom_call" | custom-call | flops 1 | bytes 1 | tf_op jit(solution)/shard_map/pallas_call | solution.py:393
  108.7 3.8 %collective-permute-done.8.refs_1_ = bf16[336,1152]{1,0:T(8,128)(2,1)S(1)} collective-permute-done((bf16[336,1152]{1,0:T(8,128)(2,1)}, bf16[336,1152]{1,0:T(8,128)(2,1)S(1)}, u32[]{:S(2)}, u32[]{:S(2)}) %collective-permute-start.8) | collective-permute-done | bytes 774176 | tf_op jit(solution)/shard_map/ppermute | solution.py:317
  112.4 1.9 %collective-permute-done.10.refs_3_ = bf16[336,1152]{1,0:T(8,128)(2,1)S(1)} collective-permute-done((bf16[336,1152]{1,0:T(8,128)(2,1)}, bf16[336,1152]{1,0:T(8,128)(2,1)S(1)}, u32[]{:S(2)}, u32[]{:S(2)}) %collective-permute-start.10) | collective-permute-done | bytes 774176 | tf_op jit(solution)/shard_map/ppermute | solution.py:317
  114.3 2.0 %shard_map.101 = bf16[384,1152]{1,0:T(8,128)(2,1)} custom-call(bf16[336,1152]{1,0:T(8,128)(2,1)S(1)} %copy-done.1, bf16[336,1152]{1,0:T(8,128)(2,1)S(1)} %collective-permute-done.8.refs_1_, bf16[336,1152]{1,0:T(8,128)(2,1)S(1)} %collective-permute-done.9.refs_2_, bf16[336,1152]{1,0:T(8,128)(2,1)S(1)} %collective-permute-done.10.refs_3_), custom_call_target="tpu_custom_call" | custom-call | flops 1 | bytes 1 | tf_op jit(solution)/shard_map/pallas_call | solution.py:405
  116.3 6.9 %all-to-all-start.3 = ((bf16[16,24,1152]{2,1,0:T(8,128)(2,1)}), bf16[16,24,1152]{2,1,0:T(8,128)(2,1)S(1)}, u32[]{:S(2)}, u32[]{:S(2)}) async-start(bf16[16,24,1152]{2,1,0:T(8,128)(2,1)} %bitcast.11), calls=%async_computation.3 | async-start | bytes 1769472 | tf_op jit(solution)/shard_map/all_to_all | solution.py:321
  123.6 0.9 copy-done.8
  124.9 2.0 %fusion = (bf16[576,1152]{1,0:T(8,128)(2,1)}, bf16[576,1152]{1,0:T(8,128)(2,1)}) fusion(f32[1152,1152]{1,0:T(8,128)S(1)} %convert_element_type.16, bf16[576,1152]{1,0:T(8,128)(2,1)S(1)} %copy-done.9, bf16[576,1152]{1,0:T(8,128)(2,1)S(1)} %copy-done.8), kind=kLoop, calls=%fused_computation.1 | loop fusion | flops 3981312 | bytes 10616832 | tf_op jit(solution)/shard_map/convert_element_type | solution.py:411
  126.9 12.6 %all-to-all-done.3 = bf16[16,24,1152]{2,1,0:T(8,128)(2,1)S(1)} async-done(((bf16[16,24,1152]{2,1,0:T(8,128)(2,1)}), bf16[16,24,1152]{2,1,0:T(8,128)(2,1)S(1)}, u32[]{:S(2)}, u32[]{:S(2)}) %all-to-all-start.3) | async-done | bytes 884768 | tf_op jit(solution)/shard_map/all_to_all | solution.py:321
  139.5 1.4 shard_map.102
  (32 shorter events, 1.5 us)
Async XLA Ops:
  0.6 11.1 %copy-start.2 = (bf16[128,1152]{1,0:T(8,128)(2,1)S(1)}, bf16[128,1152]{1,0:T(8,128)(2,1)}, u32[]{:S(2)}) copy-start(bf16[128,1152]{1,0:T(8,128)(2,1)} %dy_ref.1) | copy-start | bytes 884740
  0.6 11.1 %copy-start.3 = (s32[128,2]{0,1:T(2,128)S(1)}, s32[128,2]{0,1:T(2,128)}, u32[]{:S(2)}) copy-start(s32[128,2]{0,1:T(2,128)} %param.9) | copy-start | bytes 3076
  0.7 11.1 %copy-start.4 = (f32[128,2]{0,1:T(2,128)S(1)}, f32[128,2]{0,1:T(2,128)}, u32[]{:S(2)}) copy-start(f32[128,2]{0,1:T(2,128)} %param.8) | copy-start | bytes 3076
  3.2 19.4 %collective-permute-start.1 = (bf16[576,1152]{1,0:T(8,128)(2,1)}, bf16[576,1152]{1,0:T(8,128)(2,1)}, u32[]{:S(2)}, u32[]{:S(2)}) collective-permute-start(bf16[576,1152]{1,0:T(8,128)(2,1)} %bitcast.26), channel_id=1, source_target_pairs={{0,16},{16,0},{1,17},{17,1},{2,18},{18,2},{3,19},{19,3},{4,20},{20... | collective-permute-start | bytes 3981320 | tf_op jit(solution)/shard_map/ppermute | solution.py:317
  3.2 19.4 %collective-permute-start.2 = (bf16[576,1152]{1,0:T(8,128)(2,1)}, bf16[576,1152]{1,0:T(8,128)(2,1)}, u32[]{:S(2)}, u32[]{:S(2)}) collective-permute-start(bf16[576,1152]{1,0:T(8,128)(2,1)} %bitcast.29), channel_id=1, source_target_pairs={{0,16},{16,0},{1,17},{17,1},{2,18},{18,2},{3,19},{19,3},{4,20},{20... | collective-permute-start | bytes 3981320 | tf_op jit(solution)/shard_map/ppermute | solution.py:317
  3.7 25.3 %all-to-all-start = ((bf16[16,24,1152]{2,1,0:T(8,128)(2,1)}), bf16[16,24,1152]{2,1,0:T(8,128)(2,1)S(1)}, u32[]{:S(2)}, u32[]{:S(2)}) async-start(bf16[16,24,1152]{2,1,0:T(8,128)(2,1)} %bitcast.32), calls=%async_computation | async-start | bytes 1769472 | tf_op jit(solution)/shard_map/all_to_all | solution.py:321
  11.8 10.9 %collective-permute-start = (bf16[144,1152]{1,0:T(8,128)(2,1)S(1)}, bf16[144,1152]{1,0:T(8,128)(2,1)S(1)}, u32[]{:S(2)}, u32[]{:S(2)}) collective-permute-start(bf16[144,1152]{1,0:T(8,128)(2,1)S(1)} %shard_map.94.refs_1_), channel_id=1, source_target_pairs={{0,32},{32,64},{64,96},{96,0},{1,33},{33,65},{65,97},{97,1},{2,34}... | collective-permute-start | bytes 995336 | tf_op jit(solution)/shard_map/ppermute | solution.py:317
  13.4 15.6 %collective-permute-start.3 = (bf16[144,1152]{1,0:T(8,128)(2,1)S(1)}, bf16[144,1152]{1,0:T(8,128)(2,1)S(1)}, u32[]{:S(2)}, u32[]{:S(2)}) collective-permute-start(bf16[144,1152]{1,0:T(8,128)(2,1)S(1)} %shard_map.94.refs_1_), channel_id=1, source_target_pairs={{0,96},{32,0},{64,32},{96,64},{1,97},{33,1},{65,33},{97,65},{2,98}... | collective-permute-start | bytes 995336 | tf_op jit(solution)/shard_map/ppermute | solution.py:317
  15.1 16.7 %collective-permute-start.4 = (bf16[144,1152]{1,0:T(8,128)(2,1)S(1)}, bf16[144,1152]{1,0:T(8,128)(2,1)S(1)}, u32[]{:S(2)}, u32[]{:S(2)}) collective-permute-start(bf16[144,1152]{1,0:T(8,128)(2,1)S(1)} %shard_map.94.refs_1_), channel_id=1, source_target_pairs={{0,64},{32,96},{64,0},{96,32},{1,65},{33,97},{65,1},{97,33},{2,66}... | collective-permute-start | bytes 995336 | tf_op jit(solution)/shard_map/ppermute | solution.py:317
  29.7 34.1 %copy-start = (bf16[320,1152]{1,0:T(8,128)(2,1)}, bf16[320,1152]{1,0:T(8,128)(2,1)S(1)}, u32[]{:S(2)}) copy-start(bf16[320,1152]{1,0:T(8,128)(2,1)S(1)} %shard_map.95.refs_1_.refs_9_) | copy-start | bytes 2211844
  31.8 27.5 %all-to-all-start.1 = ((bf16[16,40,1152]{2,1,0:T(8,128)(2,1)}), bf16[16,40,1152]{2,1,0:T(8,128)(2,1)}, u32[]{:S(2)}, u32[]{:S(2)}) async-start(bf16[16,40,1152]{2,1,0:T(8,128)(2,1)} %bitcast.7), calls=%async_computation.1 | async-start | bytes 2949120 | tf_op jit(solution)/shard_map/all_to_all | solution.py:321
  38.8 17.0 %collective-permute-start.5 = (bf16[320,1152]{1,0:T(8,128)(2,1)S(1)}, bf16[320,1152]{1,0:T(8,128)(2,1)S(1)}, u32[]{:S(2)}, u32[]{:S(2)}) collective-permute-start(bf16[320,1152]{1,0:T(8,128)(2,1)S(1)} %shard_map.95.refs_1_.refs_9_), channel_id=1, source_target_pairs={{0,32},{32,64},{64,96},{96,0},{1,33},{33,65},{65,97},{97,1},{2,34}... | collective-permute-start | bytes 2211848 | tf_op jit(solution)/shard_map/ppermute | solution.py:317
  39.0 16.7 %collective-permute-start.6 = (bf16[320,1152]{1,0:T(8,128)(2,1)S(1)}, bf16[320,1152]{1,0:T(8,128)(2,1)S(1)}, u32[]{:S(2)}, u32[]{:S(2)}) collective-permute-start(bf16[320,1152]{1,0:T(8,128)(2,1)S(1)} %shard_map.95.refs_1_.refs_9_), channel_id=1, source_target_pairs={{0,96},{32,0},{64,32},{96,64},{1,97},{33,1},{65,33},{97,65},{2,98}... | collective-permute-start | bytes 2211848 | tf_op jit(solution)/shard_map/ppermute | solution.py:317
  55.7 3.5 %copy-start.5 = (bf16[320,1152]{1,0:T(8,128)(2,1)}, bf16[320,1152]{1,0:T(8,128)(2,1)S(1)}, u32[]{:S(2)}) copy-start(bf16[320,1152]{1,0:T(8,128)(2,1)S(1)} %collective-permute-done.5.refs_0_.refs_6_) | copy-start | bytes 2211844
  55.7 3.5 %copy-start.6 = (bf16[320,1152]{1,0:T(8,128)(2,1)}, bf16[320,1152]{1,0:T(8,128)(2,1)S(1)}, u32[]{:S(2)}) copy-start(bf16[320,1152]{1,0:T(8,128)(2,1)S(1)} %collective-permute-done.6.refs_1_.refs_7_) | copy-start | bytes 2211844
  59.2 24.4 %all-to-all-start.2 = ((bf16[16,40,1152]{2,1,0:T(8,128)(2,1)}), bf16[16,40,1152]{2,1,0:T(8,128)(2,1)}, u32[]{:S(2)}, u32[]{:S(2)}) async-start(bf16[16,40,1152]{2,1,0:T(8,128)(2,1)} %bitcast.9), calls=%async_computation.2 | async-start | bytes 2949120 | tf_op jit(solution)/shard_map/all_to_all | solution.py:321
  63.8 17.7 %collective-permute-start.7 = (bf16[320,1152]{1,0:T(8,128)(2,1)S(1)}, bf16[320,1152]{1,0:T(8,128)(2,1)S(1)}, u32[]{:S(2)}, u32[]{:S(2)}) collective-permute-start(bf16[320,1152]{1,0:T(8,128)(2,1)S(1)} %shard_map.95.refs_1_.refs_9_), channel_id=1, source_target_pairs={{0,64},{32,96},{64,0},{96,32},{1,65},{33,97},{65,1},{97,33},{2,66}... | collective-permute-start | bytes 2211848 | tf_op jit(solution)/shard_map/ppermute | solution.py:317
  77.9 34.6 %collective-permute-start.8 = (bf16[336,1152]{1,0:T(8,128)(2,1)}, bf16[336,1152]{1,0:T(8,128)(2,1)S(1)}, u32[]{:S(2)}, u32[]{:S(2)}) collective-permute-start(bf16[336,1152]{1,0:T(8,128)(2,1)} %get-tuple-element.68), channel_id=1, source_target_pairs={{0,96},{32,0},{64,32},{96,64},{1,97},{33,1},{65,33},{97,65},{2,98}... | collective-permute-start | bytes 2322440 | tf_op jit(solution)/shard_map/ppermute | solution.py:317
  79.9 34.4 %collective-permute-start.10 = (bf16[336,1152]{1,0:T(8,128)(2,1)}, bf16[336,1152]{1,0:T(8,128)(2,1)S(1)}, u32[]{:S(2)}, u32[]{:S(2)}) collective-permute-start(bf16[336,1152]{1,0:T(8,128)(2,1)} %get-tuple-element.70), channel_id=1, source_target_pairs={{0,32},{32,64},{64,96},{96,0},{1,33},{33,65},{65,97},{97,1},{2,34}... | collective-permute-start | bytes 2322440 | tf_op jit(solution)/shard_map/ppermute | solution.py:317
  81.5 2.1 %copy-start.7 = (bf16[320,1152]{1,0:T(8,128)(2,1)}, bf16[320,1152]{1,0:T(8,128)(2,1)S(1)}, u32[]{:S(2)}) copy-start(bf16[320,1152]{1,0:T(8,128)(2,1)S(1)} %collective-permute-done.7.refs_0_.refs_8_) | copy-start | bytes 2211844
  96.2 18.1 %collective-permute-start.9 = (bf16[336,1152]{1,0:T(8,128)(2,1)}, bf16[336,1152]{1,0:T(8,128)(2,1)S(1)}, u32[]{:S(2)}, u32[]{:S(2)}) collective-permute-start(bf16[336,1152]{1,0:T(8,128)(2,1)} %get-tuple-element.69), channel_id=1, source_target_pairs={{0,64},{32,96},{64,0},{96,32},{1,65},{33,97},{65,1},{97,33},{2,66}... | collective-permute-start | bytes 2322440 | tf_op jit(solution)/shard_map/ppermute | solution.py:317
  96.6 17.8 %copy-start.1 = (bf16[336,1152]{1,0:T(8,128)(2,1)S(1)}, bf16[336,1152]{1,0:T(8,128)(2,1)}, u32[]{:S(2)}) copy-start(bf16[336,1152]{1,0:T(8,128)(2,1)} %get-tuple-element.79.refs_0_) | copy-start | bytes 2322436
  116.3 6.9 %collective-permute-start.11 = (bf16[1152,1152]{1,0:T(8,128)(2,1)}, bf16[1152,1152]{1,0:T(8,128)(2,1)S(1)}, u32[]{:S(2)}, u32[]{:S(2)}) collective-permute-start(bf16[1152,1152]{1,0:T(8,128)(2,1)} %get-tuple-element.85), channel_id=1, source_target_pairs={{0,16},{16,0},{1,17},{17,1},{2,18},{18,2},{3,19},{19,3},{4,20},{20... | collective-permute-start | bytes 7962632 | tf_op jit(solution)/shard_map/ppermute | solution.py:317
  116.3 23.2 %all-to-all-start.3 = ((bf16[16,24,1152]{2,1,0:T(8,128)(2,1)}), bf16[16,24,1152]{2,1,0:T(8,128)(2,1)S(1)}, u32[]{:S(2)}, u32[]{:S(2)}) async-start(bf16[16,24,1152]{2,1,0:T(8,128)(2,1)} %bitcast.11), calls=%async_computation.3 | async-start | bytes 1769472 | tf_op jit(solution)/shard_map/all_to_all | solution.py:321
  123.2 1.3 copy-start.8
  123.2 1.7 %copy-start.9 = (bf16[576,1152]{1,0:T(8,128)(2,1)S(1)}, bf16[576,1152]{1,0:T(8,128)(2,1)}, u32[]{:S(2)}) copy-start(bf16[576,1152]{1,0:T(8,128)(2,1)} %get-tuple-element.86) | copy-start | bytes 3981316

commit v6 on v5

--- a/solution.py
+++ b/solution.py
@@ -103,9 +103,10 @@
     here, high, low = (jnp.concatenate(v, axis=1) for v in (here, high, low))
     own, _, slot = row_owner(experts, out.shape[0] // experts)
     picker = mm(own, here.astype(BF), NN) == slot
-    gate = jnp.where(picker, mm(own, high, NN) + mm(own, low, NN), 0.0)
+    picker = ones(picker)
+    gate = (mm(picker, high, NT) + mm(picker, low, NT)) * own.astype(F32)
     gate = jnp.sum(gate, axis=1, keepdims=True)
-    out[...] = (mm(ones(picker), dy, NN) * gate).astype(BF)
+    out[...] = (mm(picker, dy, NN) * gate).astype(BF)
 
 
 def regroup(experts, span, count):

time: 141 us -> 141 us (level)
  no operation moved by 1% of the time
where the time goes in v6:
time: 141 us
  Pallas kernels  48.2 us (34%)
  waiting for transfers between devices  47.4 us (34%)
  starting transfers between devices  40.5 us (29%)
  other arithmetic  2.34 us (2%)
    ppermute x12, waiting for transfers between devices, shift(): lax.ppermute(value, axis, [(i, (i + by) % size) for i in range(size)])  29 us
    all_to_all x4, starting transfers between devices, exchange(): lax.all_to_all(value, 'expert', split_axis=0, concat_axis=0, tiled=True)  26.3 us
    pallas_call x2, Pallas kernels, rows_call(): call(functools.partial(rows_kernel, experts, len(parts), blocks), [arr(hi...  25.2 us
    all_to_all x4, waiting for transfers between devices, exchange(): lax.all_to_all(value, 'expert', split_axis=0, concat_axis=0, tiled=True)  18.4 us
    ppermute x12, starting transfers between devices, shift(): lax.ppermute(value, axis, [(i, (i + by) % size) for i in range(size)])  14.1 us
    pallas_call x1, Pallas kernels, local(): call(functools.partial(weights_kernel, len(GROUPS), len(parts_a + parts_b...  12.1 us
    pallas_call x2, Pallas kernels, expand(): call(functools.partial(expand_kernel, experts, CAP), arr(block * len(GROU...  4.4 us
  transfers between devices with their start and end apart: 16, of which 9 were waited for; matrix products, arithmetic and copies ran while one was open for 2% of the time, Pallas kernels for 30%

profile of v6, /device:TPU:0, one launch (start us, length us, event | category | flops | bytes accessed | tf_op | source)
XLA Modules:
  0.0 140.7 jit_solution(16929401312350605973)
XLA Ops:
  0.7 2.6 %shard_map.93 = bf16[384,1152]{1,0:T(8,128)(2,1)} custom-call(bf16[128,1152]{1,0:T(8,128)(2,1)} %x_ref.1, s32[2,128]{1,0:T(2,128)} %bitcast.21), custom_call_target="tpu_custom_call" | custom-call | flops 1 | bytes 1 | tf_op jit(solution)/shard_map/pallas_call | solution.py:343
  3.2 0.5 collective-permute-start.2
  3.7 8.0 %all-to-all-start = ((bf16[16,24,1152]{2,1,0:T(8,128)(2,1)}), bf16[16,24,1152]{2,1,0:T(8,128)(2,1)S(1)}, u32[]{:S(2)}, u32[]{:S(2)}) async-start(bf16[16,24,1152]{2,1,0:T(8,128)(2,1)} %bitcast.32), calls=%async_computation | async-start | bytes 1769472 | tf_op jit(solution)/shard_map/all_to_all | solution.py:322
  11.8 1.6 %collective-permute-start = (bf16[144,1152]{1,0:T(8,128)(2,1)S(1)}, bf16[144,1152]{1,0:T(8,128)(2,1)S(1)}, u32[]{:S(2)}, u32[]{:S(2)}) collective-permute-start(bf16[144,1152]{1,0:T(8,128)(2,1)S(1)} %shard_map.94.refs_1_), channel_id=1, source_target_pairs={{0,32},{32,64},{64,96},{96,0},{1,33},{33,65},{65,97},{97,1},{2,34}... | collective-permute-start | bytes 995336 | tf_op jit(solution)/shard_map/ppermute | solution.py:318
  13.4 1.7 %collective-permute-start.3 = (bf16[144,1152]{1,0:T(8,128)(2,1)S(1)}, bf16[144,1152]{1,0:T(8,128)(2,1)S(1)}, u32[]{:S(2)}, u32[]{:S(2)}) collective-permute-start(bf16[144,1152]{1,0:T(8,128)(2,1)S(1)} %shard_map.94.refs_1_), channel_id=1, source_target_pairs={{0,96},{32,0},{64,32},{96,64},{1,97},{33,1},{65,33},{97,65},{2,98}... | collective-permute-start | bytes 995336 | tf_op jit(solution)/shard_map/ppermute | solution.py:318
  15.1 2.0 %collective-permute-start.4 = (bf16[144,1152]{1,0:T(8,128)(2,1)S(1)}, bf16[144,1152]{1,0:T(8,128)(2,1)S(1)}, u32[]{:S(2)}, u32[]{:S(2)}) collective-permute-start(bf16[144,1152]{1,0:T(8,128)(2,1)S(1)} %shard_map.94.refs_1_), channel_id=1, source_target_pairs={{0,64},{32,96},{64,0},{96,32},{1,65},{33,97},{65,1},{97,33},{2,66}... | collective-permute-start | bytes 995336 | tf_op jit(solution)/shard_map/ppermute | solution.py:318
  17.1 5.6 %collective-permute-done.refs_0_ = bf16[144,1152]{1,0:T(8,128)(2,1)S(1)} collective-permute-done((bf16[144,1152]{1,0:T(8,128)(2,1)S(1)}, bf16[144,1152]{1,0:T(8,128)(2,1)S(1)}, u32[]{:S(2)}, u32[]{:S(2)}) %collective-permute-start) | collective-permute-done | bytes 331808 | tf_op jit(solution)/shard_map/ppermute | solution.py:318
  22.6 6.4 %collective-permute-done.3.refs_1_ = bf16[144,1152]{1,0:T(8,128)(2,1)S(1)} collective-permute-done((bf16[144,1152]{1,0:T(8,128)(2,1)S(1)}, bf16[144,1152]{1,0:T(8,128)(2,1)S(1)}, u32[]{:S(2)}, u32[]{:S(2)}) %collective-permute-start.3) | collective-permute-done | bytes 331808 | tf_op jit(solution)/shard_map/ppermute | solution.py:318
  29.0 0.6 shard_map.95.refs_1_.refs_9_
  29.7 2.2 %shard_map.96 = bf16[640,1152]{1,0:T(8,128)(2,1)} custom-call(bf16[144,1152]{1,0:T(8,128)(2,1)S(1)} %collective-permute-done.refs_0_, bf16[144,1152]{1,0:T(8,128)(2,1)S(1)} %collective-permute-done.3.refs_1_), custom_call_target="tpu_custom_call" | custom-call | flops 1 | bytes 1 | tf_op jit(solution)/shard_map/pallas_call | solution.py:354
  31.9 7.0 %all-to-all-start.1 = ((bf16[16,40,1152]{2,1,0:T(8,128)(2,1)}), bf16[16,40,1152]{2,1,0:T(8,128)(2,1)}, u32[]{:S(2)}, u32[]{:S(2)}) async-start(bf16[16,40,1152]{2,1,0:T(8,128)(2,1)} %bitcast.7), calls=%async_computation.1 | async-start | bytes 2949120 | tf_op jit(solution)/shard_map/all_to_all | solution.py:322
  39.0 3.6 %collective-permute-start.6 = (bf16[320,1152]{1,0:T(8,128)(2,1)S(1)}, bf16[320,1152]{1,0:T(8,128)(2,1)S(1)}, u32[]{:S(2)}, u32[]{:S(2)}) collective-permute-start(bf16[320,1152]{1,0:T(8,128)(2,1)S(1)} %shard_map.95.refs_1_.refs_9_), channel_id=1, source_target_pairs={{0,96},{32,0},{64,32},{96,64},{1,97},{33,1},{65,33},{97,65},{2,98}... | collective-permute-start | bytes 2211848 | tf_op jit(solution)/shard_map/ppermute | solution.py:318
  42.7 2.2 %shard_map.97 = bf16[640,1152]{1,0:T(8,128)(2,1)} custom-call(bf16[144,1152]{1,0:T(8,128)(2,1)S(1)} %collective-permute-done.4.refs_0_, bf16[144,1152]{1,0:T(8,128)(2,1)S(1)} %shard_map.94.refs_1_), custom_call_target="tpu_custom_call" | custom-call | flops 1 | bytes 1 | tf_op jit(solution)/shard_map/pallas_call | solution.py:354
  44.9 10.8 %collective-permute-done.5.refs_0_.refs_6_ = bf16[320,1152]{1,0:T(8,128)(2,1)S(1)} collective-permute-done((bf16[320,1152]{1,0:T(8,128)(2,1)S(1)}, bf16[320,1152]{1,0:T(8,128)(2,1)S(1)}, u32[]{:S(2)}, u32[]{:S(2)}) %collective-permute-start.5) | collective-permute-done | bytes 737312 | tf_op jit(solution)/shard_map/ppermute | solution.py:318
  55.7 3.5 %all-to-all-done.1 = bf16[16,40,1152]{2,1,0:T(8,128)(2,1)} async-done(((bf16[16,40,1152]{2,1,0:T(8,128)(2,1)}), bf16[16,40,1152]{2,1,0:T(8,128)(2,1)}, u32[]{:S(2)}, u32[]{:S(2)}) %all-to-all-start.1) | async-done | bytes 1474592 | tf_op jit(solution)/shard_map/all_to_all | solution.py:322
  59.2 4.5 %all-to-all-start.2 = ((bf16[16,40,1152]{2,1,0:T(8,128)(2,1)}), bf16[16,40,1152]{2,1,0:T(8,128)(2,1)}, u32[]{:S(2)}, u32[]{:S(2)}) async-start(bf16[16,40,1152]{2,1,0:T(8,128)(2,1)} %bitcast.9), calls=%async_computation.2 | async-start | bytes 2949120 | tf_op jit(solution)/shard_map/all_to_all | solution.py:322
  63.8 1.5 %collective-permute-start.7 = (bf16[320,1152]{1,0:T(8,128)(2,1)S(1)}, bf16[320,1152]{1,0:T(8,128)(2,1)S(1)}, u32[]{:S(2)}, u32[]{:S(2)}) collective-permute-start(bf16[320,1152]{1,0:T(8,128)(2,1)S(1)} %shard_map.95.refs_1_.refs_9_), channel_id=1, source_target_pairs={{0,64},{32,96},{64,0},{96,32},{1,65},{33,97},{65,1},{97,33},{2,66}... | collective-permute-start | bytes 2211848 | tf_op jit(solution)/shard_map/ppermute | solution.py:318
  65.3 12.6 %shard_map.99 = (bf16[1152,640]{1,0:T(8,128)(2,1)}, bf16[1152,640]{1,0:T(8,128)(2,1)}, bf16[640,1152]{1,0:T(8,128)(2,1)}, bf16[336,1152]{1,0:T(8,128)(2,1)}, bf16[336,1152]{1,0:T(8,128)(2,1)}) custom-call(bf16[320,1152]{1,0:T(8,128)(2,1)} %copy-done.5, bf16[320,1152]{1,0:T(8,128)(2,1)} %copy-done.6, bf16[640,1152]{1,0:T(8,128)(2,1)} %bitcast.8.refs_2_, ...), custom_call_target="tpu_custom_call" | custom-call | flops 1 | bytes 1 | tf_op jit(solution)/shard_map/pallas_call | solution.py:371
  77.9 2.0 %collective-permute-start.8 = (bf16[336,1152]{1,0:T(8,128)(2,1)}, bf16[336,1152]{1,0:T(8,128)(2,1)S(1)}, u32[]{:S(2)}, u32[]{:S(2)}) collective-permute-start(bf16[336,1152]{1,0:T(8,128)(2,1)} %get-tuple-element.68), channel_id=1, source_target_pairs={{0,96},{32,0},{64,32},{96,64},{1,97},{33,1},{65,33},{97,65},{2,98}... | collective-permute-start | bytes 2322440 | tf_op jit(solution)/shard_map/ppermute | solution.py:318
  79.9 0.7 collective-permute-start.10
  80.5 0.6 collective-permute-done.7.refs_0_.refs_8_
  81.1 2.3 %all-to-all-done.2 = bf16[16,40,1152]{2,1,0:T(8,128)(2,1)} async-done(((bf16[16,40,1152]{2,1,0:T(8,128)(2,1)}), bf16[16,40,1152]{2,1,0:T(8,128)(2,1)}, u32[]{:S(2)}, u32[]{:S(2)}) %all-to-all-start.2) | async-done | bytes 1474592 | tf_op jit(solution)/shard_map/all_to_all | solution.py:322
  83.4 12.6 %shard_map.98 = (bf16[1152,640]{1,0:T(8,128)(2,1)}, bf16[1152,640]{1,0:T(8,128)(2,1)}, bf16[640,1152]{1,0:T(8,128)(2,1)}, bf16[336,1152]{1,0:T(8,128)(2,1)}, bf16[336,1152]{1,0:T(8,128)(2,1)}) custom-call(bf16[320,1152]{1,0:T(8,128)(2,1)} %copy-done.7, bf16[320,1152]{1,0:T(8,128)(2,1)} %copy-done, bf16[640,1152]{1,0:T(8,128)(2,1)} %bitcast.10.refs_2_, ...), custom_call_target="tpu_custom_call" | custom-call | flops 1 | bytes 1 | tf_op jit(solution)/shard_map/pallas_call | solution.py:371
  96.4 12.1 %shard_map.100 = (bf16[576,1152]{1,0:T(8,128)(2,1)}, bf16[576,1152]{1,0:T(8,128)(2,1)}, bf16[1152,1152]{1,0:T(8,128)(2,1)}) custom-call(bf16[1152,640]{1,0:T(8,128)(2,1)} %get-tuple-element.71.refs_0_, bf16[1152,640]{1,0:T(8,128)(2,1)} %get-tuple-element.72.refs_1_, bf16[640,1152]{1,0:T(8,128)(2,1)} %get-tuple-element.73.refs_2_, ...), custom_call_target="tpu_custom_call" | custom-call | flops 1 | bytes 1 | tf_op jit(solution)/shard_map/pallas_call | solution.py:394
  108.5 3.9 %collective-permute-done.8.refs_1_ = bf16[336,1152]{1,0:T(8,128)(2,1)S(1)} collective-permute-done((bf16[336,1152]{1,0:T(8,128)(2,1)}, bf16[336,1152]{1,0:T(8,128)(2,1)S(1)}, u32[]{:S(2)}, u32[]{:S(2)}) %collective-permute-start.8) | collective-permute-done | bytes 774176 | tf_op jit(solution)/shard_map/ppermute | solution.py:318
  112.4 1.7 %collective-permute-done.10.refs_3_ = bf16[336,1152]{1,0:T(8,128)(2,1)S(1)} collective-permute-done((bf16[336,1152]{1,0:T(8,128)(2,1)}, bf16[336,1152]{1,0:T(8,128)(2,1)S(1)}, u32[]{:S(2)}, u32[]{:S(2)}) %collective-permute-start.10) | collective-permute-done | bytes 774176 | tf_op jit(solution)/shard_map/ppermute | solution.py:318
  114.1 2.0 %shard_map.101 = bf16[384,1152]{1,0:T(8,128)(2,1)} custom-call(bf16[336,1152]{1,0:T(8,128)(2,1)S(1)} %copy-done.1, bf16[336,1152]{1,0:T(8,128)(2,1)S(1)} %collective-permute-done.8.refs_1_, bf16[336,1152]{1,0:T(8,128)(2,1)S(1)} %collective-permute-done.9.refs_2_, bf16[336,1152]{1,0:T(8,128)(2,1)S(1)} %collective-permute-done.10.refs_3_), custom_call_target="tpu_custom_call" | custom-call | flops 1 | bytes 1 | tf_op jit(solution)/shard_map/pallas_call | solution.py:406
  116.1 6.9 %all-to-all-start.3 = ((bf16[16,24,1152]{2,1,0:T(8,128)(2,1)}), bf16[16,24,1152]{2,1,0:T(8,128)(2,1)S(1)}, u32[]{:S(2)}, u32[]{:S(2)}) async-start(bf16[16,24,1152]{2,1,0:T(8,128)(2,1)} %bitcast.11), calls=%async_computation.3 | async-start | bytes 1769472 | tf_op jit(solution)/shard_map/all_to_all | solution.py:322
  123.4 0.9 copy-done.8
  124.7 2.0 %fusion = (bf16[576,1152]{1,0:T(8,128)(2,1)}, bf16[576,1152]{1,0:T(8,128)(2,1)}) fusion(f32[1152,1152]{1,0:T(8,128)S(1)} %convert_element_type.16, bf16[576,1152]{1,0:T(8,128)(2,1)S(1)} %copy-done.9, bf16[576,1152]{1,0:T(8,128)(2,1)S(1)} %copy-done.8), kind=kLoop, calls=%fused_computation.1 | loop fusion | flops 3981312 | bytes 10616832 | tf_op jit(solution)/shard_map/convert_element_type | solution.py:412
  126.7 12.6 %all-to-all-done.3 = bf16[16,24,1152]{2,1,0:T(8,128)(2,1)S(1)} async-done(((bf16[16,24,1152]{2,1,0:T(8,128)(2,1)}), bf16[16,24,1152]{2,1,0:T(8,128)(2,1)S(1)}, u32[]{:S(2)}, u32[]{:S(2)}) %all-to-all-start.3) | async-done | bytes 884768 | tf_op jit(solution)/shard_map/all_to_all | solution.py:322
  139.3 1.4 shard_map.102
  (32 shorter events, 1.3 us)
Async XLA Ops:
  0.6 11.1 %copy-start.2 = (bf16[128,1152]{1,0:T(8,128)(2,1)S(1)}, bf16[128,1152]{1,0:T(8,128)(2,1)}, u32[]{:S(2)}) copy-start(bf16[128,1152]{1,0:T(8,128)(2,1)} %dy_ref.1) | copy-start | bytes 884740
  0.6 11.1 %copy-start.3 = (s32[128,2]{0,1:T(2,128)S(1)}, s32[128,2]{0,1:T(2,128)}, u32[]{:S(2)}) copy-start(s32[128,2]{0,1:T(2,128)} %param.9) | copy-start | bytes 3076
  0.7 11.1 %copy-start.4 = (f32[128,2]{0,1:T(2,128)S(1)}, f32[128,2]{0,1:T(2,128)}, u32[]{:S(2)}) copy-start(f32[128,2]{0,1:T(2,128)} %param.8) | copy-start | bytes 3076
  3.2 19.4 %collective-permute-start.1 = (bf16[576,1152]{1,0:T(8,128)(2,1)}, bf16[576,1152]{1,0:T(8,128)(2,1)}, u32[]{:S(2)}, u32[]{:S(2)}) collective-permute-start(bf16[576,1152]{1,0:T(8,128)(2,1)} %bitcast.26), channel_id=1, source_target_pairs={{0,16},{16,0},{1,17},{17,1},{2,18},{18,2},{3,19},{19,3},{4,20},{20... | collective-permute-start | bytes 3981320 | tf_op jit(solution)/shard_map/ppermute | solution.py:318
  3.2 19.4 %collective-permute-start.2 = (bf16[576,1152]{1,0:T(8,128)(2,1)}, bf16[576,1152]{1,0:T(8,128)(2,1)}, u32[]{:S(2)}, u32[]{:S(2)}) collective-permute-start(bf16[576,1152]{1,0:T(8,128)(2,1)} %bitcast.29), channel_id=1, source_target_pairs={{0,16},{16,0},{1,17},{17,1},{2,18},{18,2},{3,19},{19,3},{4,20},{20... | collective-permute-start | bytes 3981320 | tf_op jit(solution)/shard_map/ppermute | solution.py:318
  3.7 25.3 %all-to-all-start = ((bf16[16,24,1152]{2,1,0:T(8,128)(2,1)}), bf16[16,24,1152]{2,1,0:T(8,128)(2,1)S(1)}, u32[]{:S(2)}, u32[]{:S(2)}) async-start(bf16[16,24,1152]{2,1,0:T(8,128)(2,1)} %bitcast.32), calls=%async_computation | async-start | bytes 1769472 | tf_op jit(solution)/shard_map/all_to_all | solution.py:322
  11.8 10.9 %collective-permute-start = (bf16[144,1152]{1,0:T(8,128)(2,1)S(1)}, bf16[144,1152]{1,0:T(8,128)(2,1)S(1)}, u32[]{:S(2)}, u32[]{:S(2)}) collective-permute-start(bf16[144,1152]{1,0:T(8,128)(2,1)S(1)} %shard_map.94.refs_1_), channel_id=1, source_target_pairs={{0,32},{32,64},{64,96},{96,0},{1,33},{33,65},{65,97},{97,1},{2,34}... | collective-permute-start | bytes 995336 | tf_op jit(solution)/shard_map/ppermute | solution.py:318
  13.4 15.6 %collective-permute-start.3 = (bf16[144,1152]{1,0:T(8,128)(2,1)S(1)}, bf16[144,1152]{1,0:T(8,128)(2,1)S(1)}, u32[]{:S(2)}, u32[]{:S(2)}) collective-permute-start(bf16[144,1152]{1,0:T(8,128)(2,1)S(1)} %shard_map.94.refs_1_), channel_id=1, source_target_pairs={{0,96},{32,0},{64,32},{96,64},{1,97},{33,1},{65,33},{97,65},{2,98}... | collective-permute-start | bytes 995336 | tf_op jit(solution)/shard_map/ppermute | solution.py:318
  15.1 16.8 %collective-permute-start.4 = (bf16[144,1152]{1,0:T(8,128)(2,1)S(1)}, bf16[144,1152]{1,0:T(8,128)(2,1)S(1)}, u32[]{:S(2)}, u32[]{:S(2)}) collective-permute-start(bf16[144,1152]{1,0:T(8,128)(2,1)S(1)} %shard_map.94.refs_1_), channel_id=1, source_target_pairs={{0,64},{32,96},{64,0},{96,32},{1,65},{33,97},{65,1},{97,33},{2,66}... | collective-permute-start | bytes 995336 | tf_op jit(solution)/shard_map/ppermute | solution.py:318
  29.7 34.1 %copy-start = (bf16[320,1152]{1,0:T(8,128)(2,1)}, bf16[320,1152]{1,0:T(8,128)(2,1)S(1)}, u32[]{:S(2)}) copy-start(bf16[320,1152]{1,0:T(8,128)(2,1)S(1)} %shard_map.95.refs_1_.refs_9_) | copy-start | bytes 2211844
  31.9 27.4 %all-to-all-start.1 = ((bf16[16,40,1152]{2,1,0:T(8,128)(2,1)}), bf16[16,40,1152]{2,1,0:T(8,128)(2,1)}, u32[]{:S(2)}, u32[]{:S(2)}) async-start(bf16[16,40,1152]{2,1,0:T(8,128)(2,1)} %bitcast.7), calls=%async_computation.1 | async-start | bytes 2949120 | tf_op jit(solution)/shard_map/all_to_all | solution.py:322
  38.9 16.9 %collective-permute-start.5 = (bf16[320,1152]{1,0:T(8,128)(2,1)S(1)}, bf16[320,1152]{1,0:T(8,128)(2,1)S(1)}, u32[]{:S(2)}, u32[]{:S(2)}) collective-permute-start(bf16[320,1152]{1,0:T(8,128)(2,1)S(1)} %shard_map.95.refs_1_.refs_9_), channel_id=1, source_target_pairs={{0,32},{32,64},{64,96},{96,0},{1,33},{33,65},{65,97},{97,1},{2,34}... | collective-permute-start | bytes 2211848 | tf_op jit(solution)/shard_map/ppermute | solution.py:318
  39.0 16.7 %collective-permute-start.6 = (bf16[320,1152]{1,0:T(8,128)(2,1)S(1)}, bf16[320,1152]{1,0:T(8,128)(2,1)S(1)}, u32[]{:S(2)}, u32[]{:S(2)}) collective-permute-start(bf16[320,1152]{1,0:T(8,128)(2,1)S(1)} %shard_map.95.refs_1_.refs_9_), channel_id=1, source_target_pairs={{0,96},{32,0},{64,32},{96,64},{1,97},{33,1},{65,33},{97,65},{2,98}... | collective-permute-start | bytes 2211848 | tf_op jit(solution)/shard_map/ppermute | solution.py:318
  55.7 3.5 %copy-start.5 = (bf16[320,1152]{1,0:T(8,128)(2,1)}, bf16[320,1152]{1,0:T(8,128)(2,1)S(1)}, u32[]{:S(2)}) copy-start(bf16[320,1152]{1,0:T(8,128)(2,1)S(1)} %collective-permute-done.5.refs_0_.refs_6_) | copy-start | bytes 2211844
  55.7 3.5 %copy-start.6 = (bf16[320,1152]{1,0:T(8,128)(2,1)}, bf16[320,1152]{1,0:T(8,128)(2,1)S(1)}, u32[]{:S(2)}) copy-start(bf16[320,1152]{1,0:T(8,128)(2,1)S(1)} %collective-permute-done.6.refs_1_.refs_7_) | copy-start | bytes 2211844
  59.2 24.2 %all-to-all-start.2 = ((bf16[16,40,1152]{2,1,0:T(8,128)(2,1)}), bf16[16,40,1152]{2,1,0:T(8,128)(2,1)}, u32[]{:S(2)}, u32[]{:S(2)}) async-start(bf16[16,40,1152]{2,1,0:T(8,128)(2,1)} %bitcast.9), calls=%async_computation.2 | async-start | bytes 2949120 | tf_op jit(solution)/shard_map/all_to_all | solution.py:322
  63.8 17.3 %collective-permute-start.7 = (bf16[320,1152]{1,0:T(8,128)(2,1)S(1)}, bf16[320,1152]{1,0:T(8,128)(2,1)S(1)}, u32[]{:S(2)}, u32[]{:S(2)}) collective-permute-start(bf16[320,1152]{1,0:T(8,128)(2,1)S(1)} %shard_map.95.refs_1_.refs_9_), channel_id=1, source_target_pairs={{0,64},{32,96},{64,0},{96,32},{1,65},{33,97},{65,1},{97,33},{2,66}... | collective-permute-start | bytes 2211848 | tf_op jit(solution)/shard_map/ppermute | solution.py:318
  77.9 34.5 %collective-permute-start.8 = (bf16[336,1152]{1,0:T(8,128)(2,1)}, bf16[336,1152]{1,0:T(8,128)(2,1)S(1)}, u32[]{:S(2)}, u32[]{:S(2)}) collective-permute-start(bf16[336,1152]{1,0:T(8,128)(2,1)} %get-tuple-element.68), channel_id=1, source_target_pairs={{0,96},{32,0},{64,32},{96,64},{1,97},{33,1},{65,33},{97,65},{2,98}... | collective-permute-start | bytes 2322440 | tf_op jit(solution)/shard_map/ppermute | solution.py:318
  79.9 34.2 %collective-permute-start.10 = (bf16[336,1152]{1,0:T(8,128)(2,1)}, bf16[336,1152]{1,0:T(8,128)(2,1)S(1)}, u32[]{:S(2)}, u32[]{:S(2)}) collective-permute-start(bf16[336,1152]{1,0:T(8,128)(2,1)} %get-tuple-element.70), channel_id=1, source_target_pairs={{0,32},{32,64},{64,96},{96,0},{1,33},{33,65},{65,97},{97,1},{2,34}... | collective-permute-start | bytes 2322440 | tf_op jit(solution)/shard_map/ppermute | solution.py:318
  81.1 2.3 %copy-start.7 = (bf16[320,1152]{1,0:T(8,128)(2,1)}, bf16[320,1152]{1,0:T(8,128)(2,1)S(1)}, u32[]{:S(2)}) copy-start(bf16[320,1152]{1,0:T(8,128)(2,1)S(1)} %collective-permute-done.7.refs_0_.refs_8_) | copy-start | bytes 2211844
  96.0 18.1 %collective-permute-start.9 = (bf16[336,1152]{1,0:T(8,128)(2,1)}, bf16[336,1152]{1,0:T(8,128)(2,1)S(1)}, u32[]{:S(2)}, u32[]{:S(2)}) collective-permute-start(bf16[336,1152]{1,0:T(8,128)(2,1)} %get-tuple-element.69), channel_id=1, source_target_pairs={{0,64},{32,96},{64,0},{96,32},{1,65},{33,97},{65,1},{97,33},{2,66}... | collective-permute-start | bytes 2322440 | tf_op jit(solution)/shard_map/ppermute | solution.py:318
  96.4 17.8 %copy-start.1 = (bf16[336,1152]{1,0:T(8,128)(2,1)S(1)}, bf16[336,1152]{1,0:T(8,128)(2,1)}, u32[]{:S(2)}) copy-start(bf16[336,1152]{1,0:T(8,128)(2,1)} %get-tuple-element.79.refs_0_) | copy-start | bytes 2322436
  116.1 6.9 %collective-permute-start.11 = (bf16[1152,1152]{1,0:T(8,128)(2,1)}, bf16[1152,1152]{1,0:T(8,128)(2,1)S(1)}, u32[]{:S(2)}, u32[]{:S(2)}) collective-permute-start(bf16[1152,1152]{1,0:T(8,128)(2,1)} %get-tuple-element.85), channel_id=1, source_target_pairs={{0,16},{16,0},{1,17},{17,1},{2,18},{18,2},{3,19},{19,3},{4,20},{20... | collective-permute-start | bytes 7962632 | tf_op jit(solution)/shard_map/ppermute | solution.py:318
  116.1 23.2 %all-to-all-start.3 = ((bf16[16,24,1152]{2,1,0:T(8,128)(2,1)}), bf16[16,24,1152]{2,1,0:T(8,128)(2,1)S(1)}, u32[]{:S(2)}, u32[]{:S(2)}) async-start(bf16[16,24,1152]{2,1,0:T(8,128)(2,1)} %bitcast.11), calls=%async_computation.3 | async-start | bytes 1769472 | tf_op jit(solution)/shard_map/all_to_all | solution.py:322
  123.0 1.3 copy-start.8
  123.0 1.7 %copy-start.9 = (bf16[576,1152]{1,0:T(8,128)(2,1)S(1)}, bf16[576,1152]{1,0:T(8,128)(2,1)}, u32[]{:S(2)}) copy-start(bf16[576,1152]{1,0:T(8,128)(2,1)} %get-tuple-element.86) | copy-start | bytes 3981316
